TPU v7x, 32 devices: a whole 2x2x4 slice. The times are simulated.
32 devices in a mesh: groups: 2 (over x), tm: 8 (over z, y), tile: 2 (over core).
Axes of the slice: x: 2, y: 2, z: 4, core: 2. Of those that a mesh axis runs over, the one named last changes fastest.
Arguments:
- frames: bfloat16 [2, 16, 2, 64, 2048], P(None, ('groups', 'tm'), 'tile'), parts along dimension 1, may hold values from -6 to 6
- forward_carry: bfloat16 [16, 2, 64, 2048], P(('groups', 'tm'), 'tile'), parts along dimension 0, may hold values from -6 to 6
- backward_carry: bfloat16 [16, 2, 64, 2048], P(('groups', 'tm'), 'tile'), parts along dimension 0, may hold values from -6 to 6
- forward_source: int32 [2, 16, 32], P(None, ('groups', 'tm'), 'tile'), parts along dimension 1, may hold values from 0 to 31, as said below
- backward_source: int32 [2, 16, 32], P(None, ('groups', 'tm'), 'tile'), parts along dimension 1, may hold values from 0 to 31, as said below
- forward_entry: bfloat16 [9, 64, 128], replicated, may hold values from -0.1875 to 0.1875
- forward_blocks: bfloat16 [1, 2, 9, 64, 64], replicated, may hold values from -0.25 to 0.25
- backward_entry: bfloat16 [9, 64, 128], replicated, may hold values from -0.1875 to 0.1875
- backward_blocks: bfloat16 [1, 2, 9, 64, 64], replicated, may hold values from -0.25 to 0.25
- mixing_weight: bfloat16 [64, 128], replicated, may hold values from -0.5 to 0.5
Outputs:
- restored: bfloat16 [2, 16, 2, 64, 2048], P(None, ('groups', 'tm'), 'tile'), parts along dimension 1
- forward_final: bfloat16 [16, 2, 64, 2048], P(('groups', 'tm'), 'tile'), parts along dimension 0
- backward_final: bfloat16 [16, 2, 64, 2048], P(('groups', 'tm'), 'tile'), parts along dimension 0
There are 2 independent parts, one for each index of `groups`. A program takes and returns all parts, laid end to end along the dimension named above; an argument that names none is the same for every part. Nothing has to cross between parts.
Inputs may be any that keep to these rules, and one draw needn't show every extreme that they name: `forward_source`: for each step, segment and destination block of a frame, the block whose forward features it takes: the destination moved by at most one block row and three block columns, kept inside the frame. `backward_source`: the same for backward features.
All inputs are finite; a program needn't handle non-finite values.
Results may differ from a plain program's by a relative error of at most 0.012.
Values may be sent and summed in bfloat16 or wider, within the bound.
No kernel may reach another device: no remote copies, remote signals or barrier semaphores. Data moves between devices by JAX's collectives and lax.ppermute only.
A program may use at most 64 MiB of HBM per device.

v0:
```python
import functools

import jax
import jax.numpy as jnp
from jax import lax
from jax.experimental import pallas as pl
from jax.experimental.pallas import tpu as pltpu
from jax.sharding import PartitionSpec as P

RH = 32
RW = 64
BH = 8
BW = 16
LANES = 128
BLOCK_ROWS = RH // BH
BLOCK_COLS = RW // BW
REGION_BLOCKS = BLOCK_ROWS * BLOCK_COLS
PAIRS = RW // 2
BLOCK_PAIRS = BW // 2
NATURAL = RH * RW // LANES
ROWS_IN_GROUP = LANES // RW
QUADS = BH // ROWS_IN_GROUP
BF16 = jnp.bfloat16
F32 = jnp.float32


def lanes(shape):
    return lax.broadcasted_iota(jnp.int32, shape, len(shape) - 1)


def cut(value, count):
    return [value[:, v * LANES : (v + 1) * LANES] for v in range(count)]


def one_hot(depth, target):
    row = lax.broadcasted_iota(jnp.int32, (depth, target.shape[1]), 0)
    return (row == target).astype(F32).astype(BF16)


def dot(a, b):
    return jnp.dot(a, b, preferred_element_type=F32)


def pairing():
    width = BLOCK_ROWS * LANES
    n = lanes((1, width))
    parity = n // LANES
    target = n % LANES // PAIRS * LANES + parity // 2 * RW + n % PAIRS * 2 + parity % 2
    return one_hot(width, target)


def to_paired(groups, matrix):
    channels = groups[0].shape[0]
    rows = [
        jnp.concatenate([groups[QUADS * br + j] for br in range(BLOCK_ROWS)], axis=1) for j in range(QUADS)
    ]
    moved = dot(jnp.concatenate(rows, axis=0), matrix).astype(BF16)
    out = []
    for j in range(QUADS):
        here = cut(moved[j * channels : (j + 1) * channels], BLOCK_ROWS)
        for q in range(ROWS_IN_GROUP):
            out.append(jnp.concatenate(here[2 * q : 2 * q + 2], axis=0))
    return out


def unpairing():
    width = BLOCK_ROWS * LANES
    n = lanes((1, width))
    column = n % RW
    target = (n % LANES // RW * 2 + column % 2) * LANES + n // LANES * PAIRS + column // 2
    return one_hot(width, target)


def to_natural(maps, matrix):
    channels = maps[0][0].shape[0] // 2
    rows = []
    for groups in maps:
        for j in range(QUADS):
            parts = []
            for q in range(ROWS_IN_GROUP):
                group = groups[ROWS_IN_GROUP * j + q]
                parts += [group[:channels], group[channels:]]
            rows.append(jnp.concatenate(parts, axis=1))
    moved = dot(jnp.concatenate(rows, axis=0), matrix).astype(BF16)
    out = []
    for m in range(len(maps)):
        here = [
            cut(moved[(m * QUADS + j) * channels : (m * QUADS + j + 1) * channels], BLOCK_ROWS)
            for j in range(QUADS)
        ]
        out.append([here[j][br] for br in range(BLOCK_ROWS) for j in range(QUADS)])
    return out


def lane_target(source, tile):
    slot = (source // REGION_BLOCKS + tile) % 2
    return slot * LANES + source % REGION_BLOCKS * BLOCK_PAIRS


def spread(index):
    row = lax.broadcasted_iota(jnp.int32, (REGION_BLOCKS, LANES), 0)
    places = (row == lanes((REGION_BLOCKS, LANES)) // BLOCK_PAIRS).astype(F32).astype(BF16)
    rows = jnp.broadcast_to(index.astype(F32), (REGION_BLOCKS, REGION_BLOCKS)).astype(BF16)
    return dot(rows, places)


def target_of(source, tile):
    return lane_target(source.astype(jnp.int32), tile) + lanes((1, LANES)) % BLOCK_PAIRS


def add_halo(stack):
    shape = (stack.shape[0], LANES)
    lane = lanes(shape)
    zero = jnp.zeros(shape, BF16)
    last = pltpu.roll(stack[:, BH * LANES : (BH + 1) * LANES], PAIRS, 1)
    first = pltpu.roll(stack[:, LANES : 2 * LANES], LANES - PAIRS, 1)
    stack[:, :LANES] = jnp.where(lane < PAIRS, zero, last)
    stack[:, (BH + 1) * LANES :] = jnp.where(lane >= LANES - PAIRS, zero, first)


def put_taps(stack, groups):
    channels = groups[0].shape[0] // 2
    shape = (channels, LANES)
    lane = lanes(shape)
    zero = jnp.zeros(shape, BF16)
    for i, group in enumerate(groups):
        columns = slice((i + 1) * LANES, (i + 2) * LANES)
        before = pltpu.roll(group[channels:], 1, 1)
        after = pltpu.roll(group[:channels], LANES - 1, 1)
        stack[channels : 3 * channels, columns] = group
        stack[:channels, columns] = jnp.where(lane % PAIRS == 0, zero, before)
        stack[3 * channels :, columns] = jnp.where(lane % PAIRS == PAIRS - 1, zero, after)
    add_halo(stack)


def put_warped(stack, own, other, target):
    channels = own.shape[0] // 2
    lane = lanes((1, LANES))
    before = jnp.where(lane % PAIRS == 0, -1, pltpu.roll(target, 1, 1))
    after = jnp.where(lane % PAIRS == PAIRS - 1, -1, pltpu.roll(target, LANES - 1, 1))
    depth = 2 * LANES
    even_pick = one_hot(depth, jnp.concatenate([target, after], axis=1))
    odd_pick = one_hot(depth, jnp.concatenate([before, target], axis=1))
    for rows, pick, places in (
        (slice(0, channels), even_pick, (1, 3)),
        (slice(channels, 2 * channels), odd_pick, (0, 2)),
    ):
        wide = [
            jnp.concatenate(
                [own[rows, i * LANES : (i + 1) * LANES], other[rows, i * LANES : (i + 1) * LANES]], axis=1
            )
            for i in range(BH)
        ]
        moved = dot(jnp.concatenate(wide, axis=0), pick).astype(BF16)
        for i in range(BH):
            columns = slice((i + 1) * LANES, (i + 2) * LANES)
            for half, place in enumerate(places):
                stack[place * channels : (place + 1) * channels, columns] = moved[
                    i * channels : (i + 1) * channels, half * LANES : (half + 1) * LANES
                ]
    add_halo(stack)


def convolve(stack, weight, start=None):
    out = []
    for t in range(0, BH, 2):
        total = None if start is None else start[:, t * LANES : (t + 2) * LANES]
        for a in range(3):
            part = dot(weight[a], stack[:, (t + a) * LANES : (t + a + 2) * LANES])
            total = part if total is None else total + part
        out += cut(total, 2)
    return out


def lrelu(groups):
    return [jnp.maximum(u, 0.1 * u).astype(BF16) for u in groups]


def chains(stacks, entry, starts, layers):
    both = range(2)
    hidden = [lrelu(convolve(stacks[d], entry.at[d], starts[d])) for d in both]
    for layer in range(layers.shape[1]):
        for d in both:
            put_taps(stacks[d], hidden[d])
        inner = [lrelu(convolve(stacks[d], layers.at[d, layer, 0])) for d in both]
        for d in both:
            put_taps(stacks[d], inner[d])
        update = [convolve(stacks[d], layers.at[d, layer, 1]) for d in both]
        hidden = [[(h.astype(F32) + u).astype(BF16) for h, u in zip(hidden[d], update[d])] for d in both]
    return hidden


def even_segment():
    return lax.axis_index("tm") % 2 == 0


def head_kernel(frames, forward_index, backward_index, payload, index, sem, index_sems):
    channels, pixels = frames.shape[-2:]
    copies = [pltpu.make_async_copy(frames.at[0, 0, 0], payload.at[:, :pixels], sem)]
    for d, source in enumerate((forward_index, backward_index)):
        copies.append(pltpu.make_async_copy(source, index.at[d], index_sems.at[d]))
    for copy in copies:
        copy.start()
    half = channels // 2
    for d in range(2):
        copies[1 + d].wait()
        source = spread(index[d, 0]).astype(BF16)
        for row in range(d * half, (d + 1) * half, REGION_BLOCKS):
            payload[row : row + REGION_BLOCKS, pixels:] = source
    copies[0].wait()


def pack_kernel(forward, backward, near_out, far_out):
    matrix = pairing()
    even = even_segment()
    packed = [to_paired(cut(source[0, 0], NATURAL), matrix) for source in (forward, backward)]
    for i, (f, b) in enumerate(zip(*packed)):
        columns = slice(i * LANES, (i + 1) * LANES)
        near_out[:, columns] = jnp.where(even, f, b)
        far_out[:, columns] = jnp.where(even, b, f)


def frame_kernel(frames, entry_frame, *rest):
    outs, stack = rest[:-1], rest[-1]
    matrix = pairing()
    channels = frames.shape[-2]
    for moment, out in enumerate(outs):
        put_taps(stack, to_paired(cut(frames[moment, 0, 0], NATURAL), matrix))
        for i, group in enumerate(convolve(stack, entry_frame)):
            for d in range(2):
                out[d, :, i * LANES : (i + 1) * LANES] = group[2 * d * channels : 2 * (d + 1) * channels]


def tap_weight(taps):
    zero = jnp.zeros_like(taps[0])
    return jnp.concatenate(
        [jnp.concatenate(taps + [zero], axis=1), jnp.concatenate([zero] + taps, axis=1)], axis=0
    )


def weights_kernel(fe, fb, be, bb, entry_frame, entry_warped, layers):
    channels = fe.shape[1]
    for d, (entry, blocks) in enumerate(((fe, fb), (be, bb))):
        for a in range(3):
            taps = [entry[3 * a + b] for b in range(3)]
            entry_frame[a, 2 * d * channels : 2 * (d + 1) * channels] = tap_weight(
                [t[:, :channels] for t in taps]
            )
            entry_warped[d, a] = tap_weight([t[:, channels:] for t in taps])
            for layer in range(blocks.shape[0]):
                for part in range(2):
                    layers[d, layer, part, a] = tap_weight(
                        [blocks[layer, part, 3 * a + b] for b in range(3)]
                    )


def by_direction(even, pair_side, other_side):
    first, second = pair_side[...], other_side[...]
    return jnp.where(even, second, first), jnp.where(even, first, second)


def near_frame_kernel(pair_frame, other_frame, entry_frame, out, lists, stack):
    matrix = pairing()
    even = even_segment()
    width = NATURAL * LANES
    channels = pair_frame.shape[0]
    half = channels // 2
    payloads = by_direction(even, pair_frame, other_frame)
    for d in range(2):
        put_taps(stack.at[d], to_paired(cut(payloads[d][:, :width], NATURAL), matrix))
        lists[d] = payloads[d][d * half : (d + 1) * half, width:]
    for d in range(2):
        weight = [entry_frame[a, 2 * d * channels : 2 * (d + 1) * channels] for a in range(3)]
        for i, group in enumerate(convolve(stack.at[d], weight)):
            out[d, :, i * LANES : (i + 1) * LANES] = group


def near_kernel(
    pair_own,
    pair_swapped,
    other_own,
    other_swapped,
    starts,
    lists,
    entry_warped,
    layers,
    forward_out,
    backward_out,
    forward_stack,
    backward_stack,
):
    even = even_segment()
    tile = lax.axis_index("tile")
    stacks = (forward_stack, backward_stack)
    owns = by_direction(even, pair_own, other_own)
    others = by_direction(even, pair_swapped, other_swapped)
    for d in range(2):
        source = lists[d].astype(F32)[:1]
        put_warped(stacks[d], owns[d], others[d], target_of(source, tile))
    hidden = chains(stacks, entry_warped, [starts.at[d] for d in range(2)], layers)
    for groups, out in zip(hidden, (forward_out, backward_out)):
        for i, group in enumerate(groups):
            out[:, i * LANES : (i + 1) * LANES] = group


def tick_kernel(
    moment,
    forward_index,
    backward_index,
    frames,
    first_own,
    first_swapped,
    second_own,
    second_swapped,
    starts,
    entry_warped,
    layers,
    mixing,
    *rest,
):
    *_, restored, forward_final, backward_final = rest[:-6] if moment > 0 else rest[:-6] + (None, None)
    forward_stack, backward_stack, finals, mixed, final_sems, mixed_sems = rest[-6:]
    stacks = (forward_stack, backward_stack)
    back = unpairing()
    tile = lax.axis_index("tile")
    owns, others = (first_own[...], second_own[...]), (first_swapped[...], second_swapped[...])
    if moment == 0:
        even = even_segment()
        owns = by_direction(even, first_own, second_own)
        others = by_direction(even, first_swapped, second_swapped)
    for d, index in enumerate((forward_index, backward_index)):
        put_warped(stacks[d], owns[d], others[d], target_of(spread(index[moment])[:1], tile))
    hidden = chains(stacks, entry_warped, [starts.at[d] for d in range(2)], layers)
    states = to_natural(hidden, back)
    copies = []
    if moment > 0:
        for d, out in enumerate((forward_final, backward_final)):
            for v, group in enumerate(states[d]):
                finals[d, :, v * LANES : (v + 1) * LANES] = group
            copies.append(pltpu.make_async_copy(finals.at[d], out, final_sems.at[d]))
            copies[-1].start()
    for part in range(2):
        count = NATURAL // 2
        for v in range(part * count, (part + 1) * count, 2):
            both = jnp.concatenate([jnp.concatenate(f[v : v + 2], axis=1) for f in states], axis=0)
            here = frames[moment, 0, 0, :, v * LANES : (v + 2) * LANES].astype(F32)
            mixed[:, v * LANES : (v + 2) * LANES] = (here + dot(mixing[...], both)).astype(BF16)
        columns = pl.ds(part * count * LANES, count * LANES)
        copies.append(
            pltpu.make_async_copy(mixed.at[:, columns], restored.at[moment, :, columns], mixed_sems.at[part])
        )
        copies[-1].start()
    for copy in copies:
        copy.wait()


VMEM = pl.BlockSpec(memory_space=pltpu.VMEM)
ANY = pl.BlockSpec(memory_space=pl.ANY)
PARAMS = pltpu.CompilerParams(vmem_limit_bytes=32 * 2**20)


def cost(flops, count):
    return pl.CostEstimate(flops=flops, bytes_accessed=count, transcendentals=0)


def head(frames, forward_source, backward_source):
    channels, pixels = frames.shape[-2:]
    return pl.pallas_call(
        head_kernel,
        out_shape=jax.ShapeDtypeStruct((channels, pixels + LANES), BF16),
        in_specs=[ANY] * 3,
        out_specs=VMEM,
        scratch_shapes=[
            pltpu.VMEM((2,) + forward_source.shape, jnp.int32),
            pltpu.SemaphoreType.DMA,
            pltpu.SemaphoreType.DMA((2,)),
        ],
        compiler_params=pltpu.CompilerParams(vmem_limit_bytes=60 * 2**20),
        cost_estimate=cost(2**30, 2**19),
        name="head",
    )(frames, forward_source, backward_source)


def pack(forward, backward):
    channels, pixels = forward.shape[-2:]
    shape = jax.ShapeDtypeStruct((2 * channels, pixels // 2), BF16)
    return pl.pallas_call(
        pack_kernel,
        out_shape=(shape, shape),
        in_specs=[VMEM] * 2,
        out_specs=(VMEM, VMEM),
        compiler_params=PARAMS,
        cost_estimate=cost(2**29, 2**19),
        name="pack",
    )(forward, backward)


def pair_weights(forward_entry, forward_blocks, backward_entry, backward_blocks):
    channels = forward_entry.shape[1]
    count = forward_blocks.shape[0]
    matrix = (2 * channels, 4 * channels)
    return pl.pallas_call(
        weights_kernel,
        out_shape=(
            jax.ShapeDtypeStruct((3, 4 * channels, 4 * channels), BF16),
            jax.ShapeDtypeStruct((2, 3) + matrix, BF16),
            jax.ShapeDtypeStruct((2, count, 2, 3) + matrix, BF16),
        ),
        in_specs=[VMEM] * 4,
        out_specs=(VMEM,) * 3,
        compiler_params=PARAMS,
        cost_estimate=cost(2**28, 2**19),
        name="pair_weights",
    )(forward_entry, forward_blocks, backward_entry, backward_blocks)


def stack_of(channels):
    return pltpu.VMEM((4 * channels, (BH + 2) * LANES), BF16)


def frame_parts(frames, entry_frame):
    channels, pixels = frames.shape[-2:]
    part = jax.ShapeDtypeStruct((2, 2 * channels, pixels // 2), F32)
    return pl.pallas_call(
        frame_kernel,
        out_shape=(part,) * frames.shape[0],
        in_specs=[VMEM] * 2,
        out_specs=(VMEM,) * frames.shape[0],
        scratch_shapes=[stack_of(channels)],
        compiler_params=PARAMS,
        cost_estimate=cost(2**31, 2**19),
        name="frame_parts",
    )(frames, entry_frame)


def near_frames(pair_frame, other_frame, entry_frame):
    channels, width = pair_frame.shape
    stack = stack_of(channels)
    return pl.pallas_call(
        near_frame_kernel,
        out_shape=(
            jax.ShapeDtypeStruct((2, 2 * channels, (width - LANES) // 2), F32),
            jax.ShapeDtypeStruct((2, channels // 2, LANES), BF16),
        ),
        in_specs=[VMEM] * 3,
        out_specs=(VMEM, VMEM),
        scratch_shapes=[pltpu.VMEM((2,) + stack.shape, BF16)],
        compiler_params=PARAMS,
        cost_estimate=cost(2**30, 2**19),
        name="near_frames",
    )(pair_frame, other_frame, entry_frame)


def near(pair_own, *rest):
    shape = pair_own.shape
    out = jax.ShapeDtypeStruct(shape, BF16)
    stack = stack_of(shape[0] // 2)
    return pl.pallas_call(
        near_kernel,
        out_shape=(out, out),
        in_specs=[VMEM] * (1 + len(rest)),
        out_specs=(VMEM, VMEM),
        scratch_shapes=[stack, stack],
        compiler_params=PARAMS,
        cost_estimate=cost(2**31, 2**19),
        name="near",
    )(pair_own, *rest)


def tick(moment, forward_index, backward_index, frames, *rest, earlier=None):
    channels, pixels = frames.shape[-2:]
    restored = jax.ShapeDtypeStruct((frames.shape[0], channels, pixels), BF16)
    state = jax.ShapeDtypeStruct((channels, pixels), BF16)
    operands = (forward_index, backward_index, frames, *rest)
    in_specs = [VMEM] * (3 + len(rest))
    aliases = {}
    if earlier is not None:
        aliases = {len(operands): 0}
        operands += (earlier,)
        in_specs.append(ANY)
    finals = (state, state) if moment > 0 else ()
    stack = stack_of(channels)
    return pl.pallas_call(
        functools.partial(tick_kernel, moment),
        out_shape=(restored,) + finals,
        in_specs=in_specs,
        out_specs=(ANY,) * (1 + len(finals)),
        scratch_shapes=[
            stack,
            stack,
            pltpu.VMEM((2, channels, pixels), BF16),
            pltpu.VMEM((channels, pixels), BF16),
            pltpu.SemaphoreType.DMA((2,)),
            pltpu.SemaphoreType.DMA((2,)),
        ],
        input_output_aliases=aliases,
        compiler_params=PARAMS,
        cost_estimate=cost(2**32, 2**19),
        name=f"tick_{moment}",
    )(*operands)


def sent(value, steps_even, steps_odd):
    count = lax.axis_size("tm")
    pairs = [(s, s + (steps_odd if s % 2 else steps_even)) for s in range(count)]
    return lax.ppermute(value, "tm", [(s, d) for s, d in pairs if 0 <= d < count])


def swapped(value):
    return lax.ppermute(value, "tile", [(0, 1), (1, 0)])


def later(value, *others):
    return lax.optimization_barrier((value, *others))[0]


def shards(
    frames,
    forward_carry,
    backward_carry,
    forward_source,
    backward_source,
    forward_entry,
    forward_blocks,
    backward_entry,
    backward_blocks,
    mixing_weight,
):
    payload = head(frames, forward_source, backward_source)
    pair_frame = sent(payload, 1, -1)
    near_state, far_state = pack(later(forward_carry, payload), backward_carry)
    pair_far = sent(far_state, -2, 2)
    other_far = sent(near_state, 2, -2)
    entry_frame, entry_warped, layers = pair_weights(
        later(forward_entry, near_state), forward_blocks, backward_entry, backward_blocks
    )
    parts = frame_parts(frames, later(entry_frame, pair_frame))
    other_frame = sent(pair_frame, 2, -2)
    pair_near = sent(later(near_state, pair_frame), 1, -1)
    other_near = sent(later(far_state, pair_frame), -1, 1)
    near_parts, lists = near_frames(pair_frame, other_frame, later(entry_frame, *parts))
    forward_one, backward_one = near(
        pair_far,
        swapped(later(pair_far, parts[0])),
        other_far,
        swapped(later(other_far, parts[0])),
        later(near_parts, pair_near),
        lists,
        entry_warped,
        layers,
    )
    restored, forward_final, backward_final = tick(
        1,
        forward_source,
        backward_source,
        frames,
        later(forward_one, other_near),
        swapped(forward_one),
        backward_one,
        swapped(backward_one),
        parts[1],
        entry_warped,
        layers,
        mixing_weight,
    )
    (restored,) = tick(
        0,
        forward_source,
        backward_source,
        frames,
        pair_near,
        swapped(pair_near),
        other_near,
        swapped(other_near),
        parts[0],
        entry_warped,
        layers,
        mixing_weight,
        earlier=restored,
    )
    return (restored[:, None, None], forward_final[None, None], backward_final[None, None])


def solution(mesh):
    placed = (
        P(None, ("groups", "tm"), "tile", None, None),
        P(("groups", "tm"), "tile", None, None),
        P(("groups", "tm"), "tile", None, None),
        P(None, ("groups", "tm"), "tile"),
        P(None, ("groups", "tm"), "tile"),
        P(),
        P(),
        P(),
        P(),
        P(),
    )
    return jax.shard_map(
        shards,
        mesh=mesh,
        in_specs=placed,
        out_specs=(
            P(None, ("groups", "tm"), "tile", None, None),
            P(("groups", "tm"), "tile", None, None),
            P(("groups", "tm"), "tile", None, None),
        ),
        check_vma=False,
    )
```

profile of v0, /device:TPU:17, one launch (start us, length us, event | category | flops | bytes accessed | tf_op | source)
XLA Modules:
  0.0 38.0 jit_solution(11959890200243713863)
XLA Ops:
  0.6 0.0 copy-start.3
  0.6 0.0 copy-start.4
  0.7 1.8 %head.1 = bf16[64,2176]{1,0:T(8,128)(2,1)} custom-call(bf16[2,1,1,64,2048]{4,3,2,1,0:T(8,128)(2,1)} %frames.7, s32[2,1,16]{2,1,0:T(1,128)} %forward_index.5, s32[2,1,16]{2,1,0:T(1,128)} %backward_index.5), custom_call_target="tpu_custom_call" | custom-call | flops 1073741824 | bytes 524288 | tf_op jit(solution)/shard_map/head/pallas_call | solution.py:368
  2.4 0.0 copy-start.1
  2.4 0.0 copy-start.2
  2.4 0.0 copy-start.5
  2.5 0.0 copy-start.6
  2.5 1.3 %collective-permute-start = (bf16[64,2176]{1,0:T(8,128)(2,1)}, bf16[64,2176]{1,0:T(8,128)(2,1)S(1)}, u32[]{:S(2)}, u32[]{:S(2)}) collective-permute-start(bf16[64,2176]{1,0:T(8,128)(2,1)} %head.1), channel_id=1, source_target_pairs={{0,2},{2,0},{4,6},{6,4},{8,10},{10,8},{12,14},{14,12},{1,3},{3,1},... | collective-permute-start | bytes 835592 | tf_op jit(solution)/shard_map/ppermute | solution.py:506
  3.8 0.0 copy-done.3
  3.8 0.0 copy-done.4
  3.8 0.5 %pack.1 = (bf16[128,1024]{1,0:T(8,128)(2,1)S(1)}, bf16[128,1024]{1,0:T(8,128)(2,1)S(1)}) custom-call(bf16[1,1,64,2048]{3,2,1,0:T(8,128)(2,1)S(1)} %copy-done.3, bf16[1,1,64,2048]{3,2,1,0:T(8,128)(2,1)S(1)} %copy-done.4), custom_call_target="tpu_custom_call" | custom-call | flops 536870912 | bytes 524288 | tf_op jit(solution)/shard_map/pack/pallas_call | solution.py:387
  4.3 0.0 copy-start
  4.3 3.3 %collective-permute-start.7 = (bf16[128,1024]{1,0:T(8,128)(2,1)S(1)}, bf16[128,1024]{1,0:T(8,128)(2,1)S(1)}, u32[]{:S(2)}, u32[]{:S(2)}) collective-permute-start(bf16[128,1024]{1,0:T(8,128)(2,1)S(1)} %get-tuple-element.29), channel_id=1, source_target_pairs={{0,4},{4,8},{6,2},{8,12},{10,6},{14,10},{1,5},{5,9},{7,3},{9,13},{... | collective-permute-start | bytes 786440 | tf_op jit(solution)/shard_map/ppermute | solution.py:506
  7.6 2.1 %collective-permute-start.5 = (bf16[128,1024]{1,0:T(8,128)(2,1)S(1)}, bf16[128,1024]{1,0:T(8,128)(2,1)S(1)}, u32[]{:S(2)}, u32[]{:S(2)}) collective-permute-start(bf16[128,1024]{1,0:T(8,128)(2,1)S(1)} %get-tuple-element.31), channel_id=1, source_target_pairs={{2,6},{4,0},{6,10},{8,4},{10,14},{12,8},{3,7},{5,1},{7,11},{9,5},{... | collective-permute-start | bytes 786440 | tf_op jit(solution)/shard_map/ppermute | solution.py:506
  9.7 0.0 copy-done.1
  9.7 0.0 copy-done.2
  9.8 0.0 copy-done.5
  9.8 0.0 copy-done.6
  9.8 0.3 pair_weights.1
  10.1 0.2 collective-permute-done.pair_frame
  10.3 1.2 %collective-permute-start.1 = (bf16[128,1024]{1,0:T(8,128)(2,1)S(1)}, bf16[128,1024]{1,0:T(8,128)(2,1)S(1)}, u32[]{:S(2)}, u32[]{:S(2)}) collective-permute-start(bf16[128,1024]{1,0:T(8,128)(2,1)S(1)} %get-tuple-element.29), channel_id=1, source_target_pairs={{0,2},{2,0},{4,6},{6,4},{8,10},{10,8},{12,14},{14,12},{1,3},{3,1},... | collective-permute-start | bytes 786440 | tf_op jit(solution)/shard_map/ppermute | solution.py:506
  11.5 3.2 %collective-permute-start.9 = (bf16[64,2176]{1,0:T(8,128)(2,1)S(1)}, bf16[64,2176]{1,0:T(8,128)(2,1)S(1)}, u32[]{:S(2)}, u32[]{:S(2)}) collective-permute-start(bf16[64,2176]{1,0:T(8,128)(2,1)S(1)} %collective-permute-done.pair_frame), channel_id=1, source_target_pairs={{0,4},{4,8},{6,2},{8,12},{10,6},{14,10},{1,5},{5,9},{7,3},{9,13},{... | collective-permute-start | bytes 835592 | tf_op jit(solution)/shard_map/ppermute | solution.py:506
  14.7 0.0 copy-done
  14.7 1.8 %frame_parts.1 = (f32[2,128,1024]{2,1,0:T(8,128)S(1)}, f32[2,128,1024]{2,1,0:T(8,128)S(1)}) custom-call(bf16[2,1,1,64,2048]{4,3,2,1,0:T(8,128)(2,1)S(1)} %copy-done, bf16[3,256,256]{2,1,0:T(8,128)(2,1)S(1)} %get-tuple-element.41.entry_frame), custom_call_target="tpu_custom_call" | custom-call | flops 2147483648 | bytes 524288 | tf_op jit(solution)/shard_map/frame_parts/pallas_call | solution.py:424
  16.6 0.0 collective-permute-done.7.other_own
  16.6 2.2 %collective-permute-start.8 = (bf16[128,1024]{1,0:T(8,128)(2,1)S(1)}, bf16[128,1024]{1,0:T(8,128)(2,1)S(1)}, u32[]{:S(2)}, u32[]{:S(2)}) collective-permute-start(bf16[128,1024]{1,0:T(8,128)(2,1)S(1)} %collective-permute-done.7.other_own), channel_id=1, source_target_pairs={{0,1},{1,0},{2,3},{3,2},{4,5},{5,4},{6,7},{7,6},{8,9},{9,8},{10,11... | collective-permute-start | bytes 786440 | tf_op jit(solution)/shard_map/ppermute | solution.py:510
  18.7 0.0 collective-permute-done.5.pair_own
  18.8 0.1 collective-permute-start.6
  18.8 1.9 %collective-permute-start.3 = (bf16[128,1024]{1,0:T(8,128)(2,1)S(1)}, bf16[128,1024]{1,0:T(8,128)(2,1)S(1)}, u32[]{:S(2)}, u32[]{:S(2)}) collective-permute-start(bf16[128,1024]{1,0:T(8,128)(2,1)S(1)} %get-tuple-element.31), channel_id=1, source_target_pairs={{2,4},{4,2},{6,8},{8,6},{10,12},{12,10},{3,5},{5,3},{7,9},{9,7},{1... | collective-permute-start | bytes 786440 | tf_op jit(solution)/shard_map/ppermute | solution.py:506
  20.8 0.0 collective-permute-done.9.other_frame
  20.8 1.1 %near_frames.1 = (f32[2,128,1024]{2,1,0:T(8,128)S(1)}, bf16[2,32,128]{2,1,0:T(8,128)(2,1)S(1)}) custom-call(bf16[64,2176]{1,0:T(8,128)(2,1)S(1)} %collective-permute-done.pair_frame, bf16[64,2176]{1,0:T(8,128)(2,1)S(1)} %collective-permute-done.9.other_frame, bf16[3,256,256]{2,1,0:T(8,128)(2,1)S(1)} %get-tuple-element.41.entry_frame), custom_call_target="tpu_custom_call" | custom-call | flops 1073741824 | bytes 524288 | tf_op jit(solution)/shard_map/near_frames/pallas_call | solution.py:439
  21.9 0.0 collective-permute-done.1.first_own
  21.9 0.0 collective-permute-done.8.other_swapped
  21.9 0.0 collective-permute-done.6.pair_swapped
  21.9 0.0 copy-start.7
  21.9 2.1 %near.1 = (bf16[128,1024]{1,0:T(8,128)(2,1)S(1)}, bf16[128,1024]{1,0:T(8,128)(2,1)S(1)}) custom-call(bf16[128,1024]{1,0:T(8,128)(2,1)S(1)} %collective-permute-done.5.pair_own, bf16[128,1024]{1,0:T(8,128)(2,1)S(1)} %collective-permute-done.6.pair_swapped, bf16[128,1024]{1,0:T(8,128)(2,1)S(1)} %collective-permute-done.7.other_own, ...), custom_call_target="tpu_custom_call" | custom-call | flops 2147483648 | bytes 524288 | tf_op jit(solution)/shard_map/near/pallas_call | solution.py:458
  24.0 0.0 copy-start.9
  24.0 0.0 copy-start.8
  24.0 1.8 %collective-permute-start.10 = (bf16[128,1024]{1,0:T(8,128)(2,1)S(1)}, bf16[128,1024]{1,0:T(8,128)(2,1)S(1)}, u32[]{:S(2)}, u32[]{:S(2)}) collective-permute-start(bf16[128,1024]{1,0:T(8,128)(2,1)S(1)} %get-tuple-element.46.first_own), channel_id=1, source_target_pairs={{0,1},{1,0},{2,3},{3,2},{4,5},{5,4},{6,7},{7,6},{8,9},{9,8},{10,11... | collective-permute-start | bytes 786440 | tf_op jit(solution)/shard_map/ppermute | solution.py:510
  25.8 0.1 collective-permute-start.11
  25.9 0.4 %collective-permute-start.2 = (bf16[128,1024]{1,0:T(8,128)(2,1)S(1)}, bf16[128,1024]{1,0:T(8,128)(2,1)S(1)}, u32[]{:S(2)}, u32[]{:S(2)}) collective-permute-start(bf16[128,1024]{1,0:T(8,128)(2,1)S(1)} %collective-permute-done.1.first_own), channel_id=1, source_target_pairs={{0,1},{1,0},{2,3},{3,2},{4,5},{5,4},{6,7},{7,6},{8,9},{9,8},{10,11... | collective-permute-start | bytes 786440 | tf_op jit(solution)/shard_map/ppermute | solution.py:510
  26.3 2.8 %collective-permute-done.3.second_own = bf16[128,1024]{1,0:T(8,128)(2,1)S(1)} collective-permute-done((bf16[128,1024]{1,0:T(8,128)(2,1)S(1)}, bf16[128,1024]{1,0:T(8,128)(2,1)S(1)}, u32[]{:S(2)}, u32[]{:S(2)}) %collective-permute-start.3) | collective-permute-done | bytes 262176 | tf_op jit(solution)/shard_map/ppermute | solution.py:506
  29.1 1.3 %collective-permute-start.4 = (bf16[128,1024]{1,0:T(8,128)(2,1)S(1)}, bf16[128,1024]{1,0:T(8,128)(2,1)S(1)}, u32[]{:S(2)}, u32[]{:S(2)}) collective-permute-start(bf16[128,1024]{1,0:T(8,128)(2,1)S(1)} %collective-permute-done.3.second_own), channel_id=1, source_target_pairs={{0,1},{1,0},{2,3},{3,2},{4,5},{5,4},{6,7},{7,6},{8,9},{9,8},{10,11... | collective-permute-start | bytes 786440 | tf_op jit(solution)/shard_map/ppermute | solution.py:510
  30.3 0.0 collective-permute-done.10.first_swapped
  30.3 0.0 collective-permute-done.11.second_swapped
  30.3 0.0 copy-done.7
  30.4 0.0 copy-done.9
  30.4 0.0 copy-done.8
  30.4 3.8 %tick_1.1 = (bf16[2,64,2048]{2,1,0:T(8,128)(2,1)}, bf16[64,2048]{1,0:T(8,128)(2,1)}, bf16[64,2048]{1,0:T(8,128)(2,1)}) custom-call(s32[2,1,16]{2,1,0:T(1,128)S(1)} %copy-done.8, s32[2,1,16]{2,1,0:T(1,128)S(1)} %copy-done.9, bf16[2,1,1,64,2048]{4,3,2,1,0:T(8,128)(2,1)S(1)} %copy-done, bf16[128,1024]{1,0:T(8,128)(2,1)S(1)} %get-tuple-element.46.first_own, ...), custom_call_target="tpu_custom_call" | custom-call | flops 4294967296 | bytes 524288 | tf_op jit(solution)/shard_map/tick_1/pallas_call | solution.py:483
  34.2 0.0 collective-permute-done.2.first_swapped
  34.2 0.0 collective-permute-done.4.second_swapped
  34.2 3.8 %tick_0.1 = bf16[2,64,2048]{2,1,0:T(8,128)(2,1)} custom-call(s32[2,1,16]{2,1,0:T(1,128)S(1)} %copy-done.8, s32[2,1,16]{2,1,0:T(1,128)S(1)} %copy-done.9, bf16[2,1,1,64,2048]{4,3,2,1,0:T(8,128)(2,1)S(1)} %copy-done, bf16[128,1024]{1,0:T(8,128)(2,1)S(1)} %collective-permute-done.1.first_own, ...), custom_call_target="tpu_custom_call", output_to_operand_aliasing={{}: (11, {})} | custom-call | flops 4294967296 | bytes 524288 | tf_op jit(solution)/shard_map/tick_0/pallas_call | solution.py:483
Async XLA Ops:
  0.6 3.1 %copy-start.3 = (bf16[1,1,64,2048]{3,2,1,0:T(8,128)(2,1)S(1)}, bf16[1,1,64,2048]{3,2,1,0:T(8,128)(2,1)}, u32[]{:S(2)}) copy-start(bf16[1,1,64,2048]{3,2,1,0:T(8,128)(2,1)} %forward) | copy-start | bytes 786436
  0.6 3.1 %copy-start.4 = (bf16[1,1,64,2048]{3,2,1,0:T(8,128)(2,1)S(1)}, bf16[1,1,64,2048]{3,2,1,0:T(8,128)(2,1)}, u32[]{:S(2)}) copy-start(bf16[1,1,64,2048]{3,2,1,0:T(8,128)(2,1)} %backward.1) | copy-start | bytes 786436
  2.4 7.3 %copy-start.1 = (bf16[1,2,9,64,64]{4,3,2,1,0:T(8,128)(2,1)S(1)}, bf16[1,2,9,64,64]{4,3,2,1,0:T(8,128)(2,1)}, u32[]{:S(2)}) copy-start(bf16[1,2,9,64,64]{4,3,2,1,0:T(8,128)(2,1)} %fb.1) | copy-start | bytes 442372
  2.4 7.3 %copy-start.2 = (bf16[1,2,9,64,64]{4,3,2,1,0:T(8,128)(2,1)S(1)}, bf16[1,2,9,64,64]{4,3,2,1,0:T(8,128)(2,1)}, u32[]{:S(2)}) copy-start(bf16[1,2,9,64,64]{4,3,2,1,0:T(8,128)(2,1)} %bb.1) | copy-start | bytes 442372
  2.4 7.3 %copy-start.5 = (bf16[9,64,128]{2,1,0:T(8,128)(2,1)S(1)}, bf16[9,64,128]{2,1,0:T(8,128)(2,1)}, u32[]{:S(2)}) copy-start(bf16[9,64,128]{2,1,0:T(8,128)(2,1)} %fe) | copy-start | bytes 442372
  2.5 7.3 %copy-start.6 = (bf16[9,64,128]{2,1,0:T(8,128)(2,1)S(1)}, bf16[9,64,128]{2,1,0:T(8,128)(2,1)}, u32[]{:S(2)}) copy-start(bf16[9,64,128]{2,1,0:T(8,128)(2,1)} %be.1) | copy-start | bytes 442372
  2.5 7.8 %collective-permute-start = (bf16[64,2176]{1,0:T(8,128)(2,1)}, bf16[64,2176]{1,0:T(8,128)(2,1)S(1)}, u32[]{:S(2)}, u32[]{:S(2)}) collective-permute-start(bf16[64,2176]{1,0:T(8,128)(2,1)} %head.1), channel_id=1, source_target_pairs={{0,2},{2,0},{4,6},{6,4},{8,10},{10,8},{12,14},{14,12},{1,3},{3,1},... | collective-permute-start | bytes 835592 | tf_op jit(solution)/shard_map/ppermute | solution.py:506
  4.3 10.4 %copy-start = (bf16[2,1,1,64,2048]{4,3,2,1,0:T(8,128)(2,1)S(1)}, bf16[2,1,1,64,2048]{4,3,2,1,0:T(8,128)(2,1)}, u32[]{:S(2)}) copy-start(bf16[2,1,1,64,2048]{4,3,2,1,0:T(8,128)(2,1)} %frames.7) | copy-start | bytes 1572868
  4.3 12.3 %collective-permute-start.7 = (bf16[128,1024]{1,0:T(8,128)(2,1)S(1)}, bf16[128,1024]{1,0:T(8,128)(2,1)S(1)}, u32[]{:S(2)}, u32[]{:S(2)}) collective-permute-start(bf16[128,1024]{1,0:T(8,128)(2,1)S(1)} %get-tuple-element.29), channel_id=1, source_target_pairs={{0,4},{4,8},{6,2},{8,12},{10,6},{14,10},{1,5},{5,9},{7,3},{9,13},{... | collective-permute-start | bytes 786440 | tf_op jit(solution)/shard_map/ppermute | solution.py:506
  7.6 11.1 %collective-permute-start.5 = (bf16[128,1024]{1,0:T(8,128)(2,1)S(1)}, bf16[128,1024]{1,0:T(8,128)(2,1)S(1)}, u32[]{:S(2)}, u32[]{:S(2)}) collective-permute-start(bf16[128,1024]{1,0:T(8,128)(2,1)S(1)} %get-tuple-element.31), channel_id=1, source_target_pairs={{2,6},{4,0},{6,10},{8,4},{10,14},{12,8},{3,7},{5,1},{7,11},{9,5},{... | collective-permute-start | bytes 786440 | tf_op jit(solution)/shard_map/ppermute | solution.py:506
  10.3 11.6 %collective-permute-start.1 = (bf16[128,1024]{1,0:T(8,128)(2,1)S(1)}, bf16[128,1024]{1,0:T(8,128)(2,1)S(1)}, u32[]{:S(2)}, u32[]{:S(2)}) collective-permute-start(bf16[128,1024]{1,0:T(8,128)(2,1)S(1)} %get-tuple-element.29), channel_id=1, source_target_pairs={{0,2},{2,0},{4,6},{6,4},{8,10},{10,8},{12,14},{14,12},{1,3},{3,1},... | collective-permute-start | bytes 786440 | tf_op jit(solution)/shard_map/ppermute | solution.py:506
  11.5 9.3 %collective-permute-start.9 = (bf16[64,2176]{1,0:T(8,128)(2,1)S(1)}, bf16[64,2176]{1,0:T(8,128)(2,1)S(1)}, u32[]{:S(2)}, u32[]{:S(2)}) collective-permute-start(bf16[64,2176]{1,0:T(8,128)(2,1)S(1)} %collective-permute-done.pair_frame), channel_id=1, source_target_pairs={{0,4},{4,8},{6,2},{8,12},{10,6},{14,10},{1,5},{5,9},{7,3},{9,13},{... | collective-permute-start | bytes 835592 | tf_op jit(solution)/shard_map/ppermute | solution.py:506
  16.6 5.3 %collective-permute-start.8 = (bf16[128,1024]{1,0:T(8,128)(2,1)S(1)}, bf16[128,1024]{1,0:T(8,128)(2,1)S(1)}, u32[]{:S(2)}, u32[]{:S(2)}) collective-permute-start(bf16[128,1024]{1,0:T(8,128)(2,1)S(1)} %collective-permute-done.7.other_own), channel_id=1, source_target_pairs={{0,1},{1,0},{2,3},{3,2},{4,5},{5,4},{6,7},{7,6},{8,9},{9,8},{10,11... | collective-permute-start | bytes 786440 | tf_op jit(solution)/shard_map/ppermute | solution.py:510
  18.8 3.1 %collective-permute-start.6 = (bf16[128,1024]{1,0:T(8,128)(2,1)S(1)}, bf16[128,1024]{1,0:T(8,128)(2,1)S(1)}, u32[]{:S(2)}, u32[]{:S(2)}) collective-permute-start(bf16[128,1024]{1,0:T(8,128)(2,1)S(1)} %collective-permute-done.5.pair_own), channel_id=1, source_target_pairs={{0,1},{1,0},{2,3},{3,2},{4,5},{5,4},{6,7},{7,6},{8,9},{9,8},{10,11... | collective-permute-start | bytes 786440 | tf_op jit(solution)/shard_map/ppermute | solution.py:510
  18.8 10.2 %collective-permute-start.3 = (bf16[128,1024]{1,0:T(8,128)(2,1)S(1)}, bf16[128,1024]{1,0:T(8,128)(2,1)S(1)}, u32[]{:S(2)}, u32[]{:S(2)}) collective-permute-start(bf16[128,1024]{1,0:T(8,128)(2,1)S(1)} %get-tuple-element.31), channel_id=1, source_target_pairs={{2,4},{4,2},{6,8},{8,6},{10,12},{12,10},{3,5},{5,3},{7,9},{9,7},{1... | collective-permute-start | bytes 786440 | tf_op jit(solution)/shard_map/ppermute | solution.py:506
  21.9 8.5 %copy-start.7 = (bf16[64,128]{1,0:T(8,128)(2,1)S(1)}, bf16[64,128]{1,0:T(8,128)(2,1)}, u32[]{:S(2)}) copy-start(bf16[64,128]{1,0:T(8,128)(2,1)} %mixing.3) | copy-start | bytes 49156
  24.0 6.3 %copy-start.9 = (s32[2,1,16]{2,1,0:T(1,128)S(1)}, s32[2,1,16]{2,1,0:T(1,128)}, u32[]{:S(2)}) copy-start(s32[2,1,16]{2,1,0:T(1,128)} %backward_index.5) | copy-start | bytes 388
  24.0 6.3 %copy-start.8 = (s32[2,1,16]{2,1,0:T(1,128)S(1)}, s32[2,1,16]{2,1,0:T(1,128)}, u32[]{:S(2)}) copy-start(s32[2,1,16]{2,1,0:T(1,128)} %forward_index.5) | copy-start | bytes 388
  24.0 6.3 %collective-permute-start.10 = (bf16[128,1024]{1,0:T(8,128)(2,1)S(1)}, bf16[128,1024]{1,0:T(8,128)(2,1)S(1)}, u32[]{:S(2)}, u32[]{:S(2)}) collective-permute-start(bf16[128,1024]{1,0:T(8,128)(2,1)S(1)} %get-tuple-element.46.first_own), channel_id=1, source_target_pairs={{0,1},{1,0},{2,3},{3,2},{4,5},{5,4},{6,7},{7,6},{8,9},{9,8},{10,11... | collective-permute-start | bytes 786440 | tf_op jit(solution)/shard_map/ppermute | solution.py:510
  25.8 4.6 %collective-permute-start.11 = (bf16[128,1024]{1,0:T(8,128)(2,1)S(1)}, bf16[128,1024]{1,0:T(8,128)(2,1)S(1)}, u32[]{:S(2)}, u32[]{:S(2)}) collective-permute-start(bf16[128,1024]{1,0:T(8,128)(2,1)S(1)} %get-tuple-element.47.second_own), channel_id=1, source_target_pairs={{0,1},{1,0},{2,3},{3,2},{4,5},{5,4},{6,7},{7,6},{8,9},{9,8},{10,11... | collective-permute-start | bytes 786440 | tf_op jit(solution)/shard_map/ppermute | solution.py:510
  25.9 8.3 %collective-permute-start.2 = (bf16[128,1024]{1,0:T(8,128)(2,1)S(1)}, bf16[128,1024]{1,0:T(8,128)(2,1)S(1)}, u32[]{:S(2)}, u32[]{:S(2)}) collective-permute-start(bf16[128,1024]{1,0:T(8,128)(2,1)S(1)} %collective-permute-done.1.first_own), channel_id=1, source_target_pairs={{0,1},{1,0},{2,3},{3,2},{4,5},{5,4},{6,7},{7,6},{8,9},{9,8},{10,11... | collective-permute-start | bytes 786440 | tf_op jit(solution)/shard_map/ppermute | solution.py:510
  29.1 5.1 %collective-permute-start.4 = (bf16[128,1024]{1,0:T(8,128)(2,1)S(1)}, bf16[128,1024]{1,0:T(8,128)(2,1)S(1)}, u32[]{:S(2)}, u32[]{:S(2)}) collective-permute-start(bf16[128,1024]{1,0:T(8,128)(2,1)S(1)} %collective-permute-done.3.second_own), channel_id=1, source_target_pairs={{0,1},{1,0},{2,3},{3,2},{4,5},{5,4},{6,7},{7,6},{8,9},{9,8},{10,11... | collective-permute-start | bytes 786440 | tf_op jit(solution)/shard_map/ppermute | solution.py:510
where the time goes:
time: 38.2 us; the launch traced here: 38 us
  starting transfers between devices  18.8 us (49%)
  Pallas kernels  15.2 us (40%)
  waiting for transfers between devices  2.99 us (8%)
  between operations  0.91 us (2%)
    ppermute x6, starting transfers between devices, sent(): lax.ppermute(value, 'tm', [(s, d) for s, d in pairs if 0 <= d < count])  13.1 us
    pallas_call x2, Pallas kernels, tick(): pl.pallas_call(functools.partial(tick_kernel, moment), out_shape=(restore...  7.6 us
    ppermute x6, starting transfers between devices, swapped(): return lax.ppermute(value, 'tile', [(0, 1), (1, 0)])  5.79 us
    ppermute x6, waiting for transfers between devices, sent(): lax.ppermute(value, 'tm', [(s, d) for s, d in pairs if 0 <= d < count])  2.97 us
    pallas_call x1, Pallas kernels, near(): pl.pallas_call(near_kernel, out_shape=(out, out), in_specs=[VMEM] * (1 +...  2.1 us
    pallas_call x1, Pallas kernels, frame_parts(): pl.pallas_call(frame_kernel, out_shape=(part,) * frames.shape[0], in_spec...  1.85 us
    pallas_call x1, Pallas kernels, head(): pl.pallas_call(head_kernel, out_shape=jax.ShapeDtypeStruct((channels, pix...  1.76 us
    pallas_call x1, Pallas kernels, near_frames(): pl.pallas_call(near_frame_kernel, out_shape=(jax.ShapeDtypeStruct((2, 2 *...  1.09 us
  transfers between devices with their start and end apart: 12, of which 2 were waited for; matrix products, arithmetic and copies ran while one was open for 0% of the time, Pallas kernels for 25%

commit v1 on v0

v1 whole, which is shorter than its diff:
```python
import functools

import jax
import jax.numpy as jnp
from jax import lax
from jax.experimental import pallas as pl
from jax.experimental.pallas import tpu as pltpu
from jax.sharding import PartitionSpec as P

RH = 32
RW = 64
BH = 8
BW = 16
LANES = 128
BLOCK_ROWS = RH // BH
BLOCK_COLS = RW // BW
REGION_BLOCKS = BLOCK_ROWS * BLOCK_COLS
PAIRS = RW // 2
BLOCK_PAIRS = BW // 2
NATURAL = RH * RW // LANES
ROWS_IN_GROUP = LANES // RW
QUADS = BH // ROWS_IN_GROUP
BF16 = jnp.bfloat16
F32 = jnp.float32


def lanes(shape):
    return lax.broadcasted_iota(jnp.int32, shape, len(shape) - 1)


def cut(value, count):
    return [value[:, v * LANES : (v + 1) * LANES] for v in range(count)]


def one_hot(depth, target):
    row = lax.broadcasted_iota(jnp.int32, (depth, target.shape[1]), 0)
    return (row == target).astype(F32).astype(BF16)


def dot(a, b):
    return jnp.dot(a, b, preferred_element_type=F32)


def pairing():
    width = BLOCK_ROWS * LANES
    n = lanes((1, width))
    parity = n // LANES
    target = n % LANES // PAIRS * LANES + parity // 2 * RW + n % PAIRS * 2 + parity % 2
    return one_hot(width, target)


def to_paired(groups, matrix):
    channels = groups[0].shape[0]
    rows = [
        jnp.concatenate([groups[QUADS * br + j] for br in range(BLOCK_ROWS)], axis=1) for j in range(QUADS)
    ]
    moved = dot(jnp.concatenate(rows, axis=0), matrix).astype(BF16)
    out = []
    for j in range(QUADS):
        here = cut(moved[j * channels : (j + 1) * channels], BLOCK_ROWS)
        for q in range(ROWS_IN_GROUP):
            out.append(jnp.concatenate(here[2 * q : 2 * q + 2], axis=0))
    return out


def unpairing():
    width = BLOCK_ROWS * LANES
    n = lanes((1, width))
    column = n % RW
    target = (n % LANES // RW * 2 + column % 2) * LANES + n // LANES * PAIRS + column // 2
    return one_hot(width, target)


def to_natural(maps, matrix):
    channels = maps[0][0].shape[0] // 2
    rows = []
    for groups in maps:
        for j in range(QUADS):
            parts = []
            for q in range(ROWS_IN_GROUP):
                group = groups[ROWS_IN_GROUP * j + q]
                parts += [group[:channels], group[channels:]]
            rows.append(jnp.concatenate(parts, axis=1))
    moved = dot(jnp.concatenate(rows, axis=0), matrix).astype(BF16)
    out = []
    for m in range(len(maps)):
        here = [
            cut(moved[(m * QUADS + j) * channels : (m * QUADS + j + 1) * channels], BLOCK_ROWS)
            for j in range(QUADS)
        ]
        out.append([here[j][br] for br in range(BLOCK_ROWS) for j in range(QUADS)])
    return out


def lane_target(source, tile):
    slot = (source // REGION_BLOCKS + tile) % 2
    return slot * LANES + source % REGION_BLOCKS * BLOCK_PAIRS


def spread(index):
    row = lax.broadcasted_iota(jnp.int32, (REGION_BLOCKS, LANES), 0)
    places = (row == lanes((REGION_BLOCKS, LANES)) // BLOCK_PAIRS).astype(F32).astype(BF16)
    rows = jnp.broadcast_to(index.astype(F32), (REGION_BLOCKS, REGION_BLOCKS)).astype(BF16)
    return dot(rows, places)


def target_of(source, tile):
    return lane_target(source.astype(jnp.int32), tile) + lanes((1, LANES)) % BLOCK_PAIRS


def put_taps(stack, i, group):
    channels = group.shape[0] // 2
    shape = (channels, LANES)
    lane = lanes(shape)
    zero = jnp.zeros(shape, BF16)
    before = jnp.where(lane % PAIRS == 0, zero, pltpu.roll(group[channels:], 1, 1))
    after = jnp.where(lane % PAIRS == PAIRS - 1, zero, pltpu.roll(group[:channels], LANES - 1, 1))
    put_rows(stack, i, (before, group[:channels], group[channels:], after))


def put_rows(stack, i, parts):
    value = jnp.concatenate(parts, axis=0)
    stack[:, (i + 1) * LANES : (i + 2) * LANES] = value
    lane = lanes(value.shape)
    zero = jnp.zeros(value.shape, BF16)
    if i == BH - 1:
        stack[:, :LANES] = jnp.where(lane < PAIRS, zero, pltpu.roll(value, PAIRS, 1))
    if i == 0:
        below = pltpu.roll(value, LANES - PAIRS, 1)
        stack[:, (BH + 1) * LANES :] = jnp.where(lane >= LANES - PAIRS, zero, below)


def picks_of(target):
    lane = lanes((1, LANES))
    before = jnp.where(lane % PAIRS == 0, -1, pltpu.roll(target, 1, 1))
    after = jnp.where(lane % PAIRS == PAIRS - 1, -1, pltpu.roll(target, LANES - 1, 1))
    depth = 2 * LANES
    return (
        one_hot(depth, jnp.concatenate([target, after], axis=1)),
        one_hot(depth, jnp.concatenate([before, target], axis=1)),
    )


def put_warped(stack, tiles, picks):
    channels = tiles[0][0].shape[0] // 2
    moved = []
    for half in range(2):
        rows = slice(half * channels, (half + 1) * channels)
        wide = [jnp.concatenate([t[i][rows] for t in tiles], axis=1) for i in range(BH)]
        moved.append(dot(jnp.concatenate(wide, axis=0), picks[half]).astype(BF16))
    for i in range(BH):
        even, odd = [m[i * channels : (i + 1) * channels] for m in moved]
        put_rows(stack, i, (odd[:, :LANES], even[:, :LANES], odd[:, LANES:], even[:, LANES:]))


def convolve(stack, weight, start=None):
    for t in (2, 4, 0, 6):
        total = None if start is None else start[:, t * LANES : (t + 2) * LANES]
        for a in range(3):
            part = dot(weight[a], stack[:, (t + a) * LANES : (t + a + 2) * LANES])
            total = part if total is None else total + part
        yield t, total[:, :LANES]
        yield t + 1, total[:, LANES:]


def lrelu(u):
    return jnp.maximum(u, 0.1 * u).astype(BF16)


def both_convolve(stacks, weights, starts):
    for here in zip(*(convolve(*operands) for operands in zip(stacks, weights, starts))):
        yield here[0][0], [u for _, u in here]


def chains(first, second, entry, starts, layers):
    both = range(2)
    nothing = (None, None)
    hidden = [[None] * BH for _ in both]
    for i, values in both_convolve(first, [entry.at[d] for d in both], starts):
        for d in both:
            hidden[d][i] = lrelu(values[d])
            put_taps(second[d], i, hidden[d][i])
    for layer in range(layers.shape[1]):
        for i, values in both_convolve(second, [layers.at[d, layer, 0] for d in both], nothing):
            for d in both:
                put_taps(first[d], i, lrelu(values[d]))
        for i, values in both_convolve(first, [layers.at[d, layer, 1] for d in both], nothing):
            for d in both:
                hidden[d][i] = (hidden[d][i].astype(F32) + values[d]).astype(BF16)
                if layer + 1 < layers.shape[1]:
                    put_taps(second[d], i, hidden[d][i])
    return hidden


def even_segment():
    return lax.axis_index("tm") % 2 == 0


def head_kernel(frames, forward_index, backward_index, payload, index, sem, index_sems):
    channels, pixels = frames.shape[-2:]
    copies = [pltpu.make_async_copy(frames.at[0, 0, 0], payload.at[:, :pixels], sem)]
    for d, source in enumerate((forward_index, backward_index)):
        copies.append(pltpu.make_async_copy(source, index.at[d], index_sems.at[d]))
    for copy in copies:
        copy.start()
    half = channels // 2
    for d in range(2):
        copies[1 + d].wait()
        source = spread(index[d, 0]).astype(BF16)
        for row in range(d * half, (d + 1) * half, REGION_BLOCKS):
            payload[row : row + REGION_BLOCKS, pixels:] = source
    copies[0].wait()


def pack_kernel(forward, backward, near_out, far_out):
    matrix = pairing()
    even = even_segment()
    packed = [to_paired(cut(source[0, 0], NATURAL), matrix) for source in (forward, backward)]
    for i, (f, b) in enumerate(zip(*packed)):
        columns = slice(i * LANES, (i + 1) * LANES)
        near_out[:, columns] = jnp.where(even, f, b)
        far_out[:, columns] = jnp.where(even, b, f)


def frame_kernel(frames, entry_frame, matrix, *rest):
    paired, parts, stack = rest
    channels = frames.shape[-2]
    for moment in range(frames.shape[0]):
        for i, group in enumerate(to_paired(cut(frames[moment, 0, 0], NATURAL), matrix[...])):
            put_taps(stack, i, group)
            paired[moment, :, i * LANES : (i + 1) * LANES] = group
        for i, group in convolve(stack, entry_frame):
            for d in range(2):
                parts[moment, d, :, i * LANES : (i + 1) * LANES] = group[
                    2 * d * channels : 2 * (d + 1) * channels
                ]


def tap_weight(taps):
    zero = jnp.zeros_like(taps[0])
    return jnp.concatenate(
        [jnp.concatenate(taps + [zero], axis=1), jnp.concatenate([zero] + taps, axis=1)], axis=0
    )


def block_diagonal(weight):
    zero = jnp.zeros_like(weight)
    return jnp.concatenate(
        [jnp.concatenate([weight, zero], axis=1), jnp.concatenate([zero, weight], axis=1)], axis=0
    )


def weights_kernel(fe, fb, be, bb, mixing, entry_frame, entry_warped, layers, mix_pair, matrix, back):
    channels = fe.shape[1]
    matrix[...] = pairing()
    back[...] = unpairing()
    for d, (entry, blocks) in enumerate(((fe, fb), (be, bb))):
        mix_pair[d] = block_diagonal(mixing[:, d * channels : (d + 1) * channels])
        for a in range(3):
            taps = [entry[3 * a + b] for b in range(3)]
            entry_frame[a, 2 * d * channels : 2 * (d + 1) * channels] = tap_weight(
                [t[:, :channels] for t in taps]
            )
            entry_warped[d, a] = tap_weight([t[:, channels:] for t in taps])
            for layer in range(blocks.shape[0]):
                for part in range(2):
                    layers[d, layer, part, a] = tap_weight(
                        [blocks[layer, part, 3 * a + b] for b in range(3)]
                    )


def picks_kernel(forward_index, backward_index, out):
    tile = lax.axis_index("tile")
    for moment in range(out.shape[0]):
        for d, index in enumerate((forward_index, backward_index)):
            for half, pick in enumerate(picks_of(target_of(spread(index[moment])[:1], tile))):
                out[moment, d, half] = pick


def by_direction(even, pair_side, other_side):
    first, second = pair_side[...], other_side[...]
    return jnp.where(even, second, first), jnp.where(even, first, second)


def near_frame_kernel(pair_frame, other_frame, entry_frame, matrix, out, picks, stack):
    even = even_segment()
    tile = lax.axis_index("tile")
    width = NATURAL * LANES
    channels = pair_frame.shape[0]
    half = channels // 2
    payloads = by_direction(even, pair_frame, other_frame)
    for d in range(2):
        for i, group in enumerate(to_paired(cut(payloads[d][:, :width], NATURAL), matrix[...])):
            put_taps(stack.at[d], i, group)
        source = payloads[d][d * half : d * half + REGION_BLOCKS, width:].astype(F32)[:1]
        for part, pick in enumerate(picks_of(target_of(source, tile))):
            picks[d, part] = pick
    for d in range(2):
        weight = [entry_frame[a, 2 * d * channels : 2 * (d + 1) * channels] for a in range(3)]
        for i, group in convolve(stack.at[d], weight):
            out[d, :, i * LANES : (i + 1) * LANES] = group


def near_kernel(
    pair_own,
    pair_swapped,
    other_own,
    other_swapped,
    starts,
    picks,
    entry_warped,
    layers,
    forward_out,
    backward_out,
    *stacks,
):
    even = even_segment()
    firsts, seconds = stacks[:2], stacks[2:]
    owns = by_direction(even, pair_own, other_own)
    others = by_direction(even, pair_swapped, other_swapped)
    for d in range(2):
        put_warped(firsts[d], (cut(owns[d], BH), cut(others[d], BH)), picks[d])
    hidden = chains(firsts, seconds, entry_warped, [starts.at[d] for d in range(2)], layers)
    for groups, out in zip(hidden, (forward_out, backward_out)):
        for i, group in enumerate(groups):
            out[:, i * LANES : (i + 1) * LANES] = group


def mix(weight, state, total):
    out = []
    for i in range(0, BH, 2):
        wide = dot(weight, jnp.concatenate(state[i : i + 2], axis=1))
        out += [total[i] + wide[:, :LANES], total[i + 1] + wide[:, LANES:]]
    return out


def rounded(groups):
    return [u.astype(BF16) for u in groups]


def put_natural(out, groups):
    for v, group in enumerate(groups):
        out[:, v * LANES : (v + 1) * LANES] = group


def tick_kernel(
    moment,
    first_own,
    first_swapped,
    second_own,
    second_swapped,
    picks,
    paired,
    parts,
    entry_warped,
    layers,
    mix_pair,
    back,
    *rest,
):
    *_, restored, forward_final, backward_final = rest[:-8] if moment > 0 else rest[:-8] + (None, None)
    *stacks, finals, mixed, final_sems, mixed_sem = rest[-8:]
    firsts, seconds = stacks[:2], stacks[2:]
    owns, others = (first_own[...], second_own[...]), (first_swapped[...], second_swapped[...])
    if moment == 0:
        even = even_segment()
        owns = by_direction(even, first_own, second_own)
        others = by_direction(even, first_swapped, second_swapped)
    for d in range(2):
        put_warped(firsts[d], (cut(owns[d], BH), cut(others[d], BH)), picks[moment, d])
    hidden = chains(firsts, seconds, entry_warped, [parts.at[moment, d] for d in range(2)], layers)
    total = cut(paired[moment].astype(F32), BH)
    for d in range(2):
        total = mix(mix_pair[d], hidden[d], total)
    natural = to_natural([rounded(total)] + (hidden if moment > 0 else []), back[...])
    put_natural(mixed, natural[0])
    copies = [pltpu.make_async_copy(mixed, restored.at[moment], mixed_sem)]
    copies[0].start()
    for d, groups in enumerate(natural[1:]):
        put_natural(finals.at[d], groups)
        out = (forward_final, backward_final)[d]
        copies.append(pltpu.make_async_copy(finals.at[d], out, final_sems.at[d]))
        copies[-1].start()
    for copy in copies:
        copy.wait()


VMEM = pl.BlockSpec(memory_space=pltpu.VMEM)
ANY = pl.BlockSpec(memory_space=pl.ANY)
PARAMS = pltpu.CompilerParams(vmem_limit_bytes=32 * 2**20)


def cost(flops, count):
    return pl.CostEstimate(flops=flops, bytes_accessed=count, transcendentals=0)


def head(frames, forward_source, backward_source):
    channels, pixels = frames.shape[-2:]
    return pl.pallas_call(
        head_kernel,
        out_shape=jax.ShapeDtypeStruct((channels, pixels + LANES), BF16),
        in_specs=[ANY] * 3,
        out_specs=VMEM,
        scratch_shapes=[
            pltpu.VMEM((2,) + forward_source.shape, jnp.int32),
            pltpu.SemaphoreType.DMA,
            pltpu.SemaphoreType.DMA((2,)),
        ],
        compiler_params=pltpu.CompilerParams(vmem_limit_bytes=62 * 2**20),
        cost_estimate=cost(2**30, 2**19),
        name="head",
    )(frames, forward_source, backward_source)


def pack(forward, backward):
    channels, pixels = forward.shape[-2:]
    shape = jax.ShapeDtypeStruct((2 * channels, pixels // 2), BF16)
    return pl.pallas_call(
        pack_kernel,
        out_shape=(shape, shape),
        in_specs=[VMEM] * 2,
        out_specs=(VMEM, VMEM),
        compiler_params=PARAMS,
        cost_estimate=cost(2**29, 2**19),
        name="pack",
    )(forward, backward)


def pair_weights(forward_entry, forward_blocks, backward_entry, backward_blocks, mixing):
    channels = forward_entry.shape[1]
    count = forward_blocks.shape[0]
    tall, wide, square = 2 * channels, 4 * channels, BLOCK_ROWS * LANES
    shapes = (
        (3, wide, wide),
        (2, 3, tall, wide),
        (2, count, 2, 3, tall, wide),
        (2, tall, tall),
        (square, square),
        (square, square),
    )
    return pl.pallas_call(
        weights_kernel,
        out_shape=tuple(jax.ShapeDtypeStruct(shape, BF16) for shape in shapes),
        in_specs=[VMEM] * 5,
        out_specs=(VMEM,) * len(shapes),
        compiler_params=PARAMS,
        cost_estimate=cost(2**29, 2**20),
        name="pair_weights",
    )(forward_entry, forward_blocks, backward_entry, backward_blocks, mixing)


def all_picks(forward_source, backward_source):
    return pl.pallas_call(
        picks_kernel,
        out_shape=jax.ShapeDtypeStruct((forward_source.shape[0], 2, 2, 2 * LANES, 2 * LANES), BF16),
        in_specs=[VMEM] * 2,
        out_specs=VMEM,
        compiler_params=PARAMS,
        cost_estimate=cost(2**29, 2**20),
        name="all_picks",
    )(forward_source, backward_source)


def stack_of(channels):
    return pltpu.VMEM((4 * channels, (BH + 2) * LANES), BF16)


def paired_shape(frames):
    channels, pixels = frames.shape[-2:]
    return (2 * channels, pixels // 2)


def frame_parts(frames, entry_frame, matrix):
    moments = frames.shape[0]
    paired = paired_shape(frames)
    return pl.pallas_call(
        frame_kernel,
        out_shape=(
            jax.ShapeDtypeStruct((moments,) + paired, BF16),
            jax.ShapeDtypeStruct((moments, 2) + paired, F32),
        ),
        in_specs=[VMEM] * 3,
        out_specs=(VMEM, VMEM),
        scratch_shapes=[stack_of(frames.shape[-2])],
        compiler_params=PARAMS,
        cost_estimate=cost(2**31, 2**20),
        name="frame_parts",
    )(frames, entry_frame, matrix)


def near_frames(pair_frame, other_frame, entry_frame, matrix):
    channels, width = pair_frame.shape
    stack = stack_of(channels)
    return pl.pallas_call(
        near_frame_kernel,
        out_shape=(
            jax.ShapeDtypeStruct((2, 2 * channels, (width - LANES) // 2), F32),
            jax.ShapeDtypeStruct((2, 2, 2 * LANES, 2 * LANES), BF16),
        ),
        in_specs=[VMEM] * 4,
        out_specs=(VMEM, VMEM),
        scratch_shapes=[pltpu.VMEM((2,) + stack.shape, BF16)],
        compiler_params=PARAMS,
        cost_estimate=cost(2**30, 2**19),
        name="near_frames",
    )(pair_frame, other_frame, entry_frame, matrix)


def near(pair_own, *rest):
    shape = pair_own.shape
    out = jax.ShapeDtypeStruct(shape, BF16)
    stack = stack_of(shape[0] // 2)
    return pl.pallas_call(
        near_kernel,
        out_shape=(out, out),
        in_specs=[VMEM] * (1 + len(rest)),
        out_specs=(VMEM, VMEM),
        scratch_shapes=[stack] * 4,
        compiler_params=PARAMS,
        cost_estimate=cost(2**31, 2**19),
        name="near",
    )(pair_own, *rest)


def tick(moment, frames, *operands, earlier=None):
    channels, pixels = frames.shape[-2:]
    restored = jax.ShapeDtypeStruct((frames.shape[0], channels, pixels), BF16)
    state = jax.ShapeDtypeStruct((channels, pixels), BF16)
    in_specs = [VMEM] * len(operands)
    aliases = {}
    if earlier is not None:
        aliases = {len(operands): 0}
        operands += (earlier,)
        in_specs.append(ANY)
    finals = (state, state) if moment > 0 else ()
    stack = stack_of(channels)
    return pl.pallas_call(
        functools.partial(tick_kernel, moment),
        out_shape=(restored,) + finals,
        in_specs=in_specs,
        out_specs=(ANY,) * (1 + len(finals)),
        scratch_shapes=[
            *[stack] * 4,
            pltpu.VMEM((2, channels, pixels), BF16),
            pltpu.VMEM((channels, pixels), BF16),
            pltpu.SemaphoreType.DMA((2,)),
            pltpu.SemaphoreType.DMA,
        ],
        input_output_aliases=aliases,
        compiler_params=PARAMS,
        cost_estimate=cost(2**32, 2**19),
        name=f"tick_{moment}",
    )(*operands)


def sent(value, steps_even, steps_odd):
    count = lax.axis_size("tm")
    pairs = [(s, s + (steps_odd if s % 2 else steps_even)) for s in range(count)]
    return lax.ppermute(value, "tm", [(s, d) for s, d in pairs if 0 <= d < count])


def swapped(value):
    return lax.ppermute(value, "tile", [(0, 1), (1, 0)])


def later(value, *others):
    return lax.optimization_barrier((value, *others))[0]


def shards(
    frames,
    forward_carry,
    backward_carry,
    forward_source,
    backward_source,
    forward_entry,
    forward_blocks,
    backward_entry,
    backward_blocks,
    mixing_weight,
):
    payload = head(frames, forward_source, backward_source)
    pair_frame = sent(payload, 1, -1)
    near_state, far_state = pack(later(forward_carry, payload), backward_carry)
    pair_far = sent(far_state, -2, 2)
    other_far = sent(near_state, 2, -2)
    entry_frame, entry_warped, layers, mix_pair, matrix, back = pair_weights(
        later(forward_entry, near_state), forward_blocks, backward_entry, backward_blocks, mixing_weight
    )
    picks = all_picks(forward_source, backward_source)
    paired, parts = frame_parts(frames, later(entry_frame, pair_frame), matrix)
    other_frame = sent(pair_frame, 2, -2)
    pair_near = sent(later(near_state, pair_frame), 1, -1)
    other_near = sent(later(far_state, pair_frame), -1, 1)
    near_parts, near_picks = near_frames(pair_frame, other_frame, later(entry_frame, parts, picks), matrix)
    forward_one, backward_one = near(
        pair_far,
        swapped(later(pair_far, parts)),
        other_far,
        swapped(later(other_far, parts)),
        later(near_parts, pair_near, other_near),
        near_picks,
        entry_warped,
        layers,
    )
    tables = (picks, paired, parts, entry_warped, layers, mix_pair, back)
    (restored,) = tick(
        0, frames, pair_near, swapped(pair_near), other_near, swapped(other_near), *tables
    )
    restored, forward_final, backward_final = tick(
        1,
        frames,
        forward_one,
        swapped(forward_one),
        backward_one,
        swapped(backward_one),
        *tables,
        earlier=restored,
    )
    return (restored[:, None, None], forward_final[None, None], backward_final[None, None])


def solution(mesh):
    placed = (
        P(None, ("groups", "tm"), "tile", None, None),
        P(("groups", "tm"), "tile", None, None),
        P(("groups", "tm"), "tile", None, None),
        P(None, ("groups", "tm"), "tile"),
        P(None, ("groups", "tm"), "tile"),
        P(),
        P(),
        P(),
        P(),
        P(),
    )
    return jax.shard_map(
        shards,
        mesh=mesh,
        in_specs=placed,
        out_specs=(
            P(None, ("groups", "tm"), "tile", None, None),
            P(("groups", "tm"), "tile", None, None),
            P(("groups", "tm"), "tile", None, None),
        ),
        check_vma=False,
    )
```

time: 38.2 us -> 36 us (0.942)
  the two profiles are of different devices: /device:TPU:17 before, /device:TPU:13 now
where the time goes in v1:
time: 36 us; the launch traced here: 35.8 us
  starting transfers between devices  18.8 us (52%)
  Pallas kernels  15.1 us (42%)
  waiting for transfers between devices  0.91 us (3%)
  between operations  0.91 us (3%)
    ppermute x6, starting transfers between devices, sent(): lax.ppermute(value, 'tm', [(s, d) for s, d in pairs if 0 <= d < count])  12 us
    pallas_call x2, Pallas kernels, tick(): pl.pallas_call(functools.partial(tick_kernel, moment), out_shape=(restore...  6.87 us
    ppermute x6, starting transfers between devices, swapped(): return lax.ppermute(value, 'tile', [(0, 1), (1, 0)])  6.79 us
    pallas_call x1, Pallas kernels, near(): pl.pallas_call(near_kernel, out_shape=(out, out), in_specs=[VMEM] * (1 +...  2.02 us
    pallas_call x1, Pallas kernels, head(): pl.pallas_call(head_kernel, out_shape=jax.ShapeDtypeStruct((channels, pix...  1.8 us
    pallas_call x1, Pallas kernels, frame_parts(): pl.pallas_call(frame_kernel, out_shape=(jax.ShapeDtypeStruct((moments,) +...  1.72 us
    pallas_call x1, Pallas kernels, near_frames(): pl.pallas_call(near_frame_kernel, out_shape=(jax.ShapeDtypeStruct((2, 2 *...  1 us
    ppermute x6, waiting for transfers between devices, sent(): lax.ppermute(value, 'tm', [(s, d) for s, d in pairs if 0 <= d < count])  0.89 us
  transfers between devices with their start and end apart: 12, of which 1 were waited for; matrix products, arithmetic and copies ran while one was open for 0% of the time, Pallas kernels for 27%

profile of v1, /device:TPU:13, one launch (start us, length us, event | category | flops | bytes accessed | tf_op | source)
XLA Modules:
  0.0 35.8 jit_solution(9673357690650600744)
XLA Ops:
  0.6 0.0 copy-start.3
  0.6 0.0 copy-start.4
  0.7 0.0 copy-start.5
  0.7 0.0 copy-start.7
  0.7 0.0 copy-start.2
  0.7 0.0 copy-start.6
  0.7 0.0 copy-start.1
  0.7 1.8 %head.1 = bf16[64,2176]{1,0:T(8,128)(2,1)} custom-call(bf16[2,1,1,64,2048]{4,3,2,1,0:T(8,128)(2,1)} %frames.3, s32[2,1,16]{2,1,0:T(1,128)} %forward_index.3, s32[2,1,16]{2,1,0:T(1,128)} %backward_index.3), custom_call_target="tpu_custom_call" | custom-call | flops 1073741824 | bytes 524288 | tf_op jit(solution)/shard_map/head/pallas_call | solution.py:399
  2.5 0.0 copy-start
  2.5 0.3 collective-permute-start.1
  2.8 0.0 copy-done.3
  2.8 0.0 copy-done.4
  2.8 0.5 %pack.1 = (bf16[128,1024]{1,0:T(8,128)(2,1)S(1)}, bf16[128,1024]{1,0:T(8,128)(2,1)S(1)}) custom-call(bf16[1,1,64,2048]{3,2,1,0:T(8,128)(2,1)S(1)} %copy-done.3, bf16[1,1,64,2048]{3,2,1,0:T(8,128)(2,1)S(1)} %copy-done.4), custom_call_target="tpu_custom_call" | custom-call | flops 536870912 | bytes 524288 | tf_op jit(solution)/shard_map/pack/pallas_call | solution.py:418
  3.3 1.9 %collective-permute-start.3 = (bf16[128,1024]{1,0:T(8,128)(2,1)S(1)}, bf16[128,1024]{1,0:T(8,128)(2,1)S(1)}, u32[]{:S(2)}, u32[]{:S(2)}) collective-permute-start(bf16[128,1024]{1,0:T(8,128)(2,1)S(1)} %get-tuple-element.41), channel_id=1, source_target_pairs={{0,4},{4,8},{6,2},{8,12},{10,6},{14,10},{1,5},{5,9},{7,3},{9,13},{... | collective-permute-start | bytes 786440 | tf_op jit(solution)/shard_map/ppermute | solution.py:559
  5.3 3.4 %collective-permute-start = (bf16[128,1024]{1,0:T(8,128)(2,1)S(1)}, bf16[128,1024]{1,0:T(8,128)(2,1)S(1)}, u32[]{:S(2)}, u32[]{:S(2)}) collective-permute-start(bf16[128,1024]{1,0:T(8,128)(2,1)S(1)} %get-tuple-element.42), channel_id=1, source_target_pairs={{2,6},{4,0},{6,10},{8,4},{10,14},{12,8},{3,7},{5,1},{7,11},{9,5},{... | collective-permute-start | bytes 786440 | tf_op jit(solution)/shard_map/ppermute | solution.py:559
  8.6 0.0 copy-done.5
  8.7 0.0 copy-done.7
  8.7 0.0 copy-done.2
  8.7 0.0 copy-done.6
  8.7 0.0 copy-done.1
  8.7 0.7 %pair_weights.1 = (bf16[3,256,256]{2,1,0:T(8,128)(2,1)S(1)}, bf16[2,3,128,256]{3,2,1,0:T(8,128)(2,1)S(1)}, bf16[2,1,2,3,128,256]{5,4,3,2,1,0:T(8,128)(2,1)S(1)},...) custom-call(bf16[9,64,128]{2,1,0:T(8,128)(2,1)S(1)} %copy-done.5, ...), custom_call_target="tpu_custom_call" | custom-call | flops 536870912 | bytes 1048576 | tf_op jit(solution)/shard_map/pair_weights/pallas_call | solution.py:441
  9.4 0.9 %collective-permute-done.1.pair_frame = bf16[64,2176]{1,0:T(8,128)(2,1)S(1)} collective-permute-done((bf16[64,2176]{1,0:T(8,128)(2,1)}, bf16[64,2176]{1,0:T(8,128)(2,1)S(1)}, u32[]{:S(2)}, u32[]{:S(2)}) %collective-permute-start.1) | collective-permute-done | bytes 278560 | tf_op jit(solution)/shard_map/ppermute | solution.py:559
  10.3 0.4 %collective-permute-start.6 = (bf16[128,1024]{1,0:T(8,128)(2,1)S(1)}, bf16[128,1024]{1,0:T(8,128)(2,1)S(1)}, u32[]{:S(2)}, u32[]{:S(2)}) collective-permute-start(bf16[128,1024]{1,0:T(8,128)(2,1)S(1)} %get-tuple-element.41), channel_id=1, source_target_pairs={{0,2},{2,0},{4,6},{6,4},{8,10},{10,8},{12,14},{14,12},{1,3},{3,1},... | collective-permute-start | bytes 786440 | tf_op jit(solution)/shard_map/ppermute | solution.py:559
  10.8 3.9 %collective-permute-start.7 = (bf16[128,1024]{1,0:T(8,128)(2,1)S(1)}, bf16[128,1024]{1,0:T(8,128)(2,1)S(1)}, u32[]{:S(2)}, u32[]{:S(2)}) collective-permute-start(bf16[128,1024]{1,0:T(8,128)(2,1)S(1)} %get-tuple-element.42), channel_id=1, source_target_pairs={{2,4},{4,2},{6,8},{8,6},{10,12},{12,10},{3,5},{5,3},{7,9},{9,7},{1... | collective-permute-start | bytes 786440 | tf_op jit(solution)/shard_map/ppermute | solution.py:559
  14.7 2.1 %collective-permute-start.5 = (bf16[64,2176]{1,0:T(8,128)(2,1)S(1)}, bf16[64,2176]{1,0:T(8,128)(2,1)S(1)}, u32[]{:S(2)}, u32[]{:S(2)}) collective-permute-start(bf16[64,2176]{1,0:T(8,128)(2,1)S(1)} %collective-permute-done.1.pair_frame), channel_id=1, source_target_pairs={{0,4},{4,8},{6,2},{8,12},{10,6},{14,10},{1,5},{5,9},{7,3},{9,13},{... | collective-permute-start | bytes 835592 | tf_op jit(solution)/shard_map/ppermute | solution.py:559
  16.8 0.0 copy-done
  16.8 0.0 copy-start.8
  16.8 0.0 copy-start.9
  16.8 1.7 %frame_parts.1 = (bf16[2,128,1024]{2,1,0:T(8,128)(2,1)S(1)}, f32[2,2,128,1024]{3,2,1,0:T(8,128)S(1)}) custom-call(bf16[2,1,1,64,2048]{4,3,2,1,0:T(8,128)(2,1)S(1)} %copy-done, bf16[3,256,256]{2,1,0:T(8,128)(2,1)S(1)} %get-tuple-element.39.entry_frame, bf16[512,512]{1,0:T(8,128)(2,1)S(1)} %get-tuple-element.35.matrix), custom_call_target="tpu_custom_call" | custom-call | flops 2147483648 | bytes 1048576 | tf_op jit(solution)/shard_map/frame_parts/pallas_call | solution.py:476
  18.6 0.0 collective-permute-done.3.other_own
  18.6 0.0 collective-permute-done.pair_own
  18.6 2.5 %collective-permute-start.2 = (bf16[128,1024]{1,0:T(8,128)(2,1)S(1)}, bf16[128,1024]{1,0:T(8,128)(2,1)S(1)}, u32[]{:S(2)}, u32[]{:S(2)}) collective-permute-start(bf16[128,1024]{1,0:T(8,128)(2,1)S(1)} %collective-permute-done.pair_own), channel_id=1, source_target_pairs={{0,1},{1,0},{2,3},{3,2},{4,5},{5,4},{6,7},{7,6},{8,9},{9,8},{10,11... | collective-permute-start | bytes 786440 | tf_op jit(solution)/shard_map/ppermute | solution.py:563
  21.0 0.1 collective-permute-start.4
  21.1 0.0 copy-done.8
  21.1 0.0 copy-done.9
  21.1 0.4 %all_picks.1.picks = bf16[2,2,2,256,256]{4,3,2,1,0:T(8,128)(2,1)S(1)} custom-call(s32[2,1,16]{2,1,0:T(1,128)S(1)} %copy-done.8, s32[2,1,16]{2,1,0:T(1,128)S(1)} %copy-done.9), custom_call_target="tpu_custom_call" | custom-call | flops 536870912 | bytes 1048576 | tf_op jit(solution)/shard_map/all_picks/pallas_call | solution.py:453
  21.5 0.0 collective-permute-done.6.first_own
  21.6 3.1 %collective-permute-start.10 = (bf16[128,1024]{1,0:T(8,128)(2,1)S(1)}, bf16[128,1024]{1,0:T(8,128)(2,1)S(1)}, u32[]{:S(2)}, u32[]{:S(2)}) collective-permute-start(bf16[128,1024]{1,0:T(8,128)(2,1)S(1)} %collective-permute-done.6.first_own), channel_id=1, source_target_pairs={{0,1},{1,0},{2,3},{3,2},{4,5},{5,4},{6,7},{7,6},{8,9},{9,8},{10,11... | collective-permute-start | bytes 786440 | tf_op jit(solution)/shard_map/ppermute | solution.py:563
  24.7 0.0 collective-permute-done.7.second_own
  24.7 0.0 collective-permute-start.11
  24.7 0.0 collective-permute-done.5.other_frame
  24.7 1.0 %near_frames.1 = (f32[2,128,1024]{2,1,0:T(8,128)S(1)}, bf16[2,2,256,256]{3,2,1,0:T(8,128)(2,1)S(1)}) custom-call(bf16[64,2176]{1,0:T(8,128)(2,1)S(1)} %collective-permute-done.1.pair_frame, bf16[64,2176]{1,0:T(8,128)(2,1)S(1)} %collective-permute-done.5.other_frame, bf16[3,256,256]{2,1,0:T(8,128)(2,1)S(1)} %get-tuple-element.39.entry_frame, ...), custom_call_target="tpu_custom_call" | custom-call | flops 1073741824 | bytes 524288 | tf_op jit(solution)/shard_map/near_frames/pallas_call | solution.py:494
  25.7 0.0 collective-permute-done.2.pair_swapped
  25.7 0.0 collective-permute-done.4.other_swapped
  25.7 2.0 %near.1 = (bf16[128,1024]{1,0:T(8,128)(2,1)S(1)}, bf16[128,1024]{1,0:T(8,128)(2,1)S(1)}) custom-call(bf16[128,1024]{1,0:T(8,128)(2,1)S(1)} %collective-permute-done.pair_own, bf16[128,1024]{1,0:T(8,128)(2,1)S(1)} %collective-permute-done.2.pair_swapped, bf16[128,1024]{1,0:T(8,128)(2,1)S(1)} %collective-permute-done.3.other_own, ...), custom_call_target="tpu_custom_call" | custom-call | flops 2147483648 | bytes 524288 | tf_op jit(solution)/shard_map/near/pallas_call | solution.py:513
  27.7 1.1 %collective-permute-start.8 = (bf16[128,1024]{1,0:T(8,128)(2,1)S(1)}, bf16[128,1024]{1,0:T(8,128)(2,1)S(1)}, u32[]{:S(2)}, u32[]{:S(2)}) collective-permute-start(bf16[128,1024]{1,0:T(8,128)(2,1)S(1)} %get-tuple-element.47.first_own), channel_id=1, source_target_pairs={{0,1},{1,0},{2,3},{3,2},{4,5},{5,4},{6,7},{7,6},{8,9},{9,8},{10,11... | collective-permute-start | bytes 786440 | tf_op jit(solution)/shard_map/ppermute | solution.py:563
  28.8 0.1 collective-permute-start.9
  28.9 0.0 collective-permute-done.10.first_swapped
  28.9 0.0 collective-permute-done.11.second_swapped
  28.9 3.3 %tick_0.1.rest_0_ = bf16[2,64,2048]{2,1,0:T(8,128)(2,1)} custom-call(bf16[128,1024]{1,0:T(8,128)(2,1)S(1)} %collective-permute-done.6.first_own, bf16[128,1024]{1,0:T(8,128)(2,1)S(1)} %collective-permute-done.10.first_swapped, bf16[128,1024]{1,0:T(8,128)(2,1)S(1)} %collective-permute-done.7.second_own, ...), custom_call_target="tpu_custom_call" | custom-call | flops 4294967296 | bytes 524288 | tf_op jit(solution)/shard_map/tick_0/pallas_call | solution.py:537
  32.2 0.0 collective-permute-done.8.first_swapped
  32.2 0.0 collective-permute-done.9.second_swapped
  32.2 3.6 %tick_1.1 = (bf16[2,64,2048]{2,1,0:T(8,128)(2,1)}, bf16[64,2048]{1,0:T(8,128)(2,1)}, bf16[64,2048]{1,0:T(8,128)(2,1)}) custom-call(bf16[128,1024]{1,0:T(8,128)(2,1)S(1)} %get-tuple-element.47.first_own, bf16[128,1024]{1,0:T(8,128)(2,1)S(1)} %collective-permute-done.8.first_swapped, ...), custom_call_target="tpu_custom_call", output_to_operand_aliasing={{0}: (11, {})} | custom-call | flops 4294967296 | bytes 524288 | tf_op jit(solution)/shard_map/tick_1/pallas_call | solution.py:537
Async XLA Ops:
  0.6 2.2 %copy-start.3 = (bf16[1,1,64,2048]{3,2,1,0:T(8,128)(2,1)S(1)}, bf16[1,1,64,2048]{3,2,1,0:T(8,128)(2,1)}, u32[]{:S(2)}) copy-start(bf16[1,1,64,2048]{3,2,1,0:T(8,128)(2,1)} %forward) | copy-start | bytes 786436
  0.6 2.2 %copy-start.4 = (bf16[1,1,64,2048]{3,2,1,0:T(8,128)(2,1)S(1)}, bf16[1,1,64,2048]{3,2,1,0:T(8,128)(2,1)}, u32[]{:S(2)}) copy-start(bf16[1,1,64,2048]{3,2,1,0:T(8,128)(2,1)} %backward.1) | copy-start | bytes 786436
  0.7 8.0 %copy-start.5 = (bf16[9,64,128]{2,1,0:T(8,128)(2,1)S(1)}, bf16[9,64,128]{2,1,0:T(8,128)(2,1)}, u32[]{:S(2)}) copy-start(bf16[9,64,128]{2,1,0:T(8,128)(2,1)} %fe) | copy-start | bytes 442372
  0.7 8.0 %copy-start.7 = (bf16[64,128]{1,0:T(8,128)(2,1)S(1)}, bf16[64,128]{1,0:T(8,128)(2,1)}, u32[]{:S(2)}) copy-start(bf16[64,128]{1,0:T(8,128)(2,1)} %mixing.1) | copy-start | bytes 49156
  0.7 8.0 %copy-start.2 = (bf16[1,2,9,64,64]{4,3,2,1,0:T(8,128)(2,1)S(1)}, bf16[1,2,9,64,64]{4,3,2,1,0:T(8,128)(2,1)}, u32[]{:S(2)}) copy-start(bf16[1,2,9,64,64]{4,3,2,1,0:T(8,128)(2,1)} %bb.1) | copy-start | bytes 442372
  0.7 8.0 %copy-start.6 = (bf16[9,64,128]{2,1,0:T(8,128)(2,1)S(1)}, bf16[9,64,128]{2,1,0:T(8,128)(2,1)}, u32[]{:S(2)}) copy-start(bf16[9,64,128]{2,1,0:T(8,128)(2,1)} %be.1) | copy-start | bytes 442372
  0.7 8.0 %copy-start.1 = (bf16[1,2,9,64,64]{4,3,2,1,0:T(8,128)(2,1)S(1)}, bf16[1,2,9,64,64]{4,3,2,1,0:T(8,128)(2,1)}, u32[]{:S(2)}) copy-start(bf16[1,2,9,64,64]{4,3,2,1,0:T(8,128)(2,1)} %fb.1) | copy-start | bytes 442372
  2.5 14.3 %copy-start = (bf16[2,1,1,64,2048]{4,3,2,1,0:T(8,128)(2,1)S(1)}, bf16[2,1,1,64,2048]{4,3,2,1,0:T(8,128)(2,1)}, u32[]{:S(2)}) copy-start(bf16[2,1,1,64,2048]{4,3,2,1,0:T(8,128)(2,1)} %frames.3) | copy-start | bytes 1572868
  2.5 7.8 %collective-permute-start.1 = (bf16[64,2176]{1,0:T(8,128)(2,1)}, bf16[64,2176]{1,0:T(8,128)(2,1)S(1)}, u32[]{:S(2)}, u32[]{:S(2)}) collective-permute-start(bf16[64,2176]{1,0:T(8,128)(2,1)} %head.1), channel_id=1, source_target_pairs={{0,2},{2,0},{4,6},{6,4},{8,10},{10,8},{12,14},{14,12},{1,3},{3,1},... | collective-permute-start | bytes 835592 | tf_op jit(solution)/shard_map/ppermute | solution.py:559
  3.3 15.2 %collective-permute-start.3 = (bf16[128,1024]{1,0:T(8,128)(2,1)S(1)}, bf16[128,1024]{1,0:T(8,128)(2,1)S(1)}, u32[]{:S(2)}, u32[]{:S(2)}) collective-permute-start(bf16[128,1024]{1,0:T(8,128)(2,1)S(1)} %get-tuple-element.41), channel_id=1, source_target_pairs={{0,4},{4,8},{6,2},{8,12},{10,6},{14,10},{1,5},{5,9},{7,3},{9,13},{... | collective-permute-start | bytes 786440 | tf_op jit(solution)/shard_map/ppermute | solution.py:559
  5.3 13.3 %collective-permute-start = (bf16[128,1024]{1,0:T(8,128)(2,1)S(1)}, bf16[128,1024]{1,0:T(8,128)(2,1)S(1)}, u32[]{:S(2)}, u32[]{:S(2)}) collective-permute-start(bf16[128,1024]{1,0:T(8,128)(2,1)S(1)} %get-tuple-element.42), channel_id=1, source_target_pairs={{2,6},{4,0},{6,10},{8,4},{10,14},{12,8},{3,7},{5,1},{7,11},{9,5},{... | collective-permute-start | bytes 786440 | tf_op jit(solution)/shard_map/ppermute | solution.py:559
  10.3 11.2 %collective-permute-start.6 = (bf16[128,1024]{1,0:T(8,128)(2,1)S(1)}, bf16[128,1024]{1,0:T(8,128)(2,1)S(1)}, u32[]{:S(2)}, u32[]{:S(2)}) collective-permute-start(bf16[128,1024]{1,0:T(8,128)(2,1)S(1)} %get-tuple-element.41), channel_id=1, source_target_pairs={{0,2},{2,0},{4,6},{6,4},{8,10},{10,8},{12,14},{14,12},{1,3},{3,1},... | collective-permute-start | bytes 786440 | tf_op jit(solution)/shard_map/ppermute | solution.py:559
  10.8 13.9 %collective-permute-start.7 = (bf16[128,1024]{1,0:T(8,128)(2,1)S(1)}, bf16[128,1024]{1,0:T(8,128)(2,1)S(1)}, u32[]{:S(2)}, u32[]{:S(2)}) collective-permute-start(bf16[128,1024]{1,0:T(8,128)(2,1)S(1)} %get-tuple-element.42), channel_id=1, source_target_pairs={{2,4},{4,2},{6,8},{8,6},{10,12},{12,10},{3,5},{5,3},{7,9},{9,7},{1... | collective-permute-start | bytes 786440 | tf_op jit(solution)/shard_map/ppermute | solution.py:559
  14.7 10.0 %collective-permute-start.5 = (bf16[64,2176]{1,0:T(8,128)(2,1)S(1)}, bf16[64,2176]{1,0:T(8,128)(2,1)S(1)}, u32[]{:S(2)}, u32[]{:S(2)}) collective-permute-start(bf16[64,2176]{1,0:T(8,128)(2,1)S(1)} %collective-permute-done.1.pair_frame), channel_id=1, source_target_pairs={{0,4},{4,8},{6,2},{8,12},{10,6},{14,10},{1,5},{5,9},{7,3},{9,13},{... | collective-permute-start | bytes 835592 | tf_op jit(solution)/shard_map/ppermute | solution.py:559
  16.8 4.3 %copy-start.8 = (s32[2,1,16]{2,1,0:T(1,128)S(1)}, s32[2,1,16]{2,1,0:T(1,128)}, u32[]{:S(2)}) copy-start(s32[2,1,16]{2,1,0:T(1,128)} %forward_index.3) | copy-start | bytes 388
  16.8 4.3 %copy-start.9 = (s32[2,1,16]{2,1,0:T(1,128)S(1)}, s32[2,1,16]{2,1,0:T(1,128)}, u32[]{:S(2)}) copy-start(s32[2,1,16]{2,1,0:T(1,128)} %backward_index.3) | copy-start | bytes 388
  18.6 7.1 %collective-permute-start.2 = (bf16[128,1024]{1,0:T(8,128)(2,1)S(1)}, bf16[128,1024]{1,0:T(8,128)(2,1)S(1)}, u32[]{:S(2)}, u32[]{:S(2)}) collective-permute-start(bf16[128,1024]{1,0:T(8,128)(2,1)S(1)} %collective-permute-done.pair_own), channel_id=1, source_target_pairs={{0,1},{1,0},{2,3},{3,2},{4,5},{5,4},{6,7},{7,6},{8,9},{9,8},{10,11... | collective-permute-start | bytes 786440 | tf_op jit(solution)/shard_map/ppermute | solution.py:563
  21.0 4.7 %collective-permute-start.4 = (bf16[128,1024]{1,0:T(8,128)(2,1)S(1)}, bf16[128,1024]{1,0:T(8,128)(2,1)S(1)}, u32[]{:S(2)}, u32[]{:S(2)}) collective-permute-start(bf16[128,1024]{1,0:T(8,128)(2,1)S(1)} %collective-permute-done.3.other_own), channel_id=1, source_target_pairs={{0,1},{1,0},{2,3},{3,2},{4,5},{5,4},{6,7},{7,6},{8,9},{9,8},{10,11... | collective-permute-start | bytes 786440 | tf_op jit(solution)/shard_map/ppermute | solution.py:563
  21.6 7.3 %collective-permute-start.10 = (bf16[128,1024]{1,0:T(8,128)(2,1)S(1)}, bf16[128,1024]{1,0:T(8,128)(2,1)S(1)}, u32[]{:S(2)}, u32[]{:S(2)}) collective-permute-start(bf16[128,1024]{1,0:T(8,128)(2,1)S(1)} %collective-permute-done.6.first_own), channel_id=1, source_target_pairs={{0,1},{1,0},{2,3},{3,2},{4,5},{5,4},{6,7},{7,6},{8,9},{9,8},{10,11... | collective-permute-start | bytes 786440 | tf_op jit(solution)/shard_map/ppermute | solution.py:563
  24.7 4.2 %collective-permute-start.11 = (bf16[128,1024]{1,0:T(8,128)(2,1)S(1)}, bf16[128,1024]{1,0:T(8,128)(2,1)S(1)}, u32[]{:S(2)}, u32[]{:S(2)}) collective-permute-start(bf16[128,1024]{1,0:T(8,128)(2,1)S(1)} %collective-permute-done.7.second_own), channel_id=1, source_target_pairs={{0,1},{1,0},{2,3},{3,2},{4,5},{5,4},{6,7},{7,6},{8,9},{9,8},{10,11... | collective-permute-start | bytes 786440 | tf_op jit(solution)/shard_map/ppermute | solution.py:563
  27.7 4.4 %collective-permute-start.8 = (bf16[128,1024]{1,0:T(8,128)(2,1)S(1)}, bf16[128,1024]{1,0:T(8,128)(2,1)S(1)}, u32[]{:S(2)}, u32[]{:S(2)}) collective-permute-start(bf16[128,1024]{1,0:T(8,128)(2,1)S(1)} %get-tuple-element.47.first_own), channel_id=1, source_target_pairs={{0,1},{1,0},{2,3},{3,2},{4,5},{5,4},{6,7},{7,6},{8,9},{9,8},{10,11... | collective-permute-start | bytes 786440 | tf_op jit(solution)/shard_map/ppermute | solution.py:563
  28.8 3.4 %collective-permute-start.9 = (bf16[128,1024]{1,0:T(8,128)(2,1)S(1)}, bf16[128,1024]{1,0:T(8,128)(2,1)S(1)}, u32[]{:S(2)}, u32[]{:S(2)}) collective-permute-start(bf16[128,1024]{1,0:T(8,128)(2,1)S(1)} %get-tuple-element.48.second_own), channel_id=1, source_target_pairs={{0,1},{1,0},{2,3},{3,2},{4,5},{5,4},{6,7},{7,6},{8,9},{9,8},{10,11... | collective-permute-start | bytes 786440 | tf_op jit(solution)/shard_map/ppermute | solution.py:563

commit v2 on v1

--- a/solution.py
+++ b/solution.py
@@ -369,18 +369,18 @@
     for d in range(2):
         put_warped(firsts[d], (cut(owns[d], BH), cut(others[d], BH)), picks[moment, d])
     hidden = chains(firsts, seconds, entry_warped, [parts.at[moment, d] for d in range(2)], layers)
-    total = cut(paired[moment].astype(F32), BH)
-    for d in range(2):
-        total = mix(mix_pair[d], hidden[d], total)
-    natural = to_natural([rounded(total)] + (hidden if moment > 0 else []), back[...])
-    put_natural(mixed, natural[0])
-    copies = [pltpu.make_async_copy(mixed, restored.at[moment], mixed_sem)]
-    copies[0].start()
-    for d, groups in enumerate(natural[1:]):
+    copies = []
+    for d, groups in enumerate(to_natural(hidden, back[...]) if moment > 0 else []):
         put_natural(finals.at[d], groups)
         out = (forward_final, backward_final)[d]
         copies.append(pltpu.make_async_copy(finals.at[d], out, final_sems.at[d]))
         copies[-1].start()
+    total = cut(paired[moment].astype(F32), BH)
+    for d in range(2):
+        total = mix(mix_pair[d], hidden[d], total)
+    put_natural(mixed, to_natural([rounded(total)], back[...])[0])
+    copies.append(pltpu.make_async_copy(mixed, restored.at[moment], mixed_sem))
+    copies[-1].start()
     for copy in copies:
         copy.wait()
 
@@ -590,7 +590,7 @@
     picks = all_picks(forward_source, backward_source)
     paired, parts = frame_parts(frames, later(entry_frame, pair_frame), matrix)
     other_frame = sent(pair_frame, 2, -2)
-    pair_near = sent(later(near_state, pair_frame), 1, -1)
+    pair_near = sent(near_state, 1, -1)
     other_near = sent(later(far_state, pair_frame), -1, 1)
     near_parts, near_picks = near_frames(pair_frame, other_frame, later(entry_frame, parts, picks), matrix)
     forward_one, backward_one = near(

time: 36 us -> 35.1 us (0.975)
  waiting for transfers between devices: 0.91 us -> 0.03 us
    ppermute x6, waiting for transfers between devices: 0.89 us -> 0.02 us  [sent(): lax.ppermute(value, 'tm', [(s, d) for s, d in pairs if 0 <= d < count])]
  transfers between devices with their start and end apart: 12 -> 12, of which waited for: 1 -> 0; matrix products, arithmetic and copies ran while one was open for 0% -> 0% of each run, Pallas kernels for 27% -> 28%
where the time goes in v2:
time: 35.1 us; the launch traced here: 34.9 us
  starting transfers between devices  18.9 us (54%)
  Pallas kernels  15 us (43%)
  between operations  0.89 us (3%)
    ppermute x6, starting transfers between devices, sent(): lax.ppermute(value, 'tm', [(s, d) for s, d in pairs if 0 <= d < count])  12.1 us
    pallas_call x2, Pallas kernels, tick(): pl.pallas_call(functools.partial(tick_kernel, moment), out_shape=(restore...  6.82 us
    ppermute x6, starting transfers between devices, swapped(): return lax.ppermute(value, 'tile', [(0, 1), (1, 0)])  6.8 us
    pallas_call x1, Pallas kernels, near(): pl.pallas_call(near_kernel, out_shape=(out, out), in_specs=[VMEM] * (1 +...  2.02 us
    pallas_call x1, Pallas kernels, head(): pl.pallas_call(head_kernel, out_shape=jax.ShapeDtypeStruct((channels, pix...  1.8 us
    pallas_call x1, Pallas kernels, frame_parts(): pl.pallas_call(frame_kernel, out_shape=(jax.ShapeDtypeStruct((moments,) +...  1.73 us
    pallas_call x1, Pallas kernels, near_frames(): pl.pallas_call(near_frame_kernel, out_shape=(jax.ShapeDtypeStruct((2, 2 *...  1 us
    pallas_call x1, Pallas kernels, pair_weights(): pl.pallas_call(weights_kernel, out_shape=tuple((jax.ShapeDtypeStruct(shap...  0.74 us
  transfers between devices with their start and end apart: 12, of which 0 were waited for; matrix products, arithmetic and copies ran while one was open for 0% of the time, Pallas kernels for 28%

profile of v2, /device:TPU:13, one launch (start us, length us, event | category | flops | bytes accessed | tf_op | source)
XLA Modules:
  0.0 34.9 jit_solution(17347598067716770819)
XLA Ops:
  0.6 0.0 copy-start.3
  0.6 0.0 copy-start.4
  0.7 0.0 copy-start.5
  0.7 0.0 copy-start.7
  0.7 0.0 copy-start.2
  0.7 0.0 copy-start.6
  0.7 0.0 copy-start.1
  0.7 1.8 %head.1 = bf16[64,2176]{1,0:T(8,128)(2,1)} custom-call(bf16[2,1,1,64,2048]{4,3,2,1,0:T(8,128)(2,1)} %frames.3, s32[2,1,16]{2,1,0:T(1,128)} %forward_index.3, s32[2,1,16]{2,1,0:T(1,128)} %backward_index.3), custom_call_target="tpu_custom_call" | custom-call | flops 1073741824 | bytes 524288 | tf_op jit(solution)/shard_map/head/pallas_call | solution.py:399
  2.5 0.0 copy-start
  2.5 0.3 collective-permute-start.1
  2.8 0.0 copy-done.3
  2.8 0.0 copy-done.4
  2.8 0.5 %pack.1 = (bf16[128,1024]{1,0:T(8,128)(2,1)S(1)}, bf16[128,1024]{1,0:T(8,128)(2,1)S(1)}) custom-call(bf16[1,1,64,2048]{3,2,1,0:T(8,128)(2,1)S(1)} %copy-done.3, bf16[1,1,64,2048]{3,2,1,0:T(8,128)(2,1)S(1)} %copy-done.4), custom_call_target="tpu_custom_call" | custom-call | flops 536870912 | bytes 524288 | tf_op jit(solution)/shard_map/pack/pallas_call | solution.py:418
  3.3 1.9 %collective-permute-start.3 = (bf16[128,1024]{1,0:T(8,128)(2,1)S(1)}, bf16[128,1024]{1,0:T(8,128)(2,1)S(1)}, u32[]{:S(2)}, u32[]{:S(2)}) collective-permute-start(bf16[128,1024]{1,0:T(8,128)(2,1)S(1)} %get-tuple-element.30), channel_id=1, source_target_pairs={{0,4},{4,8},{6,2},{8,12},{10,6},{14,10},{1,5},{5,9},{7,3},{9,13},{... | collective-permute-start | bytes 786440 | tf_op jit(solution)/shard_map/ppermute | solution.py:559
  5.3 3.4 %collective-permute-start = (bf16[128,1024]{1,0:T(8,128)(2,1)S(1)}, bf16[128,1024]{1,0:T(8,128)(2,1)S(1)}, u32[]{:S(2)}, u32[]{:S(2)}) collective-permute-start(bf16[128,1024]{1,0:T(8,128)(2,1)S(1)} %get-tuple-element.40), channel_id=1, source_target_pairs={{2,6},{4,0},{6,10},{8,4},{10,14},{12,8},{3,7},{5,1},{7,11},{9,5},{... | collective-permute-start | bytes 786440 | tf_op jit(solution)/shard_map/ppermute | solution.py:559
  8.6 1.3 %collective-permute-start.6 = (bf16[128,1024]{1,0:T(8,128)(2,1)S(1)}, bf16[128,1024]{1,0:T(8,128)(2,1)S(1)}, u32[]{:S(2)}, u32[]{:S(2)}) collective-permute-start(bf16[128,1024]{1,0:T(8,128)(2,1)S(1)} %get-tuple-element.30), channel_id=1, source_target_pairs={{0,2},{2,0},{4,6},{6,4},{8,10},{10,8},{12,14},{14,12},{1,3},{3,1},... | collective-permute-start | bytes 786440 | tf_op jit(solution)/shard_map/ppermute | solution.py:559
  10.0 0.0 copy-done.5
  10.0 0.0 copy-done.7
  10.0 0.0 copy-done.2
  10.0 0.0 copy-done.6
  10.0 0.0 copy-done.1
  10.0 0.7 %pair_weights.1 = (bf16[3,256,256]{2,1,0:T(8,128)(2,1)S(1)}, bf16[2,3,128,256]{3,2,1,0:T(8,128)(2,1)S(1)}, bf16[2,1,2,3,128,256]{5,4,3,2,1,0:T(8,128)(2,1)S(1)},...) custom-call(bf16[9,64,128]{2,1,0:T(8,128)(2,1)S(1)} %copy-done.5, ...), custom_call_target="tpu_custom_call" | custom-call | flops 536870912 | bytes 1048576 | tf_op jit(solution)/shard_map/pair_weights/pallas_call | solution.py:441
  10.7 0.0 collective-permute-done.1.pair_frame
  10.7 3.1 %collective-permute-start.7 = (bf16[128,1024]{1,0:T(8,128)(2,1)S(1)}, bf16[128,1024]{1,0:T(8,128)(2,1)S(1)}, u32[]{:S(2)}, u32[]{:S(2)}) collective-permute-start(bf16[128,1024]{1,0:T(8,128)(2,1)S(1)} %get-tuple-element.40), channel_id=1, source_target_pairs={{2,4},{4,2},{6,8},{8,6},{10,12},{12,10},{3,5},{5,3},{7,9},{9,7},{1... | collective-permute-start | bytes 786440 | tf_op jit(solution)/shard_map/ppermute | solution.py:559
  13.9 2.1 %collective-permute-start.5 = (bf16[64,2176]{1,0:T(8,128)(2,1)S(1)}, bf16[64,2176]{1,0:T(8,128)(2,1)S(1)}, u32[]{:S(2)}, u32[]{:S(2)}) collective-permute-start(bf16[64,2176]{1,0:T(8,128)(2,1)S(1)} %collective-permute-done.1.pair_frame), channel_id=1, source_target_pairs={{0,4},{4,8},{6,2},{8,12},{10,6},{14,10},{1,5},{5,9},{7,3},{9,13},{... | collective-permute-start | bytes 835592 | tf_op jit(solution)/shard_map/ppermute | solution.py:559
  16.0 0.0 copy-done
  16.0 0.0 copy-start.8
  16.0 0.0 copy-start.9
  16.0 1.7 %frame_parts.1 = (bf16[2,128,1024]{2,1,0:T(8,128)(2,1)S(1)}, f32[2,2,128,1024]{3,2,1,0:T(8,128)S(1)}) custom-call(bf16[2,1,1,64,2048]{4,3,2,1,0:T(8,128)(2,1)S(1)} %copy-done, bf16[3,256,256]{2,1,0:T(8,128)(2,1)S(1)} %get-tuple-element.38.entry_frame, bf16[512,512]{1,0:T(8,128)(2,1)S(1)} %get-tuple-element.34.matrix), custom_call_target="tpu_custom_call" | custom-call | flops 2147483648 | bytes 1048576 | tf_op jit(solution)/shard_map/frame_parts/pallas_call | solution.py:476
  17.7 0.0 collective-permute-done.3.other_own
  17.8 0.0 collective-permute-done.pair_own
  17.8 2.4 %collective-permute-start.2 = (bf16[128,1024]{1,0:T(8,128)(2,1)S(1)}, bf16[128,1024]{1,0:T(8,128)(2,1)S(1)}, u32[]{:S(2)}, u32[]{:S(2)}) collective-permute-start(bf16[128,1024]{1,0:T(8,128)(2,1)S(1)} %collective-permute-done.pair_own), channel_id=1, source_target_pairs={{0,1},{1,0},{2,3},{3,2},{4,5},{5,4},{6,7},{7,6},{8,9},{9,8},{10,11... | collective-permute-start | bytes 786440 | tf_op jit(solution)/shard_map/ppermute | solution.py:563
  20.2 0.1 collective-permute-start.4
  20.3 0.0 copy-done.8
  20.3 0.0 copy-done.9
  20.3 0.4 %all_picks.1.picks = bf16[2,2,2,256,256]{4,3,2,1,0:T(8,128)(2,1)S(1)} custom-call(s32[2,1,16]{2,1,0:T(1,128)S(1)} %copy-done.8, s32[2,1,16]{2,1,0:T(1,128)S(1)} %copy-done.9), custom_call_target="tpu_custom_call" | custom-call | flops 536870912 | bytes 1048576 | tf_op jit(solution)/shard_map/all_picks/pallas_call | solution.py:453
  20.7 0.0 collective-permute-done.6.first_own
  20.7 1.4 %collective-permute-start.10 = (bf16[128,1024]{1,0:T(8,128)(2,1)S(1)}, bf16[128,1024]{1,0:T(8,128)(2,1)S(1)}, u32[]{:S(2)}, u32[]{:S(2)}) collective-permute-start(bf16[128,1024]{1,0:T(8,128)(2,1)S(1)} %collective-permute-done.6.first_own), channel_id=1, source_target_pairs={{0,1},{1,0},{2,3},{3,2},{4,5},{5,4},{6,7},{7,6},{8,9},{9,8},{10,11... | collective-permute-start | bytes 786440 | tf_op jit(solution)/shard_map/ppermute | solution.py:563
  22.1 0.0 collective-permute-done.7.second_own
  22.1 1.6 %collective-permute-start.11 = (bf16[128,1024]{1,0:T(8,128)(2,1)S(1)}, bf16[128,1024]{1,0:T(8,128)(2,1)S(1)}, u32[]{:S(2)}, u32[]{:S(2)}) collective-permute-start(bf16[128,1024]{1,0:T(8,128)(2,1)S(1)} %collective-permute-done.7.second_own), channel_id=1, source_target_pairs={{0,1},{1,0},{2,3},{3,2},{4,5},{5,4},{6,7},{7,6},{8,9},{9,8},{10,11... | collective-permute-start | bytes 786440 | tf_op jit(solution)/shard_map/ppermute | solution.py:563
  23.8 0.0 collective-permute-done.5.other_frame
  23.8 1.0 %near_frames.1 = (f32[2,128,1024]{2,1,0:T(8,128)S(1)}, bf16[2,2,256,256]{3,2,1,0:T(8,128)(2,1)S(1)}) custom-call(bf16[64,2176]{1,0:T(8,128)(2,1)S(1)} %collective-permute-done.1.pair_frame, bf16[64,2176]{1,0:T(8,128)(2,1)S(1)} %collective-permute-done.5.other_frame, bf16[3,256,256]{2,1,0:T(8,128)(2,1)S(1)} %get-tuple-element.38.entry_frame, ...), custom_call_target="tpu_custom_call" | custom-call | flops 1073741824 | bytes 524288 | tf_op jit(solution)/shard_map/near_frames/pallas_call | solution.py:494
  24.8 0.0 collective-permute-done.2.pair_swapped
  24.8 0.0 collective-permute-done.4.other_swapped
  24.8 2.0 %near.1 = (bf16[128,1024]{1,0:T(8,128)(2,1)S(1)}, bf16[128,1024]{1,0:T(8,128)(2,1)S(1)}) custom-call(bf16[128,1024]{1,0:T(8,128)(2,1)S(1)} %collective-permute-done.pair_own, bf16[128,1024]{1,0:T(8,128)(2,1)S(1)} %collective-permute-done.2.pair_swapped, bf16[128,1024]{1,0:T(8,128)(2,1)S(1)} %collective-permute-done.3.other_own, ...), custom_call_target="tpu_custom_call" | custom-call | flops 2147483648 | bytes 524288 | tf_op jit(solution)/shard_map/near/pallas_call | solution.py:513
  26.8 1.2 %collective-permute-start.8 = (bf16[128,1024]{1,0:T(8,128)(2,1)S(1)}, bf16[128,1024]{1,0:T(8,128)(2,1)S(1)}, u32[]{:S(2)}, u32[]{:S(2)}) collective-permute-start(bf16[128,1024]{1,0:T(8,128)(2,1)S(1)} %get-tuple-element.45.first_own), channel_id=1, source_target_pairs={{0,1},{1,0},{2,3},{3,2},{4,5},{5,4},{6,7},{7,6},{8,9},{9,8},{10,11... | collective-permute-start | bytes 786440 | tf_op jit(solution)/shard_map/ppermute | solution.py:563
  28.0 0.1 collective-permute-start.9
  28.1 0.0 collective-permute-done.10.first_swapped
  28.1 0.0 collective-permute-done.11.second_swapped
  28.1 3.3 %tick_0.1.rest_0_ = bf16[2,64,2048]{2,1,0:T(8,128)(2,1)} custom-call(bf16[128,1024]{1,0:T(8,128)(2,1)S(1)} %collective-permute-done.6.first_own, bf16[128,1024]{1,0:T(8,128)(2,1)S(1)} %collective-permute-done.10.first_swapped, bf16[128,1024]{1,0:T(8,128)(2,1)S(1)} %collective-permute-done.7.second_own, ...), custom_call_target="tpu_custom_call" | custom-call | flops 4294967296 | bytes 524288 | tf_op jit(solution)/shard_map/tick_0/pallas_call | solution.py:537
  31.4 0.0 collective-permute-done.8.first_swapped
  31.4 0.0 collective-permute-done.9.second_swapped
  31.4 3.5 %tick_1.1 = (bf16[2,64,2048]{2,1,0:T(8,128)(2,1)}, bf16[64,2048]{1,0:T(8,128)(2,1)}, bf16[64,2048]{1,0:T(8,128)(2,1)}) custom-call(bf16[128,1024]{1,0:T(8,128)(2,1)S(1)} %get-tuple-element.45.first_own, bf16[128,1024]{1,0:T(8,128)(2,1)S(1)} %collective-permute-done.8.first_swapped, ...), custom_call_target="tpu_custom_call", output_to_operand_aliasing={{0}: (11, {})} | custom-call | flops 4294967296 | bytes 524288 | tf_op jit(solution)/shard_map/tick_1/pallas_call | solution.py:537
Async XLA Ops:
  0.6 2.2 %copy-start.3 = (bf16[1,1,64,2048]{3,2,1,0:T(8,128)(2,1)S(1)}, bf16[1,1,64,2048]{3,2,1,0:T(8,128)(2,1)}, u32[]{:S(2)}) copy-start(bf16[1,1,64,2048]{3,2,1,0:T(8,128)(2,1)} %forward) | copy-start | bytes 786436
  0.6 2.2 %copy-start.4 = (bf16[1,1,64,2048]{3,2,1,0:T(8,128)(2,1)S(1)}, bf16[1,1,64,2048]{3,2,1,0:T(8,128)(2,1)}, u32[]{:S(2)}) copy-start(bf16[1,1,64,2048]{3,2,1,0:T(8,128)(2,1)} %backward.1) | copy-start | bytes 786436
  0.7 9.3 %copy-start.5 = (bf16[9,64,128]{2,1,0:T(8,128)(2,1)S(1)}, bf16[9,64,128]{2,1,0:T(8,128)(2,1)}, u32[]{:S(2)}) copy-start(bf16[9,64,128]{2,1,0:T(8,128)(2,1)} %fe) | copy-start | bytes 442372
  0.7 9.3 %copy-start.7 = (bf16[64,128]{1,0:T(8,128)(2,1)S(1)}, bf16[64,128]{1,0:T(8,128)(2,1)}, u32[]{:S(2)}) copy-start(bf16[64,128]{1,0:T(8,128)(2,1)} %mixing.1) | copy-start | bytes 49156
  0.7 9.3 %copy-start.2 = (bf16[1,2,9,64,64]{4,3,2,1,0:T(8,128)(2,1)S(1)}, bf16[1,2,9,64,64]{4,3,2,1,0:T(8,128)(2,1)}, u32[]{:S(2)}) copy-start(bf16[1,2,9,64,64]{4,3,2,1,0:T(8,128)(2,1)} %bb.1) | copy-start | bytes 442372
  0.7 9.3 %copy-start.6 = (bf16[9,64,128]{2,1,0:T(8,128)(2,1)S(1)}, bf16[9,64,128]{2,1,0:T(8,128)(2,1)}, u32[]{:S(2)}) copy-start(bf16[9,64,128]{2,1,0:T(8,128)(2,1)} %be.1) | copy-start | bytes 442372
  0.7 9.3 %copy-start.1 = (bf16[1,2,9,64,64]{4,3,2,1,0:T(8,128)(2,1)S(1)}, bf16[1,2,9,64,64]{4,3,2,1,0:T(8,128)(2,1)}, u32[]{:S(2)}) copy-start(bf16[1,2,9,64,64]{4,3,2,1,0:T(8,128)(2,1)} %fb.1) | copy-start | bytes 442372
  2.5 13.5 %copy-start = (bf16[2,1,1,64,2048]{4,3,2,1,0:T(8,128)(2,1)S(1)}, bf16[2,1,1,64,2048]{4,3,2,1,0:T(8,128)(2,1)}, u32[]{:S(2)}) copy-start(bf16[2,1,1,64,2048]{4,3,2,1,0:T(8,128)(2,1)} %frames.3) | copy-start | bytes 1572868
  2.5 8.2 %collective-permute-start.1 = (bf16[64,2176]{1,0:T(8,128)(2,1)}, bf16[64,2176]{1,0:T(8,128)(2,1)S(1)}, u32[]{:S(2)}, u32[]{:S(2)}) collective-permute-start(bf16[64,2176]{1,0:T(8,128)(2,1)} %head.1), channel_id=1, source_target_pairs={{0,2},{2,0},{4,6},{6,4},{8,10},{10,8},{12,14},{14,12},{1,3},{3,1},... | collective-permute-start | bytes 835592 | tf_op jit(solution)/shard_map/ppermute | solution.py:559
  3.3 14.4 %collective-permute-start.3 = (bf16[128,1024]{1,0:T(8,128)(2,1)S(1)}, bf16[128,1024]{1,0:T(8,128)(2,1)S(1)}, u32[]{:S(2)}, u32[]{:S(2)}) collective-permute-start(bf16[128,1024]{1,0:T(8,128)(2,1)S(1)} %get-tuple-element.30), channel_id=1, source_target_pairs={{0,4},{4,8},{6,2},{8,12},{10,6},{14,10},{1,5},{5,9},{7,3},{9,13},{... | collective-permute-start | bytes 786440 | tf_op jit(solution)/shard_map/ppermute | solution.py:559
  5.3 12.5 %collective-permute-start = (bf16[128,1024]{1,0:T(8,128)(2,1)S(1)}, bf16[128,1024]{1,0:T(8,128)(2,1)S(1)}, u32[]{:S(2)}, u32[]{:S(2)}) collective-permute-start(bf16[128,1024]{1,0:T(8,128)(2,1)S(1)} %get-tuple-element.40), channel_id=1, source_target_pairs={{2,6},{4,0},{6,10},{8,4},{10,14},{12,8},{3,7},{5,1},{7,11},{9,5},{... | collective-permute-start | bytes 786440 | tf_op jit(solution)/shard_map/ppermute | solution.py:559
  8.6 12.0 %collective-permute-start.6 = (bf16[128,1024]{1,0:T(8,128)(2,1)S(1)}, bf16[128,1024]{1,0:T(8,128)(2,1)S(1)}, u32[]{:S(2)}, u32[]{:S(2)}) collective-permute-start(bf16[128,1024]{1,0:T(8,128)(2,1)S(1)} %get-tuple-element.30), channel_id=1, source_target_pairs={{0,2},{2,0},{4,6},{6,4},{8,10},{10,8},{12,14},{14,12},{1,3},{3,1},... | collective-permute-start | bytes 786440 | tf_op jit(solution)/shard_map/ppermute | solution.py:559
  10.7 11.4 %collective-permute-start.7 = (bf16[128,1024]{1,0:T(8,128)(2,1)S(1)}, bf16[128,1024]{1,0:T(8,128)(2,1)S(1)}, u32[]{:S(2)}, u32[]{:S(2)}) collective-permute-start(bf16[128,1024]{1,0:T(8,128)(2,1)S(1)} %get-tuple-element.40), channel_id=1, source_target_pairs={{2,4},{4,2},{6,8},{8,6},{10,12},{12,10},{3,5},{5,3},{7,9},{9,7},{1... | collective-permute-start | bytes 786440 | tf_op jit(solution)/shard_map/ppermute | solution.py:559
  13.9 9.9 %collective-permute-start.5 = (bf16[64,2176]{1,0:T(8,128)(2,1)S(1)}, bf16[64,2176]{1,0:T(8,128)(2,1)S(1)}, u32[]{:S(2)}, u32[]{:S(2)}) collective-permute-start(bf16[64,2176]{1,0:T(8,128)(2,1)S(1)} %collective-permute-done.1.pair_frame), channel_id=1, source_target_pairs={{0,4},{4,8},{6,2},{8,12},{10,6},{14,10},{1,5},{5,9},{7,3},{9,13},{... | collective-permute-start | bytes 835592 | tf_op jit(solution)/shard_map/ppermute | solution.py:559
  16.0 4.3 %copy-start.8 = (s32[2,1,16]{2,1,0:T(1,128)S(1)}, s32[2,1,16]{2,1,0:T(1,128)}, u32[]{:S(2)}) copy-start(s32[2,1,16]{2,1,0:T(1,128)} %forward_index.3) | copy-start | bytes 388
  16.0 4.3 %copy-start.9 = (s32[2,1,16]{2,1,0:T(1,128)S(1)}, s32[2,1,16]{2,1,0:T(1,128)}, u32[]{:S(2)}) copy-start(s32[2,1,16]{2,1,0:T(1,128)} %backward_index.3) | copy-start | bytes 388
  17.8 7.0 %collective-permute-start.2 = (bf16[128,1024]{1,0:T(8,128)(2,1)S(1)}, bf16[128,1024]{1,0:T(8,128)(2,1)S(1)}, u32[]{:S(2)}, u32[]{:S(2)}) collective-permute-start(bf16[128,1024]{1,0:T(8,128)(2,1)S(1)} %collective-permute-done.pair_own), channel_id=1, source_target_pairs={{0,1},{1,0},{2,3},{3,2},{4,5},{5,4},{6,7},{7,6},{8,9},{9,8},{10,11... | collective-permute-start | bytes 786440 | tf_op jit(solution)/shard_map/ppermute | solution.py:563
  20.2 4.6 %collective-permute-start.4 = (bf16[128,1024]{1,0:T(8,128)(2,1)S(1)}, bf16[128,1024]{1,0:T(8,128)(2,1)S(1)}, u32[]{:S(2)}, u32[]{:S(2)}) collective-permute-start(bf16[128,1024]{1,0:T(8,128)(2,1)S(1)} %collective-permute-done.3.other_own), channel_id=1, source_target_pairs={{0,1},{1,0},{2,3},{3,2},{4,5},{5,4},{6,7},{7,6},{8,9},{9,8},{10,11... | collective-permute-start | bytes 786440 | tf_op jit(solution)/shard_map/ppermute | solution.py:563
  20.7 7.4 %collective-permute-start.10 = (bf16[128,1024]{1,0:T(8,128)(2,1)S(1)}, bf16[128,1024]{1,0:T(8,128)(2,1)S(1)}, u32[]{:S(2)}, u32[]{:S(2)}) collective-permute-start(bf16[128,1024]{1,0:T(8,128)(2,1)S(1)} %collective-permute-done.6.first_own), channel_id=1, source_target_pairs={{0,1},{1,0},{2,3},{3,2},{4,5},{5,4},{6,7},{7,6},{8,9},{9,8},{10,11... | collective-permute-start | bytes 786440 | tf_op jit(solution)/shard_map/ppermute | solution.py:563
  22.1 6.0 %collective-permute-start.11 = (bf16[128,1024]{1,0:T(8,128)(2,1)S(1)}, bf16[128,1024]{1,0:T(8,128)(2,1)S(1)}, u32[]{:S(2)}, u32[]{:S(2)}) collective-permute-start(bf16[128,1024]{1,0:T(8,128)(2,1)S(1)} %collective-permute-done.7.second_own), channel_id=1, source_target_pairs={{0,1},{1,0},{2,3},{3,2},{4,5},{5,4},{6,7},{7,6},{8,9},{9,8},{10,11... | collective-permute-start | bytes 786440 | tf_op jit(solution)/shard_map/ppermute | solution.py:563
  26.8 4.6 %collective-permute-start.8 = (bf16[128,1024]{1,0:T(8,128)(2,1)S(1)}, bf16[128,1024]{1,0:T(8,128)(2,1)S(1)}, u32[]{:S(2)}, u32[]{:S(2)}) collective-permute-start(bf16[128,1024]{1,0:T(8,128)(2,1)S(1)} %get-tuple-element.45.first_own), channel_id=1, source_target_pairs={{0,1},{1,0},{2,3},{3,2},{4,5},{5,4},{6,7},{7,6},{8,9},{9,8},{10,11... | collective-permute-start | bytes 786440 | tf_op jit(solution)/shard_map/ppermute | solution.py:563
  28.0 3.4 %collective-permute-start.9 = (bf16[128,1024]{1,0:T(8,128)(2,1)S(1)}, bf16[128,1024]{1,0:T(8,128)(2,1)S(1)}, u32[]{:S(2)}, u32[]{:S(2)}) collective-permute-start(bf16[128,1024]{1,0:T(8,128)(2,1)S(1)} %get-tuple-element.46.second_own), channel_id=1, source_target_pairs={{0,1},{1,0},{2,3},{3,2},{4,5},{5,4},{6,7},{7,6},{8,9},{9,8},{10,11... | collective-permute-start | bytes 786440 | tf_op jit(solution)/shard_map/ppermute | solution.py:563

commit v3 on v2

--- a/solution.py
+++ b/solution.py
@@ -398,7 +398,7 @@
     channels, pixels = frames.shape[-2:]
     return pl.pallas_call(
         head_kernel,
-        out_shape=jax.ShapeDtypeStruct((channels, pixels + LANES), BF16),
+        out_shape=pltpu.VMEM((channels, pixels + LANES), BF16),
         in_specs=[ANY] * 3,
         out_specs=VMEM,
         scratch_shapes=[

time: 35.1 us -> 34.4 us (0.980)
  Pallas kernels: 15 us -> 14.3 us
    pallas_call x1, Pallas kernels: 1.8 us -> 1.09 us  [head(): pl.pallas_call(head_kernel, out_shape=pltpu.VMEM((channels, pixels + LANE...]
where the time goes in v3:
time: 34.4 us; the launch traced here: 34.2 us
  starting transfers between devices  18.9 us (55%)
  Pallas kernels  14.3 us (42%)
  between operations  0.89 us (3%)
    ppermute x6, starting transfers between devices, sent(): lax.ppermute(value, 'tm', [(s, d) for s, d in pairs if 0 <= d < count])  12.1 us
    pallas_call x2, Pallas kernels, tick(): pl.pallas_call(functools.partial(tick_kernel, moment), out_shape=(restore...  6.82 us
    ppermute x6, starting transfers between devices, swapped(): return lax.ppermute(value, 'tile', [(0, 1), (1, 0)])  6.8 us
    pallas_call x1, Pallas kernels, near(): pl.pallas_call(near_kernel, out_shape=(out, out), in_specs=[VMEM] * (1 +...  2.02 us
    pallas_call x1, Pallas kernels, frame_parts(): pl.pallas_call(frame_kernel, out_shape=(jax.ShapeDtypeStruct((moments,) +...  1.73 us
    pallas_call x1, Pallas kernels, head(): pl.pallas_call(head_kernel, out_shape=pltpu.VMEM((channels, pixels + LANE...  1.09 us
    pallas_call x1, Pallas kernels, near_frames(): pl.pallas_call(near_frame_kernel, out_shape=(jax.ShapeDtypeStruct((2, 2 *...  1 us
    pallas_call x1, Pallas kernels, pair_weights(): pl.pallas_call(weights_kernel, out_shape=tuple((jax.ShapeDtypeStruct(shap...  0.74 us
  transfers between devices with their start and end apart: 12, of which 0 were waited for; matrix products, arithmetic and copies ran while one was open for 0% of the time, Pallas kernels for 28%

profile of v3, /device:TPU:13, one launch (start us, length us, event | category | flops | bytes accessed | tf_op | source)
XLA Modules:
  0.0 34.2 jit_solution(16133196534830600331)
XLA Ops:
  0.6 0.0 copy-start.3
  0.6 0.0 copy-start.4
  0.7 0.0 copy-start.5
  0.7 0.0 copy-start.7
  0.7 0.0 copy-start.2
  0.7 0.0 copy-start.6
  0.7 0.0 copy-start.1
  0.7 1.1 %head.1 = bf16[64,2176]{1,0:T(8,128)(2,1)S(1)} custom-call(bf16[2,1,1,64,2048]{4,3,2,1,0:T(8,128)(2,1)} %frames.3, s32[2,1,16]{2,1,0:T(1,128)} %forward_index.3, s32[2,1,16]{2,1,0:T(1,128)} %backward_index.3), custom_call_target="tpu_custom_call" | custom-call | flops 1073741824 | bytes 524288 | tf_op jit(solution)/shard_map/head/pallas_call | solution.py:399
  1.8 0.0 copy-start
  1.8 0.3 collective-permute-start.1
  2.1 0.0 copy-done.3
  2.1 0.0 copy-done.4
  2.1 0.5 %pack.1 = (bf16[128,1024]{1,0:T(8,128)(2,1)S(1)}, bf16[128,1024]{1,0:T(8,128)(2,1)S(1)}) custom-call(bf16[1,1,64,2048]{3,2,1,0:T(8,128)(2,1)S(1)} %copy-done.3, bf16[1,1,64,2048]{3,2,1,0:T(8,128)(2,1)S(1)} %copy-done.4), custom_call_target="tpu_custom_call" | custom-call | flops 536870912 | bytes 524288 | tf_op jit(solution)/shard_map/pack/pallas_call | solution.py:418
  2.6 1.9 %collective-permute-start.3 = (bf16[128,1024]{1,0:T(8,128)(2,1)S(1)}, bf16[128,1024]{1,0:T(8,128)(2,1)S(1)}, u32[]{:S(2)}, u32[]{:S(2)}) collective-permute-start(bf16[128,1024]{1,0:T(8,128)(2,1)S(1)} %get-tuple-element.30), channel_id=1, source_target_pairs={{0,4},{4,8},{6,2},{8,12},{10,6},{14,10},{1,5},{5,9},{7,3},{9,13},{... | collective-permute-start | bytes 786440 | tf_op jit(solution)/shard_map/ppermute | solution.py:559
  4.6 3.4 %collective-permute-start = (bf16[128,1024]{1,0:T(8,128)(2,1)S(1)}, bf16[128,1024]{1,0:T(8,128)(2,1)S(1)}, u32[]{:S(2)}, u32[]{:S(2)}) collective-permute-start(bf16[128,1024]{1,0:T(8,128)(2,1)S(1)} %get-tuple-element.40), channel_id=1, source_target_pairs={{2,6},{4,0},{6,10},{8,4},{10,14},{12,8},{3,7},{5,1},{7,11},{9,5},{... | collective-permute-start | bytes 786440 | tf_op jit(solution)/shard_map/ppermute | solution.py:559
  7.9 1.3 %collective-permute-start.6 = (bf16[128,1024]{1,0:T(8,128)(2,1)S(1)}, bf16[128,1024]{1,0:T(8,128)(2,1)S(1)}, u32[]{:S(2)}, u32[]{:S(2)}) collective-permute-start(bf16[128,1024]{1,0:T(8,128)(2,1)S(1)} %get-tuple-element.30), channel_id=1, source_target_pairs={{0,2},{2,0},{4,6},{6,4},{8,10},{10,8},{12,14},{14,12},{1,3},{3,1},... | collective-permute-start | bytes 786440 | tf_op jit(solution)/shard_map/ppermute | solution.py:559
  9.3 0.0 copy-done.5
  9.3 0.0 copy-done.7
  9.3 0.0 copy-done.2
  9.3 0.0 copy-done.6
  9.3 0.0 copy-done.1
  9.3 0.7 %pair_weights.1 = (bf16[3,256,256]{2,1,0:T(8,128)(2,1)S(1)}, bf16[2,3,128,256]{3,2,1,0:T(8,128)(2,1)S(1)}, bf16[2,1,2,3,128,256]{5,4,3,2,1,0:T(8,128)(2,1)S(1)},...) custom-call(bf16[9,64,128]{2,1,0:T(8,128)(2,1)S(1)} %copy-done.5, ...), custom_call_target="tpu_custom_call" | custom-call | flops 536870912 | bytes 1048576 | tf_op jit(solution)/shard_map/pair_weights/pallas_call | solution.py:441
  10.0 0.0 collective-permute-done.1.pair_frame
  10.0 3.1 %collective-permute-start.7 = (bf16[128,1024]{1,0:T(8,128)(2,1)S(1)}, bf16[128,1024]{1,0:T(8,128)(2,1)S(1)}, u32[]{:S(2)}, u32[]{:S(2)}) collective-permute-start(bf16[128,1024]{1,0:T(8,128)(2,1)S(1)} %get-tuple-element.40), channel_id=1, source_target_pairs={{2,4},{4,2},{6,8},{8,6},{10,12},{12,10},{3,5},{5,3},{7,9},{9,7},{1... | collective-permute-start | bytes 786440 | tf_op jit(solution)/shard_map/ppermute | solution.py:559
  13.2 2.1 %collective-permute-start.5 = (bf16[64,2176]{1,0:T(8,128)(2,1)S(1)}, bf16[64,2176]{1,0:T(8,128)(2,1)S(1)}, u32[]{:S(2)}, u32[]{:S(2)}) collective-permute-start(bf16[64,2176]{1,0:T(8,128)(2,1)S(1)} %collective-permute-done.1.pair_frame), channel_id=1, source_target_pairs={{0,4},{4,8},{6,2},{8,12},{10,6},{14,10},{1,5},{5,9},{7,3},{9,13},{... | collective-permute-start | bytes 835592 | tf_op jit(solution)/shard_map/ppermute | solution.py:559
  15.3 0.0 copy-done
  15.3 0.0 copy-start.8
  15.3 0.0 copy-start.9
  15.3 1.7 %frame_parts.1 = (bf16[2,128,1024]{2,1,0:T(8,128)(2,1)S(1)}, f32[2,2,128,1024]{3,2,1,0:T(8,128)S(1)}) custom-call(bf16[2,1,1,64,2048]{4,3,2,1,0:T(8,128)(2,1)S(1)} %copy-done, bf16[3,256,256]{2,1,0:T(8,128)(2,1)S(1)} %get-tuple-element.38.entry_frame, bf16[512,512]{1,0:T(8,128)(2,1)S(1)} %get-tuple-element.34.matrix), custom_call_target="tpu_custom_call" | custom-call | flops 2147483648 | bytes 1048576 | tf_op jit(solution)/shard_map/frame_parts/pallas_call | solution.py:476
  17.0 0.0 collective-permute-done.3.other_own
  17.0 0.0 collective-permute-done.pair_own
  17.1 2.4 %collective-permute-start.2 = (bf16[128,1024]{1,0:T(8,128)(2,1)S(1)}, bf16[128,1024]{1,0:T(8,128)(2,1)S(1)}, u32[]{:S(2)}, u32[]{:S(2)}) collective-permute-start(bf16[128,1024]{1,0:T(8,128)(2,1)S(1)} %collective-permute-done.pair_own), channel_id=1, source_target_pairs={{0,1},{1,0},{2,3},{3,2},{4,5},{5,4},{6,7},{7,6},{8,9},{9,8},{10,11... | collective-permute-start | bytes 786440 | tf_op jit(solution)/shard_map/ppermute | solution.py:563
  19.5 0.1 collective-permute-start.4
  19.5 0.0 copy-done.8
  19.6 0.0 copy-done.9
  19.6 0.4 %all_picks.1.picks = bf16[2,2,2,256,256]{4,3,2,1,0:T(8,128)(2,1)S(1)} custom-call(s32[2,1,16]{2,1,0:T(1,128)S(1)} %copy-done.8, s32[2,1,16]{2,1,0:T(1,128)S(1)} %copy-done.9), custom_call_target="tpu_custom_call" | custom-call | flops 536870912 | bytes 1048576 | tf_op jit(solution)/shard_map/all_picks/pallas_call | solution.py:453
  20.0 0.0 collective-permute-done.6.first_own
  20.0 1.4 %collective-permute-start.10 = (bf16[128,1024]{1,0:T(8,128)(2,1)S(1)}, bf16[128,1024]{1,0:T(8,128)(2,1)S(1)}, u32[]{:S(2)}, u32[]{:S(2)}) collective-permute-start(bf16[128,1024]{1,0:T(8,128)(2,1)S(1)} %collective-permute-done.6.first_own), channel_id=1, source_target_pairs={{0,1},{1,0},{2,3},{3,2},{4,5},{5,4},{6,7},{7,6},{8,9},{9,8},{10,11... | collective-permute-start | bytes 786440 | tf_op jit(solution)/shard_map/ppermute | solution.py:563
  21.4 0.0 collective-permute-done.7.second_own
  21.4 1.6 %collective-permute-start.11 = (bf16[128,1024]{1,0:T(8,128)(2,1)S(1)}, bf16[128,1024]{1,0:T(8,128)(2,1)S(1)}, u32[]{:S(2)}, u32[]{:S(2)}) collective-permute-start(bf16[128,1024]{1,0:T(8,128)(2,1)S(1)} %collective-permute-done.7.second_own), channel_id=1, source_target_pairs={{0,1},{1,0},{2,3},{3,2},{4,5},{5,4},{6,7},{7,6},{8,9},{9,8},{10,11... | collective-permute-start | bytes 786440 | tf_op jit(solution)/shard_map/ppermute | solution.py:563
  23.0 0.0 collective-permute-done.5.other_frame
  23.0 1.0 %near_frames.1 = (f32[2,128,1024]{2,1,0:T(8,128)S(1)}, bf16[2,2,256,256]{3,2,1,0:T(8,128)(2,1)S(1)}) custom-call(bf16[64,2176]{1,0:T(8,128)(2,1)S(1)} %collective-permute-done.1.pair_frame, bf16[64,2176]{1,0:T(8,128)(2,1)S(1)} %collective-permute-done.5.other_frame, bf16[3,256,256]{2,1,0:T(8,128)(2,1)S(1)} %get-tuple-element.38.entry_frame, ...), custom_call_target="tpu_custom_call" | custom-call | flops 1073741824 | bytes 524288 | tf_op jit(solution)/shard_map/near_frames/pallas_call | solution.py:494
  24.1 0.0 collective-permute-done.2.pair_swapped
  24.1 0.0 collective-permute-done.4.other_swapped
  24.1 2.0 %near.1 = (bf16[128,1024]{1,0:T(8,128)(2,1)S(1)}, bf16[128,1024]{1,0:T(8,128)(2,1)S(1)}) custom-call(bf16[128,1024]{1,0:T(8,128)(2,1)S(1)} %collective-permute-done.pair_own, bf16[128,1024]{1,0:T(8,128)(2,1)S(1)} %collective-permute-done.2.pair_swapped, bf16[128,1024]{1,0:T(8,128)(2,1)S(1)} %collective-permute-done.3.other_own, ...), custom_call_target="tpu_custom_call" | custom-call | flops 2147483648 | bytes 524288 | tf_op jit(solution)/shard_map/near/pallas_call | solution.py:513
  26.1 1.2 %collective-permute-start.8 = (bf16[128,1024]{1,0:T(8,128)(2,1)S(1)}, bf16[128,1024]{1,0:T(8,128)(2,1)S(1)}, u32[]{:S(2)}, u32[]{:S(2)}) collective-permute-start(bf16[128,1024]{1,0:T(8,128)(2,1)S(1)} %get-tuple-element.45.first_own), channel_id=1, source_target_pairs={{0,1},{1,0},{2,3},{3,2},{4,5},{5,4},{6,7},{7,6},{8,9},{9,8},{10,11... | collective-permute-start | bytes 786440 | tf_op jit(solution)/shard_map/ppermute | solution.py:563
  27.3 0.1 collective-permute-start.9
  27.4 0.0 collective-permute-done.10.first_swapped
  27.4 0.0 collective-permute-done.11.second_swapped
  27.4 3.3 %tick_0.1.rest_0_ = bf16[2,64,2048]{2,1,0:T(8,128)(2,1)} custom-call(bf16[128,1024]{1,0:T(8,128)(2,1)S(1)} %collective-permute-done.6.first_own, bf16[128,1024]{1,0:T(8,128)(2,1)S(1)} %collective-permute-done.10.first_swapped, bf16[128,1024]{1,0:T(8,128)(2,1)S(1)} %collective-permute-done.7.second_own, ...), custom_call_target="tpu_custom_call" | custom-call | flops 4294967296 | bytes 524288 | tf_op jit(solution)/shard_map/tick_0/pallas_call | solution.py:537
  30.7 0.0 collective-permute-done.8.first_swapped
  30.7 0.0 collective-permute-done.9.second_swapped
  30.7 3.5 %tick_1.1 = (bf16[2,64,2048]{2,1,0:T(8,128)(2,1)}, bf16[64,2048]{1,0:T(8,128)(2,1)}, bf16[64,2048]{1,0:T(8,128)(2,1)}) custom-call(bf16[128,1024]{1,0:T(8,128)(2,1)S(1)} %get-tuple-element.45.first_own, bf16[128,1024]{1,0:T(8,128)(2,1)S(1)} %collective-permute-done.8.first_swapped, ...), custom_call_target="tpu_custom_call", output_to_operand_aliasing={{0}: (11, {})} | custom-call | flops 4294967296 | bytes 524288 | tf_op jit(solution)/shard_map/tick_1/pallas_call | solution.py:537
Async XLA Ops:
  0.6 1.5 %copy-start.3 = (bf16[1,1,64,2048]{3,2,1,0:T(8,128)(2,1)S(1)}, bf16[1,1,64,2048]{3,2,1,0:T(8,128)(2,1)}, u32[]{:S(2)}) copy-start(bf16[1,1,64,2048]{3,2,1,0:T(8,128)(2,1)} %forward) | copy-start | bytes 786436
  0.6 1.5 %copy-start.4 = (bf16[1,1,64,2048]{3,2,1,0:T(8,128)(2,1)S(1)}, bf16[1,1,64,2048]{3,2,1,0:T(8,128)(2,1)}, u32[]{:S(2)}) copy-start(bf16[1,1,64,2048]{3,2,1,0:T(8,128)(2,1)} %backward.1) | copy-start | bytes 786436
  0.7 8.6 %copy-start.5 = (bf16[9,64,128]{2,1,0:T(8,128)(2,1)S(1)}, bf16[9,64,128]{2,1,0:T(8,128)(2,1)}, u32[]{:S(2)}) copy-start(bf16[9,64,128]{2,1,0:T(8,128)(2,1)} %fe) | copy-start | bytes 442372
  0.7 8.6 %copy-start.7 = (bf16[64,128]{1,0:T(8,128)(2,1)S(1)}, bf16[64,128]{1,0:T(8,128)(2,1)}, u32[]{:S(2)}) copy-start(bf16[64,128]{1,0:T(8,128)(2,1)} %mixing.1) | copy-start | bytes 49156
  0.7 8.6 %copy-start.2 = (bf16[1,2,9,64,64]{4,3,2,1,0:T(8,128)(2,1)S(1)}, bf16[1,2,9,64,64]{4,3,2,1,0:T(8,128)(2,1)}, u32[]{:S(2)}) copy-start(bf16[1,2,9,64,64]{4,3,2,1,0:T(8,128)(2,1)} %bb.1) | copy-start | bytes 442372
  0.7 8.6 %copy-start.6 = (bf16[9,64,128]{2,1,0:T(8,128)(2,1)S(1)}, bf16[9,64,128]{2,1,0:T(8,128)(2,1)}, u32[]{:S(2)}) copy-start(bf16[9,64,128]{2,1,0:T(8,128)(2,1)} %be.1) | copy-start | bytes 442372
  0.7 8.6 %copy-start.1 = (bf16[1,2,9,64,64]{4,3,2,1,0:T(8,128)(2,1)S(1)}, bf16[1,2,9,64,64]{4,3,2,1,0:T(8,128)(2,1)}, u32[]{:S(2)}) copy-start(bf16[1,2,9,64,64]{4,3,2,1,0:T(8,128)(2,1)} %fb.1) | copy-start | bytes 442372
  1.8 13.5 %copy-start = (bf16[2,1,1,64,2048]{4,3,2,1,0:T(8,128)(2,1)S(1)}, bf16[2,1,1,64,2048]{4,3,2,1,0:T(8,128)(2,1)}, u32[]{:S(2)}) copy-start(bf16[2,1,1,64,2048]{4,3,2,1,0:T(8,128)(2,1)} %frames.3) | copy-start | bytes 1572868
  1.8 8.2 %collective-permute-start.1 = (bf16[64,2176]{1,0:T(8,128)(2,1)S(1)}, bf16[64,2176]{1,0:T(8,128)(2,1)S(1)}, u32[]{:S(2)}, u32[]{:S(2)}) collective-permute-start(bf16[64,2176]{1,0:T(8,128)(2,1)S(1)} %head.1), channel_id=1, source_target_pairs={{0,2},{2,0},{4,6},{6,4},{8,10},{10,8},{12,14},{14,12},{1,3},{3,1},... | collective-permute-start | bytes 835592 | tf_op jit(solution)/shard_map/ppermute | solution.py:559
  2.6 14.4 %collective-permute-start.3 = (bf16[128,1024]{1,0:T(8,128)(2,1)S(1)}, bf16[128,1024]{1,0:T(8,128)(2,1)S(1)}, u32[]{:S(2)}, u32[]{:S(2)}) collective-permute-start(bf16[128,1024]{1,0:T(8,128)(2,1)S(1)} %get-tuple-element.30), channel_id=1, source_target_pairs={{0,4},{4,8},{6,2},{8,12},{10,6},{14,10},{1,5},{5,9},{7,3},{9,13},{... | collective-permute-start | bytes 786440 | tf_op jit(solution)/shard_map/ppermute | solution.py:559
  4.6 12.5 %collective-permute-start = (bf16[128,1024]{1,0:T(8,128)(2,1)S(1)}, bf16[128,1024]{1,0:T(8,128)(2,1)S(1)}, u32[]{:S(2)}, u32[]{:S(2)}) collective-permute-start(bf16[128,1024]{1,0:T(8,128)(2,1)S(1)} %get-tuple-element.40), channel_id=1, source_target_pairs={{2,6},{4,0},{6,10},{8,4},{10,14},{12,8},{3,7},{5,1},{7,11},{9,5},{... | collective-permute-start | bytes 786440 | tf_op jit(solution)/shard_map/ppermute | solution.py:559
  7.9 12.0 %collective-permute-start.6 = (bf16[128,1024]{1,0:T(8,128)(2,1)S(1)}, bf16[128,1024]{1,0:T(8,128)(2,1)S(1)}, u32[]{:S(2)}, u32[]{:S(2)}) collective-permute-start(bf16[128,1024]{1,0:T(8,128)(2,1)S(1)} %get-tuple-element.30), channel_id=1, source_target_pairs={{0,2},{2,0},{4,6},{6,4},{8,10},{10,8},{12,14},{14,12},{1,3},{3,1},... | collective-permute-start | bytes 786440 | tf_op jit(solution)/shard_map/ppermute | solution.py:559
  10.0 11.4 %collective-permute-start.7 = (bf16[128,1024]{1,0:T(8,128)(2,1)S(1)}, bf16[128,1024]{1,0:T(8,128)(2,1)S(1)}, u32[]{:S(2)}, u32[]{:S(2)}) collective-permute-start(bf16[128,1024]{1,0:T(8,128)(2,1)S(1)} %get-tuple-element.40), channel_id=1, source_target_pairs={{2,4},{4,2},{6,8},{8,6},{10,12},{12,10},{3,5},{5,3},{7,9},{9,7},{1... | collective-permute-start | bytes 786440 | tf_op jit(solution)/shard_map/ppermute | solution.py:559
  13.2 9.9 %collective-permute-start.5 = (bf16[64,2176]{1,0:T(8,128)(2,1)S(1)}, bf16[64,2176]{1,0:T(8,128)(2,1)S(1)}, u32[]{:S(2)}, u32[]{:S(2)}) collective-permute-start(bf16[64,2176]{1,0:T(8,128)(2,1)S(1)} %collective-permute-done.1.pair_frame), channel_id=1, source_target_pairs={{0,4},{4,8},{6,2},{8,12},{10,6},{14,10},{1,5},{5,9},{7,3},{9,13},{... | collective-permute-start | bytes 835592 | tf_op jit(solution)/shard_map/ppermute | solution.py:559
  15.3 4.3 %copy-start.8 = (s32[2,1,16]{2,1,0:T(1,128)S(1)}, s32[2,1,16]{2,1,0:T(1,128)}, u32[]{:S(2)}) copy-start(s32[2,1,16]{2,1,0:T(1,128)} %forward_index.3) | copy-start | bytes 388
  15.3 4.3 %copy-start.9 = (s32[2,1,16]{2,1,0:T(1,128)S(1)}, s32[2,1,16]{2,1,0:T(1,128)}, u32[]{:S(2)}) copy-start(s32[2,1,16]{2,1,0:T(1,128)} %backward_index.3) | copy-start | bytes 388
  17.1 7.0 %collective-permute-start.2 = (bf16[128,1024]{1,0:T(8,128)(2,1)S(1)}, bf16[128,1024]{1,0:T(8,128)(2,1)S(1)}, u32[]{:S(2)}, u32[]{:S(2)}) collective-permute-start(bf16[128,1024]{1,0:T(8,128)(2,1)S(1)} %collective-permute-done.pair_own), channel_id=1, source_target_pairs={{0,1},{1,0},{2,3},{3,2},{4,5},{5,4},{6,7},{7,6},{8,9},{9,8},{10,11... | collective-permute-start | bytes 786440 | tf_op jit(solution)/shard_map/ppermute | solution.py:563
  19.5 4.6 %collective-permute-start.4 = (bf16[128,1024]{1,0:T(8,128)(2,1)S(1)}, bf16[128,1024]{1,0:T(8,128)(2,1)S(1)}, u32[]{:S(2)}, u32[]{:S(2)}) collective-permute-start(bf16[128,1024]{1,0:T(8,128)(2,1)S(1)} %collective-permute-done.3.other_own), channel_id=1, source_target_pairs={{0,1},{1,0},{2,3},{3,2},{4,5},{5,4},{6,7},{7,6},{8,9},{9,8},{10,11... | collective-permute-start | bytes 786440 | tf_op jit(solution)/shard_map/ppermute | solution.py:563
  20.0 7.4 %collective-permute-start.10 = (bf16[128,1024]{1,0:T(8,128)(2,1)S(1)}, bf16[128,1024]{1,0:T(8,128)(2,1)S(1)}, u32[]{:S(2)}, u32[]{:S(2)}) collective-permute-start(bf16[128,1024]{1,0:T(8,128)(2,1)S(1)} %collective-permute-done.6.first_own), channel_id=1, source_target_pairs={{0,1},{1,0},{2,3},{3,2},{4,5},{5,4},{6,7},{7,6},{8,9},{9,8},{10,11... | collective-permute-start | bytes 786440 | tf_op jit(solution)/shard_map/ppermute | solution.py:563
  21.4 6.0 %collective-permute-start.11 = (bf16[128,1024]{1,0:T(8,128)(2,1)S(1)}, bf16[128,1024]{1,0:T(8,128)(2,1)S(1)}, u32[]{:S(2)}, u32[]{:S(2)}) collective-permute-start(bf16[128,1024]{1,0:T(8,128)(2,1)S(1)} %collective-permute-done.7.second_own), channel_id=1, source_target_pairs={{0,1},{1,0},{2,3},{3,2},{4,5},{5,4},{6,7},{7,6},{8,9},{9,8},{10,11... | collective-permute-start | bytes 786440 | tf_op jit(solution)/shard_map/ppermute | solution.py:563
  26.1 4.6 %collective-permute-start.8 = (bf16[128,1024]{1,0:T(8,128)(2,1)S(1)}, bf16[128,1024]{1,0:T(8,128)(2,1)S(1)}, u32[]{:S(2)}, u32[]{:S(2)}) collective-permute-start(bf16[128,1024]{1,0:T(8,128)(2,1)S(1)} %get-tuple-element.45.first_own), channel_id=1, source_target_pairs={{0,1},{1,0},{2,3},{3,2},{4,5},{5,4},{6,7},{7,6},{8,9},{9,8},{10,11... | collective-permute-start | bytes 786440 | tf_op jit(solution)/shard_map/ppermute | solution.py:563
  27.3 3.4 %collective-permute-start.9 = (bf16[128,1024]{1,0:T(8,128)(2,1)S(1)}, bf16[128,1024]{1,0:T(8,128)(2,1)S(1)}, u32[]{:S(2)}, u32[]{:S(2)}) collective-permute-start(bf16[128,1024]{1,0:T(8,128)(2,1)S(1)} %get-tuple-element.46.second_own), channel_id=1, source_target_pairs={{0,1},{1,0},{2,3},{3,2},{4,5},{5,4},{6,7},{7,6},{8,9},{9,8},{10,11... | collective-permute-start | bytes 786440 | tf_op jit(solution)/shard_map/ppermute | solution.py:563

commit v4 on v3

--- a/solution.py
+++ b/solution.py
@@ -167,28 +167,29 @@
     return jnp.maximum(u, 0.1 * u).astype(BF16)
 
 
-def both_convolve(stacks, weights, starts):
+def side_by_side(stacks, weights, starts):
     for here in zip(*(convolve(*operands) for operands in zip(stacks, weights, starts))):
         yield here[0][0], [u for _, u in here]
 
 
-def chains(first, second, entry, starts, layers):
-    both = range(2)
-    nothing = (None, None)
-    hidden = [[None] * BH for _ in both]
-    for i, values in both_convolve(first, [entry.at[d] for d in both], starts):
-        for d in both:
-            hidden[d][i] = lrelu(values[d])
-            put_taps(second[d], i, hidden[d][i])
-    for layer in range(layers.shape[1]):
-        for i, values in both_convolve(second, [layers.at[d, layer, 0] for d in both], nothing):
-            for d in both:
-                put_taps(first[d], i, lrelu(values[d]))
-        for i, values in both_convolve(first, [layers.at[d, layer, 1] for d in both], nothing):
-            for d in both:
-                hidden[d][i] = (hidden[d][i].astype(F32) + values[d]).astype(BF16)
-                if layer + 1 < layers.shape[1]:
-                    put_taps(second[d], i, hidden[d][i])
+def chains(first, second, entries, starts, layers):
+    count = range(len(first))
+    nothing = [None] * len(first)
+    hidden = [[None] * BH for _ in count]
+    for i, values in side_by_side(first, entries, starts):
+        for c in count:
+            hidden[c][i] = lrelu(values[c])
+            put_taps(second[c], i, hidden[c][i])
+    depth = layers[0].shape[0]
+    for layer in range(depth):
+        for i, values in side_by_side(second, [w.at[layer, 0] for w in layers], nothing):
+            for c in count:
+                put_taps(first[c], i, lrelu(values[c]))
+        for i, values in side_by_side(first, [w.at[layer, 1] for w in layers], nothing):
+            for c in count:
+                hidden[c][i] = (hidden[c][i].astype(F32) + values[c]).astype(BF16)
+                if layer + 1 < depth:
+                    put_taps(second[c], i, hidden[c][i])
     return hidden
 
 
@@ -222,8 +223,27 @@
         far_out[:, columns] = jnp.where(even, b, f)
 
 
-def frame_kernel(frames, entry_frame, matrix, *rest):
-    paired, parts, stack = rest
+def side_direction(pair_side):
+    parity = lax.axis_index("tm") % 2
+    return 1 - parity if pair_side else parity
+
+
+def neighbour_part(payload, direction, entry_frame, matrix, part, picks, stack):
+    channels = payload.shape[0]
+    width = NATURAL * LANES
+    half = channels // 2
+    for i, group in enumerate(to_paired(cut(payload[:, :width], NATURAL), matrix[...])):
+        put_taps(stack, i, group)
+    lists = [payload[d * half : d * half + REGION_BLOCKS, width:].astype(F32)[:1] for d in range(2)]
+    source = jnp.where(direction == 0, lists[0], lists[1])
+    for k, pick in enumerate(picks_of(target_of(source, lax.axis_index("tile")))):
+        picks[k] = pick
+    rows = pl.ds(pl.multiple_of(direction * 2 * channels, 2 * channels), 2 * channels)
+    for i, group in convolve(stack, [entry_frame[a, rows] for a in range(3)]):
+        part[:, i * LANES : (i + 1) * LANES] = group
+
+
+def frame_kernel(frames, pair_frame, entry_frame, matrix, paired, parts, pair_part, pair_picks, stack, pair_stack):
     channels = frames.shape[-2]
     for moment in range(frames.shape[0]):
         for i, group in enumerate(to_paired(cut(frames[moment, 0, 0], NATURAL), matrix[...])):
@@ -234,6 +254,11 @@
                 parts[moment, d, :, i * LANES : (i + 1) * LANES] = group[
                     2 * d * channels : 2 * (d + 1) * channels
                 ]
+    neighbour_part(pair_frame, side_direction(True), entry_frame, matrix, pair_part, pair_picks, pair_stack)
+
+
+def other_frame_kernel(other_frame, entry_frame, matrix, part, picks, stack):
+    neighbour_part(other_frame, side_direction(False), entry_frame, matrix, part, picks, stack)
 
 
 def tap_weight(taps):
@@ -277,51 +302,35 @@
                 out[moment, d, half] = pick
 
 
-def by_direction(even, pair_side, other_side):
-    first, second = pair_side[...], other_side[...]
-    return jnp.where(even, second, first), jnp.where(even, first, second)
-
-
-def near_frame_kernel(pair_frame, other_frame, entry_frame, matrix, out, picks, stack):
-    even = even_segment()
-    tile = lax.axis_index("tile")
-    width = NATURAL * LANES
-    channels = pair_frame.shape[0]
-    half = channels // 2
-    payloads = by_direction(even, pair_frame, other_frame)
-    for d in range(2):
-        for i, group in enumerate(to_paired(cut(payloads[d][:, :width], NATURAL), matrix[...])):
-            put_taps(stack.at[d], i, group)
-        source = payloads[d][d * half : d * half + REGION_BLOCKS, width:].astype(F32)[:1]
-        for part, pick in enumerate(picks_of(target_of(source, tile))):
-            picks[d, part] = pick
-    for d in range(2):
-        weight = [entry_frame[a, 2 * d * channels : 2 * (d + 1) * channels] for a in range(3)]
-        for i, group in convolve(stack.at[d], weight):
-            out[d, :, i * LANES : (i + 1) * LANES] = group
-
-
 def near_kernel(
     pair_own,
     pair_swapped,
     other_own,
     other_swapped,
-    starts,
-    picks,
-    entry_warped,
+    pair_part,
+    other_part,
+    pair_picks,
+    other_picks,
+    entry,
     layers,
-    forward_out,
-    backward_out,
+    pair_out,
+    other_out,
     *stacks,
 ):
-    even = even_segment()
     firsts, seconds = stacks[:2], stacks[2:]
-    owns = by_direction(even, pair_own, other_own)
-    others = by_direction(even, pair_swapped, other_swapped)
-    for d in range(2):
-        put_warped(firsts[d], (cut(owns[d], BH), cut(others[d], BH)), picks[d])
-    hidden = chains(firsts, seconds, entry_warped, [starts.at[d] for d in range(2)], layers)
-    for groups, out in zip(hidden, (forward_out, backward_out)):
+    directions = (side_direction(True), side_direction(False))
+    for c, (tiles, picks) in enumerate(
+        (((pair_own, pair_swapped), pair_picks), ((other_own, other_swapped), other_picks))
+    ):
+        put_warped(firsts[c], [cut(t[...], BH) for t in tiles], [picks[k] for k in range(2)])
+    hidden = chains(
+        firsts,
+        seconds,
+        [entry.at[d] for d in directions],
+        [pair_part, other_part],
+        [layers.at[d] for d in directions],
+    )
+    for groups, out in zip(hidden, (pair_out, other_out)):
         for i, group in enumerate(groups):
             out[:, i * LANES : (i + 1) * LANES] = group
 
@@ -345,42 +354,52 @@
 
 def tick_kernel(
     moment,
-    first_own,
-    first_swapped,
-    second_own,
-    second_swapped,
+    pair_own,
+    pair_swapped,
+    other_own,
+    other_swapped,
     picks,
     paired,
     parts,
-    entry_warped,
+    entry,
     layers,
     mix_pair,
     back,
     *rest,
 ):
-    *_, restored, forward_final, backward_final = rest[:-8] if moment > 0 else rest[:-8] + (None, None)
-    *stacks, finals, mixed, final_sems, mixed_sem = rest[-8:]
+    copies = []
+    if moment > 0:
+        earlier, restored, forward_final, backward_final, *stacks, finals, mixed, sems = rest
+        copies.append(pltpu.make_async_copy(earlier, restored.at[0], sems.at[3]))
+        copies[-1].start()
+    else:
+        mixed, *stacks = rest
     firsts, seconds = stacks[:2], stacks[2:]
-    owns, others = (first_own[...], second_own[...]), (first_swapped[...], second_swapped[...])
-    if moment == 0:
-        even = even_segment()
-        owns = by_direction(even, first_own, second_own)
-        others = by_direction(even, first_swapped, second_swapped)
-    for d in range(2):
-        put_warped(firsts[d], (cut(owns[d], BH), cut(others[d], BH)), picks[moment, d])
-    hidden = chains(firsts, seconds, entry_warped, [parts.at[moment, d] for d in range(2)], layers)
-    copies = []
-    for d, groups in enumerate(to_natural(hidden, back[...]) if moment > 0 else []):
-        put_natural(finals.at[d], groups)
-        out = (forward_final, backward_final)[d]
-        copies.append(pltpu.make_async_copy(finals.at[d], out, final_sems.at[d]))
+    directions = (side_direction(True), side_direction(False))
+    for c, tiles in enumerate(((pair_own, pair_swapped), (other_own, other_swapped))):
+        here = [picks[moment, directions[c], k] for k in range(2)]
+        put_warped(firsts[c], [cut(t[...], BH) for t in tiles], here)
+    hidden = chains(
+        firsts,
+        seconds,
+        [entry.at[d] for d in directions],
+        [parts.at[moment, d] for d in directions],
+        [layers.at[d] for d in directions],
+    )
+    for c, groups in enumerate(to_natural(hidden, back[...]) if moment > 0 else []):
+        put_natural(finals.at[c], groups)
+        forward_copy = pltpu.make_async_copy(finals.at[c], forward_final, sems.at[c])
+        backward_copy = pltpu.make_async_copy(finals.at[c], backward_final, sems.at[c])
+        pl.when(directions[c] == 0)(forward_copy.start)
+        pl.when(directions[c] == 1)(backward_copy.start)
+        copies.append(forward_copy)
+    total = cut(paired[moment].astype(F32), BH)
+    for d, state in zip(directions, hidden):
+        total = mix(mix_pair[d], state, total)
+    put_natural(mixed, to_natural([rounded(total)], back[...])[0])
+    if moment > 0:
+        copies.append(pltpu.make_async_copy(mixed, restored.at[moment], sems.at[2]))
         copies[-1].start()
-    total = cut(paired[moment].astype(F32), BH)
-    for d in range(2):
-        total = mix(mix_pair[d], hidden[d], total)
-    put_natural(mixed, to_natural([rounded(total)], back[...])[0])
-    copies.append(pltpu.make_async_copy(mixed, restored.at[moment], mixed_sem))
-    copies[-1].start()
     for copy in copies:
         copy.wait()
 
@@ -470,40 +489,42 @@
     return (2 * channels, pixels // 2)
 
 
-def frame_parts(frames, entry_frame, matrix):
+def frame_parts(frames, pair_frame, entry_frame, matrix):
     moments = frames.shape[0]
     paired = paired_shape(frames)
+    stack = stack_of(frames.shape[-2])
     return pl.pallas_call(
         frame_kernel,
         out_shape=(
             jax.ShapeDtypeStruct((moments,) + paired, BF16),
             jax.ShapeDtypeStruct((moments, 2) + paired, F32),
+            jax.ShapeDtypeStruct(paired, F32),
+            jax.ShapeDtypeStruct((2, 2 * LANES, 2 * LANES), BF16),
+        ),
+        in_specs=[VMEM] * 4,
+        out_specs=(VMEM,) * 4,
+        scratch_shapes=[stack, stack],
+        compiler_params=PARAMS,
+        cost_estimate=cost(2**31, 2**20),
+        name="frame_parts",
+    )(frames, pair_frame, entry_frame, matrix)
+
+
+def other_frame_part(other_frame, entry_frame, matrix):
+    channels, width = other_frame.shape
+    return pl.pallas_call(
+        other_frame_kernel,
+        out_shape=(
+            jax.ShapeDtypeStruct((2 * channels, (width - LANES) // 2), F32),
+            jax.ShapeDtypeStruct((2, 2 * LANES, 2 * LANES), BF16),
         ),
         in_specs=[VMEM] * 3,
         out_specs=(VMEM, VMEM),
-        scratch_shapes=[stack_of(frames.shape[-2])],
-        compiler_params=PARAMS,
-        cost_estimate=cost(2**31, 2**20),
-        name="frame_parts",
-    )(frames, entry_frame, matrix)
-
-
-def near_frames(pair_frame, other_frame, entry_frame, matrix):
-    channels, width = pair_frame.shape
-    stack = stack_of(channels)
-    return pl.pallas_call(
-        near_frame_kernel,
-        out_shape=(
-            jax.ShapeDtypeStruct((2, 2 * channels, (width - LANES) // 2), F32),
-            jax.ShapeDtypeStruct((2, 2, 2 * LANES, 2 * LANES), BF16),
-        ),
-        in_specs=[VMEM] * 4,
-        out_specs=(VMEM, VMEM),
-        scratch_shapes=[pltpu.VMEM((2,) + stack.shape, BF16)],
+        scratch_shapes=[stack_of(channels)],
         compiler_params=PARAMS,
         cost_estimate=cost(2**30, 2**19),
-        name="near_frames",
-    )(pair_frame, other_frame, entry_frame, matrix)
+        name="other_frame_part",
+    )(other_frame, entry_frame, matrix)
 
 
 def near(pair_own, *rest):
@@ -522,34 +543,38 @@
     )(pair_own, *rest)
 
 
-def tick(moment, frames, *operands, earlier=None):
-    channels, pixels = frames.shape[-2:]
-    restored = jax.ShapeDtypeStruct((frames.shape[0], channels, pixels), BF16)
-    state = jax.ShapeDtypeStruct((channels, pixels), BF16)
-    in_specs = [VMEM] * len(operands)
-    aliases = {}
-    if earlier is not None:
-        aliases = {len(operands): 0}
-        operands += (earlier,)
-        in_specs.append(ANY)
-    finals = (state, state) if moment > 0 else ()
-    stack = stack_of(channels)
-    return pl.pallas_call(
-        functools.partial(tick_kernel, moment),
-        out_shape=(restored,) + finals,
-        in_specs=in_specs,
-        out_specs=(ANY,) * (1 + len(finals)),
+def first_tick(frames, *operands):
+    stack = stack_of(frames.shape[-2])
+    return pl.pallas_call(
+        functools.partial(tick_kernel, 0),
+        out_shape=jax.ShapeDtypeStruct(frames.shape[-2:], BF16),
+        in_specs=[VMEM] * len(operands),
+        out_specs=VMEM,
+        scratch_shapes=[stack] * 4,
+        compiler_params=PARAMS,
+        cost_estimate=cost(2**32, 2**19),
+        name="tick_0",
+    )(*operands)
+
+
+def last_tick(frames, *operands):
+    shape = frames.shape[-2:]
+    state = jax.ShapeDtypeStruct(shape, BF16)
+    stack = stack_of(shape[0])
+    return pl.pallas_call(
+        functools.partial(tick_kernel, 1),
+        out_shape=(jax.ShapeDtypeStruct(frames.shape[:1] + shape, BF16), state, state),
+        in_specs=[VMEM] * len(operands),
+        out_specs=(ANY,) * 3,
         scratch_shapes=[
             *[stack] * 4,
-            pltpu.VMEM((2, channels, pixels), BF16),
-            pltpu.VMEM((channels, pixels), BF16),
-            pltpu.SemaphoreType.DMA((2,)),
-            pltpu.SemaphoreType.DMA,
+            pltpu.VMEM((2,) + shape, BF16),
+            pltpu.VMEM(shape, BF16),
+            pltpu.SemaphoreType.DMA((4,)),
         ],
-        input_output_aliases=aliases,
         compiler_params=PARAMS,
         cost_estimate=cost(2**32, 2**19),
-        name=f"tick_{moment}",
+        name="tick_1",
     )(*operands)
 
 
@@ -588,34 +613,27 @@
         later(forward_entry, near_state), forward_blocks, backward_entry, backward_blocks, mixing_weight
     )
     picks = all_picks(forward_source, backward_source)
-    paired, parts = frame_parts(frames, later(entry_frame, pair_frame), matrix)
+    paired, parts, pair_part, pair_picks = frame_parts(frames, pair_frame, entry_frame, matrix)
     other_frame = sent(pair_frame, 2, -2)
     pair_near = sent(near_state, 1, -1)
     other_near = sent(later(far_state, pair_frame), -1, 1)
-    near_parts, near_picks = near_frames(pair_frame, other_frame, later(entry_frame, parts, picks), matrix)
-    forward_one, backward_one = near(
+    other_part, other_picks = other_frame_part(other_frame, later(entry_frame, parts, picks), matrix)
+    pair_one, other_one = near(
         pair_far,
         swapped(later(pair_far, parts)),
         other_far,
         swapped(later(other_far, parts)),
-        later(near_parts, pair_near, other_near),
-        near_picks,
+        pair_part,
+        later(other_part, pair_near, other_near),
+        pair_picks,
+        other_picks,
         entry_warped,
         layers,
     )
     tables = (picks, paired, parts, entry_warped, layers, mix_pair, back)
-    (restored,) = tick(
-        0, frames, pair_near, swapped(pair_near), other_near, swapped(other_near), *tables
-    )
-    restored, forward_final, backward_final = tick(
-        1,
-        frames,
-        forward_one,
-        swapped(forward_one),
-        backward_one,
-        swapped(backward_one),
-        *tables,
-        earlier=restored,
+    first = first_tick(frames, pair_near, swapped(pair_near), other_near, swapped(other_near), *tables)
+    restored, forward_final, backward_final = last_tick(
+        frames, pair_one, swapped(pair_one), other_one, swapped(other_one), *tables, first
     )
     return (restored[:, None, None], forward_final[None, None], backward_final[None, None])
 

time: 34.4 us -> 33.4 us (0.971)
  starting transfers between devices: 18.9 us -> 18.3 us
  Pallas kernels: 14.3 us -> 13.9 us
    pallas_call x3, Pallas kernels: 7.82 us -> 6.82 us  [the longest x1 3.53 us: last_tick(): pl.pallas_call(functools.partial(tick_kernel, 1), out_shape=(jax.ShapeDty...]
    pallas_call x1, Pallas kernels: 1.73 us -> 2.32 us  [frame_parts(): pl.pallas_call(frame_kernel, out_shape=(jax.ShapeDtypeStruct((moments,) +...]
    ppermute x6, starting transfers between devices: 6.8 us -> 6.22 us  [swapped(): return lax.ppermute(value, 'tile', [(0, 1), (1, 0)])]
where the time goes in v4:
time: 33.4 us; the launch traced here: 33.2 us
  starting transfers between devices  18.3 us (55%)
  Pallas kernels  13.9 us (42%)
  between operations  0.89 us (3%)
    ppermute x6, starting transfers between devices, sent(): lax.ppermute(value, 'tm', [(s, d) for s, d in pairs if 0 <= d < count])  12.1 us
    ppermute x6, starting transfers between devices, swapped(): return lax.ppermute(value, 'tile', [(0, 1), (1, 0)])  6.22 us
    pallas_call x1, Pallas kernels, last_tick(): pl.pallas_call(functools.partial(tick_kernel, 1), out_shape=(jax.ShapeDty...  3.53 us
    pallas_call x1, Pallas kernels, first_tick(): pl.pallas_call(functools.partial(tick_kernel, 0), out_shape=jax.ShapeDtyp...  2.55 us
    pallas_call x1, Pallas kernels, frame_parts(): pl.pallas_call(frame_kernel, out_shape=(jax.ShapeDtypeStruct((moments,) +...  2.32 us
    pallas_call x1, Pallas kernels, near(): pl.pallas_call(near_kernel, out_shape=(out, out), in_specs=[VMEM] * (1 +...  1.99 us
    pallas_call x1, Pallas kernels, head(): pl.pallas_call(head_kernel, out_shape=pltpu.VMEM((channels, pixels + LANE...  1.09 us
    pallas_call x1, Pallas kernels, pair_weights(): pl.pallas_call(weights_kernel, out_shape=tuple((jax.ShapeDtypeStruct(shap...  0.74 us
  transfers between devices with their start and end apart: 12, of which 0 were waited for; matrix products, arithmetic and copies ran while one was open for 0% of the time, Pallas kernels for 28%

profile of v4, /device:TPU:13, one launch (start us, length us, event | category | flops | bytes accessed | tf_op | source)
XLA Modules:
  0.0 33.2 jit_solution(11173859207678102259)
XLA Ops:
  0.6 0.0 copy-start.3
  0.6 0.0 copy-start.4
  0.7 0.0 copy-start.5
  0.7 0.0 copy-start.7
  0.7 0.0 copy-start.2
  0.7 0.0 copy-start.6
  0.7 0.0 copy-start.1
  0.7 1.1 %head.1 = bf16[64,2176]{1,0:T(8,128)(2,1)S(1)} custom-call(bf16[2,1,1,64,2048]{4,3,2,1,0:T(8,128)(2,1)} %frames.3, s32[2,1,16]{2,1,0:T(1,128)} %forward_index.3, s32[2,1,16]{2,1,0:T(1,128)} %backward_index.3), custom_call_target="tpu_custom_call" | custom-call | flops 1073741824 | bytes 524288 | tf_op jit(solution)/shard_map/head/pallas_call | solution.py:418
  1.8 0.0 copy-start
  1.8 0.3 collective-permute-start.1
  2.1 0.0 copy-done.3
  2.1 0.0 copy-done.4
  2.1 0.5 %pack.1 = (bf16[128,1024]{1,0:T(8,128)(2,1)S(1)}, bf16[128,1024]{1,0:T(8,128)(2,1)S(1)}) custom-call(bf16[1,1,64,2048]{3,2,1,0:T(8,128)(2,1)S(1)} %copy-done.3, bf16[1,1,64,2048]{3,2,1,0:T(8,128)(2,1)S(1)} %copy-done.4), custom_call_target="tpu_custom_call" | custom-call | flops 536870912 | bytes 524288 | tf_op jit(solution)/shard_map/pack/pallas_call | solution.py:437
  2.6 1.9 %collective-permute-start.3 = (bf16[128,1024]{1,0:T(8,128)(2,1)S(1)}, bf16[128,1024]{1,0:T(8,128)(2,1)S(1)}, u32[]{:S(2)}, u32[]{:S(2)}) collective-permute-start(bf16[128,1024]{1,0:T(8,128)(2,1)S(1)} %get-tuple-element.31), channel_id=1, source_target_pairs={{0,4},{4,8},{6,2},{8,12},{10,6},{14,10},{1,5},{5,9},{7,3},{9,13},{... | collective-permute-start | bytes 786440 | tf_op jit(solution)/shard_map/ppermute | solution.py:584
  4.6 3.4 %collective-permute-start = (bf16[128,1024]{1,0:T(8,128)(2,1)S(1)}, bf16[128,1024]{1,0:T(8,128)(2,1)S(1)}, u32[]{:S(2)}, u32[]{:S(2)}) collective-permute-start(bf16[128,1024]{1,0:T(8,128)(2,1)S(1)} %get-tuple-element.41), channel_id=1, source_target_pairs={{2,6},{4,0},{6,10},{8,4},{10,14},{12,8},{3,7},{5,1},{7,11},{9,5},{... | collective-permute-start | bytes 786440 | tf_op jit(solution)/shard_map/ppermute | solution.py:584
  7.9 1.3 %collective-permute-start.6 = (bf16[128,1024]{1,0:T(8,128)(2,1)S(1)}, bf16[128,1024]{1,0:T(8,128)(2,1)S(1)}, u32[]{:S(2)}, u32[]{:S(2)}) collective-permute-start(bf16[128,1024]{1,0:T(8,128)(2,1)S(1)} %get-tuple-element.31), channel_id=1, source_target_pairs={{0,2},{2,0},{4,6},{6,4},{8,10},{10,8},{12,14},{14,12},{1,3},{3,1},... | collective-permute-start | bytes 786440 | tf_op jit(solution)/shard_map/ppermute | solution.py:584
  9.3 0.0 copy-done.5
  9.3 0.0 copy-done.7
  9.3 0.0 copy-done.2
  9.3 0.0 copy-done.6
  9.3 0.0 copy-done.1
  9.3 0.7 %pair_weights.1 = (bf16[3,256,256]{2,1,0:T(8,128)(2,1)S(1)}, bf16[2,3,128,256]{3,2,1,0:T(8,128)(2,1)S(1)}, bf16[2,1,2,3,128,256]{5,4,3,2,1,0:T(8,128)(2,1)S(1)},...) custom-call(bf16[9,64,128]{2,1,0:T(8,128)(2,1)S(1)} %copy-done.5, ...), custom_call_target="tpu_custom_call" | custom-call | flops 536870912 | bytes 1048576 | tf_op jit(solution)/shard_map/pair_weights/pallas_call | solution.py:460
  10.0 0.0 collective-permute-done.1.pair_frame
  10.0 3.1 %collective-permute-start.7 = (bf16[128,1024]{1,0:T(8,128)(2,1)S(1)}, bf16[128,1024]{1,0:T(8,128)(2,1)S(1)}, u32[]{:S(2)}, u32[]{:S(2)}) collective-permute-start(bf16[128,1024]{1,0:T(8,128)(2,1)S(1)} %get-tuple-element.41), channel_id=1, source_target_pairs={{2,4},{4,2},{6,8},{8,6},{10,12},{12,10},{3,5},{5,3},{7,9},{9,7},{1... | collective-permute-start | bytes 786440 | tf_op jit(solution)/shard_map/ppermute | solution.py:584
  13.2 2.1 %collective-permute-start.5 = (bf16[64,2176]{1,0:T(8,128)(2,1)S(1)}, bf16[64,2176]{1,0:T(8,128)(2,1)S(1)}, u32[]{:S(2)}, u32[]{:S(2)}) collective-permute-start(bf16[64,2176]{1,0:T(8,128)(2,1)S(1)} %collective-permute-done.1.pair_frame), channel_id=1, source_target_pairs={{0,4},{4,8},{6,2},{8,12},{10,6},{14,10},{1,5},{5,9},{7,3},{9,13},{... | collective-permute-start | bytes 835592 | tf_op jit(solution)/shard_map/ppermute | solution.py:584
  15.3 0.0 copy-done
  15.3 0.0 copy-start.8
  15.3 0.0 copy-start.9
  15.3 2.3 %frame_parts.1 = (bf16[2,128,1024]{2,1,0:T(8,128)(2,1)S(1)}, f32[2,2,128,1024]{3,2,1,0:T(8,128)S(1)}, f32[128,1024]{1,0:T(8,128)S(1)}, bf16[2,256,256]{2,1,0:T(8,128)(2,1)S(1)}) custom-call(bf16[2,1,1,64,2048]{4,3,2,1,0:T(8,128)(2,1)S(1)} %copy-done, bf16[64,2176]{1,0:T(8,128)(2,1)S(1)} %collective-permute-done.1.pair_frame, ...), custom_call_target="tpu_custom_call" | custom-call | flops 2147483648 | bytes 1048576 | tf_op jit(solution)/shard_map/frame_parts/pallas_call | solution.py:496
  17.6 0.0 collective-permute-done.3.other_own
  17.6 0.0 collective-permute-done.pair_own
  17.7 2.4 %collective-permute-start.2 = (bf16[128,1024]{1,0:T(8,128)(2,1)S(1)}, bf16[128,1024]{1,0:T(8,128)(2,1)S(1)}, u32[]{:S(2)}, u32[]{:S(2)}) collective-permute-start(bf16[128,1024]{1,0:T(8,128)(2,1)S(1)} %collective-permute-done.pair_own), channel_id=1, source_target_pairs={{0,1},{1,0},{2,3},{3,2},{4,5},{5,4},{6,7},{7,6},{8,9},{9,8},{10,11... | collective-permute-start | bytes 786440 | tf_op jit(solution)/shard_map/ppermute | solution.py:588
  20.1 0.1 collective-permute-start.4
  20.2 0.0 copy-done.8
  20.2 0.0 copy-done.9
  20.2 0.4 %all_picks.1.picks = bf16[2,2,2,256,256]{4,3,2,1,0:T(8,128)(2,1)S(1)} custom-call(s32[2,1,16]{2,1,0:T(1,128)S(1)} %copy-done.8, s32[2,1,16]{2,1,0:T(1,128)S(1)} %copy-done.9), custom_call_target="tpu_custom_call" | custom-call | flops 536870912 | bytes 1048576 | tf_op jit(solution)/shard_map/all_picks/pallas_call | solution.py:472
  20.6 0.0 collective-permute-done.6.pair_own
  20.6 0.8 %collective-permute-start.10 = (bf16[128,1024]{1,0:T(8,128)(2,1)S(1)}, bf16[128,1024]{1,0:T(8,128)(2,1)S(1)}, u32[]{:S(2)}, u32[]{:S(2)}) collective-permute-start(bf16[128,1024]{1,0:T(8,128)(2,1)S(1)} %collective-permute-done.6.pair_own), channel_id=1, source_target_pairs={{0,1},{1,0},{2,3},{3,2},{4,5},{5,4},{6,7},{7,6},{8,9},{9,8},{10,11... | collective-permute-start | bytes 786440 | tf_op jit(solution)/shard_map/ppermute | solution.py:588
  21.4 0.0 collective-permute-done.7.other_own
  21.4 1.6 %collective-permute-start.11 = (bf16[128,1024]{1,0:T(8,128)(2,1)S(1)}, bf16[128,1024]{1,0:T(8,128)(2,1)S(1)}, u32[]{:S(2)}, u32[]{:S(2)}) collective-permute-start(bf16[128,1024]{1,0:T(8,128)(2,1)S(1)} %collective-permute-done.7.other_own), channel_id=1, source_target_pairs={{0,1},{1,0},{2,3},{3,2},{4,5},{5,4},{6,7},{7,6},{8,9},{9,8},{10,11... | collective-permute-start | bytes 786440 | tf_op jit(solution)/shard_map/ppermute | solution.py:588
  23.0 0.0 collective-permute-done.5.other_frame
  23.0 0.7 %other_frame_part.1 = (f32[128,1024]{1,0:T(8,128)S(1)}, bf16[2,256,256]{2,1,0:T(8,128)(2,1)S(1)}) custom-call(bf16[64,2176]{1,0:T(8,128)(2,1)S(1)} %collective-permute-done.5.other_frame, bf16[3,256,256]{2,1,0:T(8,128)(2,1)S(1)} %get-tuple-element.39.entry_frame, bf16[512,512]{1,0:T(8,128)(2,1)S(1)} %get-tuple-element.34.matrix), custom_call_target="tpu_custom_call" | custom-call | flops 1073741824 | bytes 524288 | tf_op jit(solution)/shard_map/other_frame_part/pallas_call | solution.py:515
  23.8 0.0 collective-permute-done.2.pair_swapped
  23.8 0.0 collective-permute-done.4.other_swapped
  23.8 2.0 %near.1 = (bf16[128,1024]{1,0:T(8,128)(2,1)S(1)}, bf16[128,1024]{1,0:T(8,128)(2,1)S(1)}) custom-call(bf16[128,1024]{1,0:T(8,128)(2,1)S(1)} %collective-permute-done.pair_own, bf16[128,1024]{1,0:T(8,128)(2,1)S(1)} %collective-permute-done.2.pair_swapped, bf16[128,1024]{1,0:T(8,128)(2,1)S(1)} %collective-permute-done.3.other_own, ...), custom_call_target="tpu_custom_call" | custom-call | flops 2147483648 | bytes 524288 | tf_op jit(solution)/shard_map/near/pallas_call | solution.py:534
  25.8 1.2 %collective-permute-start.8 = (bf16[128,1024]{1,0:T(8,128)(2,1)S(1)}, bf16[128,1024]{1,0:T(8,128)(2,1)S(1)}, u32[]{:S(2)}, u32[]{:S(2)}) collective-permute-start(bf16[128,1024]{1,0:T(8,128)(2,1)S(1)} %get-tuple-element.47.pair_own), channel_id=1, source_target_pairs={{0,1},{1,0},{2,3},{3,2},{4,5},{5,4},{6,7},{7,6},{8,9},{9,8},{10,11... | collective-permute-start | bytes 786440 | tf_op jit(solution)/shard_map/ppermute | solution.py:588
  27.0 0.1 collective-permute-start.9
  27.1 0.0 collective-permute-done.10.pair_swapped
  27.1 0.0 collective-permute-done.11.other_swapped
  27.1 2.6 %tick_0.1.rest_0_ = bf16[64,2048]{1,0:T(8,128)(2,1)S(1)} custom-call(bf16[128,1024]{1,0:T(8,128)(2,1)S(1)} %collective-permute-done.6.pair_own, bf16[128,1024]{1,0:T(8,128)(2,1)S(1)} %collective-permute-done.10.pair_swapped, bf16[128,1024]{1,0:T(8,128)(2,1)S(1)} %collective-permute-done.7.other_own, ...), custom_call_target="tpu_custom_call" | custom-call | flops 4294967296 | bytes 524288 | tf_op jit(solution)/shard_map/tick_0/pallas_call | solution.py:548
  29.6 0.0 collective-permute-done.8.pair_swapped
  29.7 0.0 collective-permute-done.9.other_swapped
  29.7 3.5 %tick_1.1 = (bf16[2,64,2048]{2,1,0:T(8,128)(2,1)}, bf16[64,2048]{1,0:T(8,128)(2,1)}, bf16[64,2048]{1,0:T(8,128)(2,1)}) custom-call(bf16[128,1024]{1,0:T(8,128)(2,1)S(1)} %get-tuple-element.47.pair_own, bf16[128,1024]{1,0:T(8,128)(2,1)S(1)} %collective-permute-done.8.pair_swapped, bf16[128,1024]{1,0:T(8,128)(2,1)S(1)} %get-tuple-element.48.other_own, ...), custom_call_target="tpu_custom_call" | custom-call | flops 4294967296 | bytes 524288 | tf_op jit(solution)/shard_map/tick_1/pallas_call | solution.py:564
Async XLA Ops:
  0.6 1.5 %copy-start.3 = (bf16[1,1,64,2048]{3,2,1,0:T(8,128)(2,1)S(1)}, bf16[1,1,64,2048]{3,2,1,0:T(8,128)(2,1)}, u32[]{:S(2)}) copy-start(bf16[1,1,64,2048]{3,2,1,0:T(8,128)(2,1)} %forward) | copy-start | bytes 786436
  0.6 1.5 %copy-start.4 = (bf16[1,1,64,2048]{3,2,1,0:T(8,128)(2,1)S(1)}, bf16[1,1,64,2048]{3,2,1,0:T(8,128)(2,1)}, u32[]{:S(2)}) copy-start(bf16[1,1,64,2048]{3,2,1,0:T(8,128)(2,1)} %backward.1) | copy-start | bytes 786436
  0.7 8.6 %copy-start.5 = (bf16[9,64,128]{2,1,0:T(8,128)(2,1)S(1)}, bf16[9,64,128]{2,1,0:T(8,128)(2,1)}, u32[]{:S(2)}) copy-start(bf16[9,64,128]{2,1,0:T(8,128)(2,1)} %fe) | copy-start | bytes 442372
  0.7 8.6 %copy-start.7 = (bf16[64,128]{1,0:T(8,128)(2,1)S(1)}, bf16[64,128]{1,0:T(8,128)(2,1)}, u32[]{:S(2)}) copy-start(bf16[64,128]{1,0:T(8,128)(2,1)} %mixing.1) | copy-start | bytes 49156
  0.7 8.6 %copy-start.2 = (bf16[1,2,9,64,64]{4,3,2,1,0:T(8,128)(2,1)S(1)}, bf16[1,2,9,64,64]{4,3,2,1,0:T(8,128)(2,1)}, u32[]{:S(2)}) copy-start(bf16[1,2,9,64,64]{4,3,2,1,0:T(8,128)(2,1)} %bb.1) | copy-start | bytes 442372
  0.7 8.6 %copy-start.6 = (bf16[9,64,128]{2,1,0:T(8,128)(2,1)S(1)}, bf16[9,64,128]{2,1,0:T(8,128)(2,1)}, u32[]{:S(2)}) copy-start(bf16[9,64,128]{2,1,0:T(8,128)(2,1)} %be.1) | copy-start | bytes 442372
  0.7 8.6 %copy-start.1 = (bf16[1,2,9,64,64]{4,3,2,1,0:T(8,128)(2,1)S(1)}, bf16[1,2,9,64,64]{4,3,2,1,0:T(8,128)(2,1)}, u32[]{:S(2)}) copy-start(bf16[1,2,9,64,64]{4,3,2,1,0:T(8,128)(2,1)} %fb.1) | copy-start | bytes 442372
  1.8 13.5 %copy-start = (bf16[2,1,1,64,2048]{4,3,2,1,0:T(8,128)(2,1)S(1)}, bf16[2,1,1,64,2048]{4,3,2,1,0:T(8,128)(2,1)}, u32[]{:S(2)}) copy-start(bf16[2,1,1,64,2048]{4,3,2,1,0:T(8,128)(2,1)} %frames.3) | copy-start | bytes 1572868
  1.8 8.2 %collective-permute-start.1 = (bf16[64,2176]{1,0:T(8,128)(2,1)S(1)}, bf16[64,2176]{1,0:T(8,128)(2,1)S(1)}, u32[]{:S(2)}, u32[]{:S(2)}) collective-permute-start(bf16[64,2176]{1,0:T(8,128)(2,1)S(1)} %head.1), channel_id=1, source_target_pairs={{0,2},{2,0},{4,6},{6,4},{8,10},{10,8},{12,14},{14,12},{1,3},{3,1},... | collective-permute-start | bytes 835592 | tf_op jit(solution)/shard_map/ppermute | solution.py:584
  2.6 15.0 %collective-permute-start.3 = (bf16[128,1024]{1,0:T(8,128)(2,1)S(1)}, bf16[128,1024]{1,0:T(8,128)(2,1)S(1)}, u32[]{:S(2)}, u32[]{:S(2)}) collective-permute-start(bf16[128,1024]{1,0:T(8,128)(2,1)S(1)} %get-tuple-element.31), channel_id=1, source_target_pairs={{0,4},{4,8},{6,2},{8,12},{10,6},{14,10},{1,5},{5,9},{7,3},{9,13},{... | collective-permute-start | bytes 786440 | tf_op jit(solution)/shard_map/ppermute | solution.py:584
  4.6 13.1 %collective-permute-start = (bf16[128,1024]{1,0:T(8,128)(2,1)S(1)}, bf16[128,1024]{1,0:T(8,128)(2,1)S(1)}, u32[]{:S(2)}, u32[]{:S(2)}) collective-permute-start(bf16[128,1024]{1,0:T(8,128)(2,1)S(1)} %get-tuple-element.41), channel_id=1, source_target_pairs={{2,6},{4,0},{6,10},{8,4},{10,14},{12,8},{3,7},{5,1},{7,11},{9,5},{... | collective-permute-start | bytes 786440 | tf_op jit(solution)/shard_map/ppermute | solution.py:584
  7.9 12.6 %collective-permute-start.6 = (bf16[128,1024]{1,0:T(8,128)(2,1)S(1)}, bf16[128,1024]{1,0:T(8,128)(2,1)S(1)}, u32[]{:S(2)}, u32[]{:S(2)}) collective-permute-start(bf16[128,1024]{1,0:T(8,128)(2,1)S(1)} %get-tuple-element.31), channel_id=1, source_target_pairs={{0,2},{2,0},{4,6},{6,4},{8,10},{10,8},{12,14},{14,12},{1,3},{3,1},... | collective-permute-start | bytes 786440 | tf_op jit(solution)/shard_map/ppermute | solution.py:584
  10.0 11.4 %collective-permute-start.7 = (bf16[128,1024]{1,0:T(8,128)(2,1)S(1)}, bf16[128,1024]{1,0:T(8,128)(2,1)S(1)}, u32[]{:S(2)}, u32[]{:S(2)}) collective-permute-start(bf16[128,1024]{1,0:T(8,128)(2,1)S(1)} %get-tuple-element.41), channel_id=1, source_target_pairs={{2,4},{4,2},{6,8},{8,6},{10,12},{12,10},{3,5},{5,3},{7,9},{9,7},{1... | collective-permute-start | bytes 786440 | tf_op jit(solution)/shard_map/ppermute | solution.py:584
  13.2 9.9 %collective-permute-start.5 = (bf16[64,2176]{1,0:T(8,128)(2,1)S(1)}, bf16[64,2176]{1,0:T(8,128)(2,1)S(1)}, u32[]{:S(2)}, u32[]{:S(2)}) collective-permute-start(bf16[64,2176]{1,0:T(8,128)(2,1)S(1)} %collective-permute-done.1.pair_frame), channel_id=1, source_target_pairs={{0,4},{4,8},{6,2},{8,12},{10,6},{14,10},{1,5},{5,9},{7,3},{9,13},{... | collective-permute-start | bytes 835592 | tf_op jit(solution)/shard_map/ppermute | solution.py:584
  15.3 4.9 %copy-start.8 = (s32[2,1,16]{2,1,0:T(1,128)S(1)}, s32[2,1,16]{2,1,0:T(1,128)}, u32[]{:S(2)}) copy-start(s32[2,1,16]{2,1,0:T(1,128)} %forward_index.3) | copy-start | bytes 388
  15.3 4.9 %copy-start.9 = (s32[2,1,16]{2,1,0:T(1,128)S(1)}, s32[2,1,16]{2,1,0:T(1,128)}, u32[]{:S(2)}) copy-start(s32[2,1,16]{2,1,0:T(1,128)} %backward_index.3) | copy-start | bytes 388
  17.7 6.1 %collective-permute-start.2 = (bf16[128,1024]{1,0:T(8,128)(2,1)S(1)}, bf16[128,1024]{1,0:T(8,128)(2,1)S(1)}, u32[]{:S(2)}, u32[]{:S(2)}) collective-permute-start(bf16[128,1024]{1,0:T(8,128)(2,1)S(1)} %collective-permute-done.pair_own), channel_id=1, source_target_pairs={{0,1},{1,0},{2,3},{3,2},{4,5},{5,4},{6,7},{7,6},{8,9},{9,8},{10,11... | collective-permute-start | bytes 786440 | tf_op jit(solution)/shard_map/ppermute | solution.py:588
  20.1 3.7 %collective-permute-start.4 = (bf16[128,1024]{1,0:T(8,128)(2,1)S(1)}, bf16[128,1024]{1,0:T(8,128)(2,1)S(1)}, u32[]{:S(2)}, u32[]{:S(2)}) collective-permute-start(bf16[128,1024]{1,0:T(8,128)(2,1)S(1)} %collective-permute-done.3.other_own), channel_id=1, source_target_pairs={{0,1},{1,0},{2,3},{3,2},{4,5},{5,4},{6,7},{7,6},{8,9},{9,8},{10,11... | collective-permute-start | bytes 786440 | tf_op jit(solution)/shard_map/ppermute | solution.py:588
  20.6 6.5 %collective-permute-start.10 = (bf16[128,1024]{1,0:T(8,128)(2,1)S(1)}, bf16[128,1024]{1,0:T(8,128)(2,1)S(1)}, u32[]{:S(2)}, u32[]{:S(2)}) collective-permute-start(bf16[128,1024]{1,0:T(8,128)(2,1)S(1)} %collective-permute-done.6.pair_own), channel_id=1, source_target_pairs={{0,1},{1,0},{2,3},{3,2},{4,5},{5,4},{6,7},{7,6},{8,9},{9,8},{10,11... | collective-permute-start | bytes 786440 | tf_op jit(solution)/shard_map/ppermute | solution.py:588
  21.4 5.7 %collective-permute-start.11 = (bf16[128,1024]{1,0:T(8,128)(2,1)S(1)}, bf16[128,1024]{1,0:T(8,128)(2,1)S(1)}, u32[]{:S(2)}, u32[]{:S(2)}) collective-permute-start(bf16[128,1024]{1,0:T(8,128)(2,1)S(1)} %collective-permute-done.7.other_own), channel_id=1, source_target_pairs={{0,1},{1,0},{2,3},{3,2},{4,5},{5,4},{6,7},{7,6},{8,9},{9,8},{10,11... | collective-permute-start | bytes 786440 | tf_op jit(solution)/shard_map/ppermute | solution.py:588
  25.8 3.8 %collective-permute-start.8 = (bf16[128,1024]{1,0:T(8,128)(2,1)S(1)}, bf16[128,1024]{1,0:T(8,128)(2,1)S(1)}, u32[]{:S(2)}, u32[]{:S(2)}) collective-permute-start(bf16[128,1024]{1,0:T(8,128)(2,1)S(1)} %get-tuple-element.47.pair_own), channel_id=1, source_target_pairs={{0,1},{1,0},{2,3},{3,2},{4,5},{5,4},{6,7},{7,6},{8,9},{9,8},{10,11... | collective-permute-start | bytes 786440 | tf_op jit(solution)/shard_map/ppermute | solution.py:588
  27.0 2.7 %collective-permute-start.9 = (bf16[128,1024]{1,0:T(8,128)(2,1)S(1)}, bf16[128,1024]{1,0:T(8,128)(2,1)S(1)}, u32[]{:S(2)}, u32[]{:S(2)}) collective-permute-start(bf16[128,1024]{1,0:T(8,128)(2,1)S(1)} %get-tuple-element.48.other_own), channel_id=1, source_target_pairs={{0,1},{1,0},{2,3},{3,2},{4,5},{5,4},{6,7},{7,6},{8,9},{9,8},{10,11... | collective-permute-start | bytes 786440 | tf_op jit(solution)/shard_map/ppermute | solution.py:588
